TPU v7x, 256 devices: a whole 4x4x8 slice. The times are simulated.
256 devices in a mesh: dp: 32 (over y, z), cam: 8 (over x, core).
Axes of the slice: x: 4, y: 4, z: 8, core: 2. Of those that a mesh axis runs over, the one named last changes fastest.
Arguments:
- x_in: bfloat16 [32, 8192, 1536], P('dp', 'cam'), may hold values from -6 to 6
- feat: bfloat16 [32, 8192, 1536], P('dp', 'cam'), may hold values from -6 to 6
- w_head: bfloat16 [1536, 192], replicated, may hold values from -0.15625 to 0.15625
- g_bev: bfloat16 [32, 32768, 128], P('dp', 'cam'), may hold values from -6 to 6
- cell_lists: int32 [32, 8, 8, 512], P('dp', 'cam'), may hold values from 0 to 4095, as said below
- point_slots: int32 [32, 8192, 64], P('dp', 'cam'), may hold values from 0 to 4096, as said below
- master: float32 [1536, 1728], P('dp'), may hold values from -0.15625 to 0.15625
- first_moment: float32 [1536, 1728], P('dp'), may hold values from -6 to 6
- second_moment: float32 [1536, 1728], P('dp'), may hold values from 0.5 to 4
Outputs:
- new_master: float32 [1536, 1728], P('dp')
- new_first: float32 [1536, 1728], P('dp')
- new_second: float32 [1536, 1728], P('dp')
Inputs may be any that keep to these rules, and one draw needn't show every extreme that they name: `cell_lists`: each list of 512 cells that a pixel block asks of one tile is strictly increasing and holds cell numbers local to that tile. `point_slots`: an entry o * 512 + k names slot k of the list that the pixel's block asks of tile o; the entry 4096 marks a point outside the grid.
All inputs are finite; a program needn't handle non-finite values.
Results may differ from a plain program's by a relative error of at most 0.0006.
Values may be sent and summed in bfloat16 or wider, within the bound.
No kernel may reach another device: no remote copies, remote signals or barrier semaphores. Data moves between devices by JAX's collectives and lax.ppermute only.
A program may use at most 128 MiB of HBM per device.

v0:
```python
import math

import jax
import jax.numpy as jnp
from jax import lax
from jax.sharding import PartitionSpec as P

beta_one = 0.9
beta_two = 0.999
bias_one = 0.9999734386011124
bias_two = 0.0952078528862911
learn_rate = 0.01
adam_epsilon = 1e-08


def adam_update(master_rows, first_rows, second_rows, gradient):
    first_new = beta_one * first_rows + (1.0 - beta_one) * gradient
    second_new = beta_two * second_rows + (1.0 - beta_two) * gradient * gradient
    direction = first_new / bias_one / (jnp.sqrt(second_new / bias_two) + adam_epsilon)
    return (master_rows - learn_rate * direction, first_new, second_new)


def expand_proj(inner_proj, w_head):
    return lax.dot_general(
        inner_proj,
        w_head.astype(jnp.float32),
        (((1,), (1,)), ((), ())),
        precision=lax.Precision.HIGHEST,
        preferred_element_type=jnp.float32,
    )


def shards(x_in, feat, w_head, g_bev, cell_lists, point_slots, master, first_moment, second_moment):
    cam_count = lax.axis_size("cam")
    data_count = lax.axis_size("dp")
    bev_tile = g_bev[0]
    tile_len = bev_tile.shape[0]
    channels = bev_tile.shape[1]
    cell_list = cell_lists[0, 0]
    all_tiles = lax.all_gather(bev_tile, "cam", axis=0, tiled=True)
    offsets = jnp.arange(cam_count, dtype=jnp.int32)[:, None] * tile_len
    row_table = all_tiles[(cell_list + offsets).reshape(-1)]
    table_wide = row_table.astype(jnp.float32)
    asked_count = table_wide.shape[0]
    inputs = x_in[0]
    features = feat[0]
    slot_ids = point_slots[0]
    pixels = features.shape[0]
    depth_bins = slot_ids.shape[1]
    head_out = jnp.dot(features, w_head, preferred_element_type=jnp.float32)
    occupancy = jax.nn.sigmoid(head_out[:, channels:])
    context = head_out[:, :channels]
    block_rows = math.gcd(pixels, 128)
    block_count = pixels // block_rows

    def block_grads(items):
        occ_block, ctx_block, slot_block = items
        columns = lax.broadcasted_iota(jnp.int32, (1, 1, asked_count), 2)
        matches = slot_block[:, :, None] == columns
        weights = jnp.sum(jnp.where(matches, occ_block[:, :, None], 0.0), axis=1)
        ctx_grad = jnp.dot(
            weights, table_wide, precision=lax.Precision.HIGHEST, preferred_element_type=jnp.float32
        )
        scores = lax.dot_general(
            ctx_block,
            table_wide,
            (((1,), (1,)), ((), ())),
            precision=lax.Precision.HIGHEST,
            preferred_element_type=jnp.float32,
        )
        occ_grad = jnp.sum(jnp.where(matches, scores[:, None, :], 0.0), axis=2)
        return (ctx_grad, occ_grad)

    g_context, g_occupancy = lax.map(
        block_grads,
        (
            occupancy.reshape(block_count, block_rows, depth_bins),
            context.reshape(block_count, block_rows, channels),
            slot_ids.reshape(block_count, block_rows, depth_bins),
        ),
    )
    g_context = g_context.reshape(pixels, channels)
    g_occupancy = g_occupancy.reshape(pixels, depth_bins)
    g_logits = occupancy * (1.0 - occupancy) * g_occupancy
    g_head = jnp.concatenate([g_context, g_logits], axis=1).astype(jnp.bfloat16)
    head_width = g_head.shape[1]
    contract = (((0,), (0,)), ((), ()))
    grad_scale = 1.0 / math.sqrt(data_count * cam_count * pixels)
    inner_proj = lax.dot_general(inputs, g_head, contract, preferred_element_type=jnp.float32)
    inner_head = lax.dot_general(features, g_head, contract, preferred_element_type=jnp.float32)
    inner_share = lax.psum_scatter(
        jnp.concatenate([inner_proj, inner_head], axis=1), "dp", scatter_dimension=0, tiled=True
    )
    inner_full = lax.psum(inner_share, "cam")
    gradient = (
        jnp.concatenate(
            [expand_proj(inner_full[:, :head_width], w_head), inner_full[:, head_width:]], axis=1
        )
        * grad_scale
    )
    return adam_update(master, first_moment, second_moment, gradient)


def solution(mesh):
    placed = (
        P("dp", "cam", None),
        P("dp", "cam", None),
        P(),
        P("dp", "cam", None),
        P("dp", "cam", None, None),
        P("dp", "cam", None),
        P("dp", None),
        P("dp", None),
        P("dp", None),
    )
    return jax.shard_map(
        shards,
        mesh=mesh,
        in_specs=placed,
        out_specs=(P("dp", None), P("dp", None), P("dp", None)),
        check_vma=False,
    )
```

profile of v0, /device:TPU:1, one launch (start us, length us, event | category | flops | bytes accessed | tf_op | source)
XLA Modules:
  0.0 863.7 jit_solution(10066786550953338886)
XLA Ops:
  10.9 2.2 fusion.9
  19.0 47.4 %all-gather.3.cloned.1.call-done = bf16[1,32768,128]{2,1,0:T(8,128)(2,1)} async-done(((bf16[1,4096,128]{2,1,0:T(8,128)(2,1)}), bf16[1,32768,128]{2,1,0:T(8,128)(2,1)}) %all-gather.3.cloned.1.call-update) | async-done | bytes 8388624 | tf_op jit(solution)/shard_map/all_gather | solution.py:40
  66.4 18.8 %gather_fusion = bf16[4096,128]{1,0:T(8,128)(2,1)} fusion(bf16[32768,128]{1,0:T(8,128)(2,1)} %bitcast.67, s32[4096]{0:T(1024)S(1)} %broadcast_clamp_fusion), kind=kCustom, calls=%fused_computation | custom fusion | bytes 2113536 | tf_op jit(solution)/shard_map/gather | solution.py:42
  85.2 2.7 convert_element_type.2
  87.9 475.3 %while.12 = (s32[]{:T(128)}, bf16[8,128,128]{2,1,0:T(8,128)(2,1)S(1)}, f32[8,128,64]{2,1,0:T(8,128)}, s32[8,128,64]{2,1,0:T(8,128)}, f32[8,128,64]{2,1,0:T(8,128...) while((s32[]{:T(128)}, bf16[8,128,128]{2,1,0:T(8,128)(2,1)S(1)}, f32[8,128,64]{2,1,0:T(8,128)}, ...), condition=%wide.region_3.4_spmd, body=%wide.region_0.3_spmd.sunk | while | flops 1777852416 | bytes 21430412 | solution.py:74
  89.6 3.5 fusion.41
  93.1 51.4 %select_reduce_fusion.3 = (f32[128,64]{1,0:T(8,128)S(1)}, f32[128,4096]{1,0:T(8,128)S(1)}) fusion(f32[128,4096]{1,0:T(8,128)S(1)} %fusion.41, s32[128,64]{1,0:T(8,128)S(1)} %dynamic-slice_bitcast_fusion.4, f32[128,64]{1,0:T(8,128)S(1)} %dynamic-slice_bitcast_fusion.5), kind=kLoop, calls=%fused_computation.1.clone.1 | loop fusion | flops 167239680 | bytes 4292608 | tf_op jit(solution)/shard_map/while/body/eval_jaxpr/reduce_sum | solution.py:71
  144.5 2.2 fusion.42
  149.0 3.5 fusion.41
  152.6 51.4 %select_reduce_fusion.3 = (f32[128,64]{1,0:T(8,128)S(1)}, f32[128,4096]{1,0:T(8,128)S(1)}) fusion(f32[128,4096]{1,0:T(8,128)S(1)} %fusion.41, s32[128,64]{1,0:T(8,128)S(1)} %dynamic-slice_bitcast_fusion.4, f32[128,64]{1,0:T(8,128)S(1)} %dynamic-slice_bitcast_fusion.5), kind=kLoop, calls=%fused_computation.1.clone.1 | loop fusion | flops 167239680 | bytes 4292608 | tf_op jit(solution)/shard_map/while/body/eval_jaxpr/reduce_sum | solution.py:71
  203.9 2.2 fusion.42
  208.4 3.5 fusion.41
  212.0 51.4 %select_reduce_fusion.3 = (f32[128,64]{1,0:T(8,128)S(1)}, f32[128,4096]{1,0:T(8,128)S(1)}) fusion(f32[128,4096]{1,0:T(8,128)S(1)} %fusion.41, s32[128,64]{1,0:T(8,128)S(1)} %dynamic-slice_bitcast_fusion.4, f32[128,64]{1,0:T(8,128)S(1)} %dynamic-slice_bitcast_fusion.5), kind=kLoop, calls=%fused_computation.1.clone.1 | loop fusion | flops 167239680 | bytes 4292608 | tf_op jit(solution)/shard_map/while/body/eval_jaxpr/reduce_sum | solution.py:71
  263.3 2.2 fusion.42
  267.8 3.5 fusion.41
  271.4 51.4 %select_reduce_fusion.3 = (f32[128,64]{1,0:T(8,128)S(1)}, f32[128,4096]{1,0:T(8,128)S(1)}) fusion(f32[128,4096]{1,0:T(8,128)S(1)} %fusion.41, s32[128,64]{1,0:T(8,128)S(1)} %dynamic-slice_bitcast_fusion.4, f32[128,64]{1,0:T(8,128)S(1)} %dynamic-slice_bitcast_fusion.5), kind=kLoop, calls=%fused_computation.1.clone.1 | loop fusion | flops 167239680 | bytes 4292608 | tf_op jit(solution)/shard_map/while/body/eval_jaxpr/reduce_sum | solution.py:71
  322.7 2.2 fusion.42
  327.3 3.5 fusion.41
  330.8 51.4 %select_reduce_fusion.3 = (f32[128,64]{1,0:T(8,128)S(1)}, f32[128,4096]{1,0:T(8,128)S(1)}) fusion(f32[128,4096]{1,0:T(8,128)S(1)} %fusion.41, s32[128,64]{1,0:T(8,128)S(1)} %dynamic-slice_bitcast_fusion.4, f32[128,64]{1,0:T(8,128)S(1)} %dynamic-slice_bitcast_fusion.5), kind=kLoop, calls=%fused_computation.1.clone.1 | loop fusion | flops 167239680 | bytes 4292608 | tf_op jit(solution)/shard_map/while/body/eval_jaxpr/reduce_sum | solution.py:71
  382.2 2.2 fusion.42
  386.7 3.5 fusion.41
  390.2 51.4 %select_reduce_fusion.3 = (f32[128,64]{1,0:T(8,128)S(1)}, f32[128,4096]{1,0:T(8,128)S(1)}) fusion(f32[128,4096]{1,0:T(8,128)S(1)} %fusion.41, s32[128,64]{1,0:T(8,128)S(1)} %dynamic-slice_bitcast_fusion.4, f32[128,64]{1,0:T(8,128)S(1)} %dynamic-slice_bitcast_fusion.5), kind=kLoop, calls=%fused_computation.1.clone.1 | loop fusion | flops 167239680 | bytes 4292608 | tf_op jit(solution)/shard_map/while/body/eval_jaxpr/reduce_sum | solution.py:71
  441.6 2.2 fusion.42
  446.1 3.5 fusion.41
  449.6 51.4 %select_reduce_fusion.3 = (f32[128,64]{1,0:T(8,128)S(1)}, f32[128,4096]{1,0:T(8,128)S(1)}) fusion(f32[128,4096]{1,0:T(8,128)S(1)} %fusion.41, s32[128,64]{1,0:T(8,128)S(1)} %dynamic-slice_bitcast_fusion.4, f32[128,64]{1,0:T(8,128)S(1)} %dynamic-slice_bitcast_fusion.5), kind=kLoop, calls=%fused_computation.1.clone.1 | loop fusion | flops 167239680 | bytes 4292608 | tf_op jit(solution)/shard_map/while/body/eval_jaxpr/reduce_sum | solution.py:71
  501.0 2.2 fusion.42
  505.5 3.5 fusion.41
  509.1 51.4 %select_reduce_fusion.3 = (f32[128,64]{1,0:T(8,128)S(1)}, f32[128,4096]{1,0:T(8,128)S(1)}) fusion(f32[128,4096]{1,0:T(8,128)S(1)} %fusion.41, s32[128,64]{1,0:T(8,128)S(1)} %dynamic-slice_bitcast_fusion.4, f32[128,64]{1,0:T(8,128)S(1)} %dynamic-slice_bitcast_fusion.5), kind=kLoop, calls=%fused_computation.1.clone.1 | loop fusion | flops 167239680 | bytes 4292608 | tf_op jit(solution)/shard_map/while/body/eval_jaxpr/reduce_sum | solution.py:71
  560.4 2.2 fusion.42
  570.9 3.0 copy.33
  574.0 212.8 %reduce-scatter.4.cloned.1.call-done = f32[48,384]{1,0:T(8,128)} async-done(((f32[1536,384]{1,0:T(8,128)}), f32[48,384]{1,0:T(8,128)}) %reduce-scatter.4.cloned.1.call-update) | async-done | bytes 73744 | tf_op jit(solution)/shard_map/reduce_scatter | solution.py:91
  786.8 65.7 %all-reduce.2.cloned.1.call-done = f32[48,384]{1,0:T(8,128)} async-done(((f32[48,384]{1,0:T(8,128)}), f32[48,384]{1,0:T(8,128)}) %all-reduce.2.cloned.1.call-update) | async-done | bytes 73744 | tf_op jit(solution)/shard_map/psum | solution.py:94
  (80 shorter events, 40.4 us)
Async XLA Ops:
  7.2 3.7 copy-start
  7.2 59.2 %all-gather.3.cloned.1.call-start = ((), (), s32[]{:S(2)}) async-start(), calls=%async_computation.2 | async-start | bytes 9437184 | tf_op jit(solution)/shard_map/all_gather | solution.py:40
  7.9 778.9 %reduce-scatter.4.cloned.1.call-start = ((), (), s32[]{:S(2)}) async-start(), calls=%async_computation.3 | async-start | bytes 2433024 | tf_op jit(solution)/shard_map/reduce_scatter | solution.py:91
  13.1 1.1 copy-start.3
  93.1 51.4 %copy-start.1 = (f32[4096,128]{1,0:T(8,128)S(1)}, f32[4096,128]{1,0:T(8,128)}, u32[]{:S(2)}) copy-start(f32[4096,128]{1,0:T(8,128)} %get-tuple-element.151) | copy-start | bytes 6291460 | tf_op jit(solution)/shard_map/while
  152.5 51.4 %copy-start.1 = (f32[4096,128]{1,0:T(8,128)S(1)}, f32[4096,128]{1,0:T(8,128)}, u32[]{:S(2)}) copy-start(f32[4096,128]{1,0:T(8,128)} %get-tuple-element.151) | copy-start | bytes 6291460 | tf_op jit(solution)/shard_map/while
  212.0 51.4 %copy-start.1 = (f32[4096,128]{1,0:T(8,128)S(1)}, f32[4096,128]{1,0:T(8,128)}, u32[]{:S(2)}) copy-start(f32[4096,128]{1,0:T(8,128)} %get-tuple-element.151) | copy-start | bytes 6291460 | tf_op jit(solution)/shard_map/while
  271.4 51.4 %copy-start.1 = (f32[4096,128]{1,0:T(8,128)S(1)}, f32[4096,128]{1,0:T(8,128)}, u32[]{:S(2)}) copy-start(f32[4096,128]{1,0:T(8,128)} %get-tuple-element.151) | copy-start | bytes 6291460 | tf_op jit(solution)/shard_map/while
  330.8 51.4 %copy-start.1 = (f32[4096,128]{1,0:T(8,128)S(1)}, f32[4096,128]{1,0:T(8,128)}, u32[]{:S(2)}) copy-start(f32[4096,128]{1,0:T(8,128)} %get-tuple-element.151) | copy-start | bytes 6291460 | tf_op jit(solution)/shard_map/while
  390.2 51.4 %copy-start.1 = (f32[4096,128]{1,0:T(8,128)S(1)}, f32[4096,128]{1,0:T(8,128)}, u32[]{:S(2)}) copy-start(f32[4096,128]{1,0:T(8,128)} %get-tuple-element.151) | copy-start | bytes 6291460 | tf_op jit(solution)/shard_map/while
  449.6 51.4 %copy-start.1 = (f32[4096,128]{1,0:T(8,128)S(1)}, f32[4096,128]{1,0:T(8,128)}, u32[]{:S(2)}) copy-start(f32[4096,128]{1,0:T(8,128)} %get-tuple-element.151) | copy-start | bytes 6291460 | tf_op jit(solution)/shard_map/while
  509.0 51.4 %copy-start.1 = (f32[4096,128]{1,0:T(8,128)S(1)}, f32[4096,128]{1,0:T(8,128)}, u32[]{:S(2)}) copy-start(f32[4096,128]{1,0:T(8,128)} %get-tuple-element.151) | copy-start | bytes 6291460 | tf_op jit(solution)/shard_map/while
  563.2 2.0 copy-start.4
  566.5 2.0 copy-start.2
  566.6 2.0 copy-start.5
  573.9 281.0 %copy-start.6 = (f32[48,1728]{1,0:T(8,128)S(1)}, f32[48,1728]{1,0:T(8,128)}, u32[]{:S(2)}) copy-start(f32[48,1728]{1,0:T(8,128)} %param.17) | copy-start | bytes 995332
  574.0 278.6 %all-reduce.2.cloned.1.call-start = ((), (), s32[]{:S(2)}) async-start(), calls=%async_computation.1 | async-start | bytes 147456 | tf_op jit(solution)/shard_map/psum | solution.py:94
Sparse Core Ops, SparseCore 0:
  9.9 56.4 all-gather.2
  574.1 212.6 reduce-scatter.3
  789.2 63.3 all-reduce.1
where the time goes:
time: 865 us; the launch traced here: 864 us
  other arithmetic  419 us (48%)
  waiting for transfers between devices  327 us (38%)
  matrix products  52.1 us (6%)
  local copies, waits for them, and re-layouts  51.6 us (6%)
  between operations  13.9 us (2%)
    reduce_sum x8, other arithmetic, block_grads(): occ_grad = jnp.sum(jnp.where(matches, scores[:, None, :], 0.0), axis=2)  411 us
    reduce_scatter x1, waiting for transfers between devices, shards(): lax.psum_scatter(jnp.concatenate([inner_proj, inner_head], axis=1), 'dp',...  213 us
    psum x1, waiting for transfers between devices, shards(): inner_full = lax.psum(inner_share, 'cam')  65.7 us
    all_gather x1, waiting for transfers between devices, shards(): all_tiles = lax.all_gather(bev_tile, 'cam', axis=0, tiled=True)  47.4 us
    dot_general x8, matrix products, block_grads(): lax.dot_general(ctx_block, table_wide, (((1,), (1,)), ((), ())), precisio...  28.2 us
    gather x1, local copies, waits for them, and re-layouts, shards(): row_table = all_tiles[(cell_list + offsets).reshape(-1)]  18.8 us
    dot_general x8, matrix products, block_grads(): jnp.dot(weights, table_wide, precision=lax.Precision.HIGHEST, preferred_e...  17.5 us
  transfers between devices with their start and end apart: 3, of which 3 were waited for; matrix products, arithmetic and copies ran while one was open for 1% of the time, Pallas kernels for 0%

commit v1 on v0

v1 whole, which is shorter than its diff:
```python
import functools
import math

import jax
import jax.numpy as jnp
from jax import lax
from jax.experimental import pallas as pl
from jax.experimental.pallas import tpu as pltpu
from jax.sharding import PartitionSpec as P

beta_one = 0.9
beta_two = 0.999
bias_one = 0.9999734386011124
bias_two = 0.0952078528862911
learn_rate = 0.01
adam_epsilon = 1e-08

bf16 = jnp.bfloat16
f32 = jnp.float32
i32 = jnp.int32

NT = (((1,), (1,)), ((), ()))
TN = (((0,), (0,)), ((), ()))

CHIPS = 4
CAP = 512
CH = 128
MIB = 1 << 20


def vmem():
    return pl.BlockSpec(memory_space=pltpu.VMEM)


def smem():
    return pl.BlockSpec(memory_space=pltpu.SMEM)


def split(value):
    high = value.astype(bf16)
    return high, (value - high.astype(f32)).astype(bf16)


def gather_kernel(me_ref, lists_ref, tile_ref, own_ref, pair_ref, one_ref, two_ref, three_ref, wide, rows):
    wide[...] = tile_ref[...].astype(f32)
    me = me_ref[0]
    places = (
        (own_ref, 0), (pair_ref, 0), (one_ref, 0), (one_ref, 1),
        (two_ref, 0), (two_ref, 1), (three_ref, 0), (three_ref, 1),
    )
    for block, (ref, part) in enumerate(places):
        start = jnp.bitwise_xor(me, block) * CAP

        def step(i, carry):
            base = i * 16
            for u in range(16):
                cell = lists_ref[start + base + u]
                rows[pl.ds(base + u, 1), :] = wide[pl.ds(cell, 1), :]
            return carry

        lax.fori_loop(0, CAP // 16, step, 0)
        ref[part] = rows[...].astype(bf16)


def gather_rows(me, lists, tile):
    one = jax.ShapeDtypeStruct((1, CAP, CH), bf16)
    two = jax.ShapeDtypeStruct((2, CAP, CH), bf16)
    return pl.pallas_call(
        gather_kernel,
        out_shape=(one, one, two, two, two),
        in_specs=[smem(), smem(), vmem()],
        out_specs=(vmem(),) * 5,
        scratch_shapes=[pltpu.VMEM(tile.shape, f32), pltpu.VMEM((CAP, CH), f32)],
        compiler_params=pltpu.CompilerParams(vmem_limit_bytes=16 * MIB),
        name="gather_rows",
    )(me, lists, tile)


def weights_kernel(feat_ref, w_ref, slot_ref, wts_ref, occ_ref, ctx_ref):
    block = feat_ref.shape[0]
    head = jnp.dot(feat_ref[...], w_ref[...], preferred_element_type=f32)
    occ_ref[...] = 1.0 / (1.0 + jnp.exp(-head[:, CH:]))
    ctx_ref[:, :CH], ctx_ref[:, CH:] = split(head[:, :CH])
    lane = lax.broadcasted_iota(i32, (8, 128), 1)
    sub = lax.broadcasted_iota(i32, (8, 128), 0)
    half = (lane >= 64).astype(i32)

    def build(i, carry):
        base = pl.multiple_of(i * 16, 16)
        pair = []
        for q in range(2):
            slot = slot_ref[pl.ds(base + q * 8, 8), :]
            occ = occ_ref[pl.ds(base + q * 8, 8), :]
            high = slot >> 8
            low = slot & 255
            occ_high = occ.astype(bf16).astype(f32)
            occ_low = occ - occ_high
            hit = high[None] == lax.broadcasted_iota(i32, (16, 8, 128), 0)
            low_rows = lax.broadcasted_iota(i32, (256, 128), 0)
            left_high, left_low, right = [], [], []
            for j in range(4):
                mine = sub == 2 * j + half
                part_high = jnp.where(mine, occ_high, 0.0)
                part_low = jnp.where(mine, occ_low, 0.0)
                left_high.append(jnp.where(hit, part_high[None], 0.0).reshape(128, 128).astype(bf16))
                left_low.append(jnp.where(hit, part_low[None], 0.0).reshape(128, 128).astype(bf16))
                row = jnp.where(lane[:1] < 64, low[2 * j : 2 * j + 1], low[2 * j + 1 : 2 * j + 2])
                right.append(jnp.where(low_rows == row, 1.0, 0.0).astype(bf16))
            left = jnp.concatenate(
                [jnp.concatenate(left_high, axis=1), jnp.concatenate(left_low, axis=1)], axis=0
            )
            both = lax.dot_general(left, jnp.concatenate(right, axis=1), NT, preferred_element_type=f32)
            pair.append(both[:128] + both[128:])
        for h in range(16):
            rows = slice(h * 8, h * 8 + 8)
            value = jnp.concatenate([pair[0][rows], pair[1][rows]], axis=0)
            columns = slice(h * 256, h * 256 + 256)
            wts_ref[pl.ds(base, 16), columns], wts_ref[pl.ds(block + base, 16), columns] = split(value)
        return carry

    lax.fori_loop(0, block // 16, build, 0)


def pixel_weights(feat, w_wide, slots, block=256):
    pixels, width = feat.shape
    table = 8 * CAP
    return pl.pallas_call(
        weights_kernel,
        grid=(pixels // block,),
        out_shape=(
            jax.ShapeDtypeStruct((2 * pixels, table), bf16),
            jax.ShapeDtypeStruct((pixels, 128), f32),
            jax.ShapeDtypeStruct((pixels, 2 * CH), bf16),
        ),
        in_specs=[
            pl.BlockSpec((block, width), lambda i: (i, 0)),
            pl.BlockSpec((width, 256), lambda i: (0, 0)),
            pl.BlockSpec((block, 128), lambda i: (i, 0)),
        ],
        out_specs=(
            pl.BlockSpec((2 * block, table), lambda i: (i, 0)),
            pl.BlockSpec((block, 128), lambda i: (i, 0)),
            pl.BlockSpec((block, 2 * CH), lambda i: (i, 0)),
        ),
        compiler_params=pltpu.CompilerParams(vmem_limit_bytes=54 * MIB),
        cost_estimate=pl.CostEstimate(flops=25 * 10**9, bytes_accessed=24 * 10**6, transcendentals=0),
        name="pixel_weights",
    )(feat, w_wide, slots)


def grads_kernel(
    own_ref, one_ref, two_ref, three_ref, far_ref, wts_ref, occ_ref, ctx_ref, slot_ref, out_ref, table, scores, picked
):
    block = occ_ref.shape[0]
    count = table.shape[0]

    @pl.when(pl.program_id(0) == 0)
    def _():
        for k, ref in enumerate((own_ref, one_ref, two_ref, three_ref)):
            table[k * CAP : (k + 1) * CAP, :] = ref[0]
        table[4 * CAP :, :] = far_ref[...]

    def score(i, carry):
        start = pl.multiple_of(i * 256, 256)
        rows = table[pl.ds(start, 256), :]
        scores[:, pl.ds(start, 256)] = lax.dot_general(
            ctx_ref[...], jnp.concatenate([rows, rows], axis=1), NT, preferred_element_type=f32
        )
        return carry

    lax.fori_loop(0, count // 256, score, 0, unroll=4)

    def pick(i, carry):
        base = pl.multiple_of(i * 8, 8)
        slot = slot_ref[pl.ds(base, 8), :]
        low = slot & 127
        high = slot >> 7
        total = jnp.zeros((8, 128), f32)
        for g in range(count // 128):
            found = jnp.take_along_axis(
                scores[pl.ds(base, 8), g * 128 : (g + 1) * 128], low, axis=1, mode="promise_in_bounds"
            )
            total = jnp.where(high == g, found, total)
        picked[pl.ds(base, 8), :] = total
        return carry

    lax.fori_loop(0, block // 8, pick, 0, unroll=2)
    both = jnp.dot(wts_ref[...], table[...], preferred_element_type=f32)
    occ = occ_ref[...]
    out_ref[:, :CH] = (both[:block] + both[block:]).astype(bf16)
    out_ref[:, CH:] = (occ * (1.0 - occ) * picked[...]).astype(bf16)


def head_grads(tables, wts, occ, ctx, slots, block=256):
    pixels = occ.shape[0]
    count = 8 * CAP
    first = pl.BlockSpec((1, CAP, CH), lambda i: (0, 0, 0))
    return pl.pallas_call(
        grads_kernel,
        grid=(pixels // block,),
        out_shape=jax.ShapeDtypeStruct((pixels, 256), bf16),
        in_specs=[
            first, first, first, first,
            pl.BlockSpec((4 * CAP, CH), lambda i: (0, 0)),
            pl.BlockSpec((2 * block, count), lambda i: (i, 0)),
            pl.BlockSpec((block, 128), lambda i: (i, 0)),
            pl.BlockSpec((block, 2 * CH), lambda i: (i, 0)),
            pl.BlockSpec((block, 128), lambda i: (i, 0)),
        ],
        out_specs=pl.BlockSpec((block, 256), lambda i: (i, 0)),
        scratch_shapes=[
            pltpu.VMEM((count, CH), bf16),
            pltpu.VMEM((block, count), f32),
            pltpu.VMEM((block, 128), f32),
        ],
        compiler_params=pltpu.CompilerParams(vmem_limit_bytes=54 * MIB),
        name="head_grads",
    )(*tables, wts, occ, ctx, slots)


def inner_kernel(core_ref, x_ref, feat_ref, head_ref, keep_ref, send_ref):
    grads = head_ref[...]
    left = lax.dot_general(x_ref[...], grads, TN, preferred_element_type=f32)
    right = lax.dot_general(feat_ref[...], grads, TN, preferred_element_type=f32)
    lane = lax.broadcasted_iota(i32, (1, 128), 1)
    tail = jnp.where(lane < 64, left[:, CH:], right[:, CH:])
    full = jnp.concatenate([left[:, :CH], right[:, :CH], tail], axis=1)
    owners, half_rows, width = keep_ref.shape
    full = full.reshape(owners, 2, half_rows, width)
    first = core_ref[0] == 0
    keep_ref[...] = jnp.where(first, full[:, 0], full[:, 1])
    send_ref[...] = jnp.where(first, full[:, 1], full[:, 0])


def inner_halves(core, x_in, feat, grads, owners):
    pixels, width = x_in.shape
    step = 384
    half_rows = width // owners // 2
    per_step = step // (2 * half_rows)
    halves = jax.ShapeDtypeStruct((owners, half_rows, 384), f32)
    spec = pl.BlockSpec((per_step, half_rows, 384), lambda i: (i, 0, 0))
    return pl.pallas_call(
        inner_kernel,
        grid=(width // step,),
        out_shape=(halves, halves),
        in_specs=[
            smem(),
            pl.BlockSpec((pixels, step), lambda i: (0, i)),
            pl.BlockSpec((pixels, step), lambda i: (0, i)),
            pl.BlockSpec((pixels, 256), lambda i: (0, 0)),
        ],
        out_specs=(spec, spec),
        compiler_params=pltpu.CompilerParams(vmem_limit_bytes=54 * MIB),
        name="inner_halves",
    )(core, x_in, feat, grads)


def adam_kernel(core_ref, mine_ref, other_ref, w_ref, master_ref, first_ref, second_ref, out_m, out_f, out_s, *, scale):
    mine, other = mine_ref[...], other_ref[...]
    upper = core_ref[0] == 0
    inner = jnp.concatenate([jnp.where(upper, mine, other), jnp.where(upper, other, mine)], axis=0)
    rows = inner.shape[0]
    proj = jnp.concatenate([inner[:, :CH], inner[:, 2 * CH : 2 * CH + 64]], axis=1)
    high = proj.astype(bf16)
    rest = proj - high.astype(f32)
    mid, low = split(rest)
    three = lax.dot_general(
        jnp.concatenate([high, mid, low], axis=0), w_ref[...], NT, preferred_element_type=f32
    )
    wide = three[2 * rows :] + three[rows : 2 * rows] + three[:rows]
    tail = jnp.concatenate([inner[:, CH : 2 * CH], inner[:, 2 * CH + 64 :]], axis=1)
    gradient = jnp.concatenate([wide, tail], axis=1) * scale
    first_new = beta_one * first_ref[...] + (1.0 - beta_one) * gradient
    second_new = beta_two * second_ref[...] + (1.0 - beta_two) * gradient * gradient
    direction = first_new / bias_one / (jnp.sqrt(second_new / bias_two) + adam_epsilon)
    out_m[...] = master_ref[...] - learn_rate * direction
    out_f[...] = first_new
    out_s[...] = second_new


def adam_update(core, mine, other, w_head, master, first, second, scale):
    out = jax.ShapeDtypeStruct(master.shape, f32)
    return pl.pallas_call(
        functools.partial(adam_kernel, scale=scale),
        out_shape=(out, out, out),
        in_specs=[smem()] + [vmem()] * 6,
        out_specs=(vmem(),) * 3,
        compiler_params=pltpu.CompilerParams(vmem_limit_bytes=32 * MIB),
        name="adam_update",
    )(core, mine, other, w_head, master, first, second)


def hop(value, distance):
    return lax.ppermute(value, "cam", [(i, i ^ distance) for i in range(2 * CHIPS)])


def shards(x_in, feat, w_head, g_bev, cell_lists, point_slots, master, first_moment, second_moment):
    cam_count = lax.axis_size("cam")
    data_count = lax.axis_size("dp")
    me = lax.axis_index("cam").astype(i32)
    core = (me & 1).reshape(1)
    features = feat[0]
    pixels = features.shape[0]

    with jax.named_scope("lists"):
        lists = lax.all_to_all(cell_lists[0, 0], "cam", 0, 0, tiled=True)
    own, pair, one, two, three = gather_rows(me.reshape(1), lists.reshape(-1), g_bev[0])
    with jax.named_scope("rows"):
        one, two, three = hop(one, 2), hop(two, 4), hop(three, 6)

    slots = point_slots[0]
    tile = (slots >> 9) ^ me
    slots = jnp.where(slots < 8 * CAP, ((tile & 1) << 11) | ((tile >> 1) << 9) | (slots & (CAP - 1)), 8 * CAP)
    slots = jnp.concatenate([slots, slots], axis=1)
    w_wide = jnp.concatenate([w_head, w_head[:, CH:]], axis=1)
    w_wide, own = lax.optimization_barrier((w_wide, own))
    wts, occ, ctx = pixel_weights(features, w_wide, slots)
    with jax.named_scope("rows_pair"):
        one, two, three, ctx = lax.optimization_barrier((one, two, three, ctx))
        far = hop(jnp.concatenate([pair[0], one[1], two[1], three[1]], axis=0), 1)
    grads = head_grads((own, one, two, three, far), wts, occ, ctx, slots)

    keep, send = inner_halves(core, x_in[0], features, grads, data_count)
    with jax.named_scope("sum_pair"):
        half = (keep + hop(send, 1)).astype(bf16)
    with jax.named_scope("sum_dp"):
        half = lax.all_to_all(half, "dp", 0, 0, tiled=True)
        half = jnp.sum(half.astype(f32), axis=0)
    with jax.named_scope("sum_x"):
        half = (half + hop(half, 2)) + (hop(half, 4) + hop(half, 6))
    with jax.named_scope("share_pair"):
        other = hop(half, 1)
    scale = 1.0 / math.sqrt(data_count * cam_count * pixels)
    return adam_update(core, half, other, w_head, master, first_moment, second_moment, scale)


def solution(mesh):
    placed = (
        P("dp", "cam", None),
        P("dp", "cam", None),
        P(),
        P("dp", "cam", None),
        P("dp", "cam", None, None),
        P("dp", "cam", None),
        P("dp", None),
        P("dp", None),
        P("dp", None),
    )
    return jax.shard_map(
        shards,
        mesh=mesh,
        in_specs=placed,
        out_specs=(P("dp", None), P("dp", None), P("dp", None)),
        check_vma=False,
    )
```

time: 865 us -> 130 us (0.15)
  other arithmetic: 419 us -> 3.9 us
  waiting for transfers between devices: 327 us -> 8.45 us
  Pallas kernels: 0 us -> 65.7 us
  matrix products: 52.1 us -> 0 us
  local copies, waits for them, and re-layouts: 51.6 us -> 4.36 us
  blocking collectives: 0 us -> 26 us
  starting transfers between devices: 0.12 us -> 20.6 us
  between operations: 13.9 us -> 0.8 us
    reduce_sum x8 -> x1, other arithmetic: 411 us -> 0.09 us  [shards(): half = jnp.sum(half.astype(f32), axis=0)]
    reduce_scatter x1 -> x0, waiting for transfers between devices: 213 us -> none  [shards(): lax.psum_scatter(jnp.concatenate([inner_proj, inner_head], axis=1), 'dp',...]
    psum x1 -> x0, waiting for transfers between devices: 65.7 us -> none  [shards(): inner_full = lax.psum(inner_share, 'cam')]
    pallas_call x0 -> x5, Pallas kernels: none -> 65.7 us  [the longest x1 29.6 us: pixel_weights(): pl.pallas_call(weights_kernel, grid=(pixels // block,), out_shape=(jax.Sh...]
    dot_general x20 -> x0, matrix products: 52.1 us -> none  [the longest x8 28.2 us: block_grads(): lax.dot_general(ctx_block, table_wide, (((1,), (1,)), ((), ())), precisio...]
    all_gather x1 -> x0, waiting for transfers between devices: 47.4 us -> none  [shards(): all_tiles = lax.all_gather(bev_tile, 'cam', axis=0, tiled=True)]
    all_to_all x0 -> x1, blocking collectives: none -> 26 us  [shards(): half = lax.all_to_all(half, 'dp', 0, 0, tiled=True)]
    gather x1 -> x0, local copies, waits for them, and re-layouts: 18.8 us -> none  [shards(): row_table = all_tiles[(cell_list + offsets).reshape(-1)]]
  transfers between devices with their start and end apart: 3 -> 10, of which waited for: 3 -> 6; matrix products, arithmetic and copies ran while one was open for 1% -> 3% of each run, Pallas kernels for 0% -> 23%
where the time goes in v1:
time: 130 us
  Pallas kernels  65.7 us (51%)
  blocking collectives  26 us (20%)
  starting transfers between devices  20.6 us (16%)
  waiting for transfers between devices  8.45 us (6%)
  local copies, waits for them, and re-layouts  4.36 us (3%)
  other arithmetic  3.9 us (3%)
    pallas_call x1, Pallas kernels, pixel_weights(): pl.pallas_call(weights_kernel, grid=(pixels // block,), out_shape=(jax.Sh...  29.6 us
    all_to_all x1, blocking collectives, shards(): half = lax.all_to_all(half, 'dp', 0, 0, tiled=True)  26 us
    pallas_call x1, Pallas kernels, head_grads(): pl.pallas_call(grads_kernel, grid=(pixels // block,), out_shape=jax.Shape...  23.1 us
    ppermute x9, starting transfers between devices, hop(): lax.ppermute(value, 'cam', [(i, i ^ distance) for i in range(2 * CHIPS)])  14.1 us
    ppermute x9, waiting for transfers between devices, hop(): lax.ppermute(value, 'cam', [(i, i ^ distance) for i in range(2 * CHIPS)])  7.6 us
    all_to_all x1, starting transfers between devices, shards(): lists = lax.all_to_all(cell_lists[0, 0], 'cam', 0, 0, tiled=True)  6.48 us
    pallas_call x1, Pallas kernels, inner_halves(): pl.pallas_call(inner_kernel, grid=(width // step,), out_shape=(halves, ha...  6.07 us
    pallas_call x1, Pallas kernels, gather_rows(): pl.pallas_call(gather_kernel, out_shape=(one, one, two, two, two), in_spe...  5.48 us
  transfers between devices with their start and end apart: 10, of which 6 were waited for; matrix products, arithmetic and copies ran while one was open for 3% of the time, Pallas kernels for 23%

profile of v1, /device:TPU:1, one launch (start us, length us, event | category | flops | bytes accessed | tf_op | source)
XLA Modules:
  0.0 129.8 jit_solution(3655762176654485627)
XLA Ops:
  0.6 1.4 %all_to_all.9 = s32[8,1,512]{2,1,0:T(1,128)} reshape(s32[1,1,8,512]{3,2,1,0:T(8,128)} %param.13) | data formatting | bytes 32768 | tf_op jit(solution)/shard_map/lists/all_to_all | solution.py:306
  2.0 6.5 %all-to-all-start = ((s32[8,1,512]{2,1,0:T(1,128)}), s32[8,1,512]{2,1,0:T(1,128)S(1)}, u32[]{:S(2)}, u32[]{:S(2)}) async-start(s32[8,1,512]{2,1,0:T(1,128)} %all_to_all.9), calls=%async_computation | async-start | bytes 32768 | tf_op jit(solution)/shard_map/lists/all_to_all | solution.py:306
  8.5 1.1 copy.20
  9.7 0.3 copy.19.w_ref
  10.0 1.2 pad_maximum_fusion.w_ref
  11.1 0.2 select_bitcast_fusion
  11.3 1.0 pad_add_fusion.slot_ref
  12.3 0.8 all-to-all-done
  13.2 5.5 %gather_rows.1 = (bf16[1,512,128]{2,1,0:T(8,128)(2,1)S(1)}, bf16[1,512,128]{2,1,0:T(8,128)(2,1)S(1)}, bf16[2,512,128]{2,1,0:T(8,128)(2,1)S(1)}, bf16[2,512,128]{2,1,0:T(8,128)(2,1)S(1)}, bf16[2,512,128]{2,1,0:T(8,128)(2,1)S(1)}) custom-call(s32[1]{0:T(128)} %bitcast.3.me_ref, s32[4096]{0:T(1024)S(1)} %bitcast.19, bf16[4096,128]{1,0:T(8,128)(2,1)S(1)} %bitcast.17), custom_call_target="tpu_custom_call" | custom-call | tf_op jit(solution)/shard_map/gather_rows/pallas_call | solution.py:68
  18.7 0.6 copy-done.4
  19.3 0.6 collective-permute-start
  19.9 2.4 %collective-permute-start.1 = (bf16[2,512,128]{2,1,0:T(8,128)(2,1)S(1)}, bf16[2,512,128]{2,1,0:T(8,128)(2,1)S(1)}, u32[]{:S(2)}, u32[]{:S(2)}) collective-permute-start(bf16[2,512,128]{2,1,0:T(8,128)(2,1)S(1)} %get-tuple-element.22), channel_id=1, source_target_pairs={{0,4},{1,5},{2,6},{3,7},{4,0},{5,1},{6,2},{7,3},{8,12},{9,13},{10,... | collective-permute-start | bytes 786440 | tf_op jit(solution)/shard_map/rows/ppermute | solution.py:294
  22.3 0.9 collective-permute-start.2
  23.2 29.6 %pixel_weights.1 = (bf16[2048,4096]{1,0:T(8,128)(2,1)}, f32[1024,128]{1,0:T(8,128)}, bf16[1024,256]{1,0:T(8,128)(2,1)}) custom-call(bf16[1024,1536]{1,0:T(8,128)(2,1)} %bitcast.21, bf16[1536,256]{1,0:T(8,128)(2,1)} %pad_maximum_fusion.w_ref, s32[1024,128]{1,0:T(8,128)} %pad_add_fusion.slot_ref), custom_call_target="tpu_custom_call" | custom-call | flops 24999999488 | bytes 24000000 | tf_op jit(solution)/shard_map/pixel_weights/pallas_call | solution.py:127
  52.8 0.0 copy-start.7
  52.9 1.6 %collective-permute-start.3 = (bf16[2048,128]{1,0:T(8,128)(2,1)S(1)}, bf16[2048,128]{1,0:T(8,128)(2,1)S(1)}, u32[]{:S(2)}, u32[]{:S(2)}) collective-permute-start(bf16[2048,128]{1,0:T(8,128)(2,1)S(1)} %pad_maximum_fusion.1), channel_id=1, source_target_pairs={{0,1},{1,0},{2,3},{3,2},{4,5},{5,4},{6,7},{7,6},{8,9},{9,8},{10,11... | collective-permute-start | bytes 1572872 | tf_op jit(solution)/shard_map/rows_pair/ppermute | solution.py:294
  54.6 1.5 %collective-permute-done.3.far_ref = bf16[2048,128]{1,0:T(8,128)(2,1)S(1)} collective-permute-done((bf16[2048,128]{1,0:T(8,128)(2,1)S(1)}, bf16[2048,128]{1,0:T(8,128)(2,1)S(1)}, u32[]{:S(2)}, u32[]{:S(2)}) %collective-permute-start.3) | collective-permute-done | bytes 524320 | tf_op jit(solution)/shard_map/rows_pair/ppermute | solution.py:294
  56.1 0.8 copy-done.9
  56.9 23.1 %head_grads.1.head_ref = bf16[1024,256]{1,0:T(8,128)(2,1)} custom-call(bf16[1,512,128]{2,1,0:T(8,128)(2,1)} %copy-done.4, bf16[2,512,128]{2,1,0:T(8,128)(2,1)} %copy-done.5, bf16[2,512,128]{2,1,0:T(8,128)(2,1)} %copy-done.6, bf16[2,512,128]{2,1,0:T(8,128)(2,1)} %copy-done.7, bf16[2048,128]{1,0:T(8,128)(2,1)} %copy-done.9, ...), custom_call_target="tpu_custom_call" | custom-call | tf_op jit(solution)/shard_map/head_grads/pallas_call | solution.py:198
  80.0 6.1 %inner_halves.1 = (f32[32,24,384]{2,1,0:T(8,128)}, f32[32,24,384]{2,1,0:T(8,128)}) custom-call(s32[1]{0:T(128)} %bitcast.core_ref, bf16[1024,1536]{1,0:T(8,128)(2,1)} %bitcast.20, bf16[1024,1536]{1,0:T(8,128)(2,1)} %bitcast.22, bf16[1024,256]{1,0:T(8,128)(2,1)} %head_grads.1.head_ref), custom_call_target="tpu_custom_call" | custom-call | tf_op jit(solution)/shard_map/inner_halves/pallas_call | solution.py:242
  86.1 0.4 collective-permute-start.4
  86.5 2.7 %collective-permute-done.4 = f32[32,24,384]{2,1,0:T(8,128)S(1)} collective-permute-done((f32[32,24,384]{2,1,0:T(8,128)}, f32[32,24,384]{2,1,0:T(8,128)S(1)}, u32[]{:S(2)}, u32[]{:S(2)}) %collective-permute-start.4) | collective-permute-done | bytes 1179680 | tf_op jit(solution)/shard_map/sum_pair/ppermute | solution.py:294
  89.1 1.4 %add_convert_fusion = bf16[32,24,384]{2,1,0:T(8,128)(2,1)S(1)} fusion(f32[32,24,384]{2,1,0:T(8,128)} %get-tuple-element.33, f32[32,24,384]{2,1,0:T(8,128)S(1)} %collective-permute-done.4), kind=kLoop, calls=%fused_computation.1 | loop fusion | flops 589824 | bytes 2949120 | tf_op jit(solution)/shard_map/sum_pair/convert_element_type | solution.py:325
  90.6 26.0 %all_to_all.14 = bf16[32,24,384]{2,1,0:T(8,128)(2,1)S(1)} all-to-all(bf16[32,24,384]{2,1,0:T(8,128)(2,1)S(1)} %add_convert_fusion), channel_id=1, replica_groups=mesh['dp'=32,'cam'=8] {'dp'}, dimensions={0} | all-to-all | bytes 1179648 | tf_op jit(solution)/shard_map/sum_dp/all_to_all | solution.py:327
  116.6 0.1 convert_reduce_fusion
  116.7 1.5 %collective-permute-start.7 = (f32[24,384]{1,0:T(8,128)S(1)}, f32[24,384]{1,0:T(8,128)S(1)}, u32[]{:S(2)}, u32[]{:S(2)}) collective-permute-start(f32[24,384]{1,0:T(8,128)S(1)} %convert_reduce_fusion), channel_id=1, source_target_pairs={{0,6},{1,7},{2,4},{3,5},{4,2},{5,3},{6,0},{7,1},{8,14},{9,15},{10,... | collective-permute-start | bytes 110600 | tf_op jit(solution)/shard_map/sum_x/ppermute | solution.py:294
  118.2 1.8 %collective-permute-start.5 = (f32[24,384]{1,0:T(8,128)S(1)}, f32[24,384]{1,0:T(8,128)S(1)}, u32[]{:S(2)}, u32[]{:S(2)}) collective-permute-start(f32[24,384]{1,0:T(8,128)S(1)} %convert_reduce_fusion), channel_id=1, source_target_pairs={{0,2},{1,3},{2,0},{3,1},{4,6},{5,7},{6,4},{7,5},{8,10},{9,11},{10,... | collective-permute-start | bytes 110600 | tf_op jit(solution)/shard_map/sum_x/ppermute | solution.py:294
  120.0 0.8 collective-permute-done.7
  120.8 1.7 %collective-permute-done.6 = f32[24,384]{1,0:T(8,128)S(1)} collective-permute-done((f32[24,384]{1,0:T(8,128)S(1)}, f32[24,384]{1,0:T(8,128)S(1)}, u32[]{:S(2)}, u32[]{:S(2)}) %collective-permute-start.6) | collective-permute-done | bytes 36896 | tf_op jit(solution)/shard_map/sum_x/ppermute | solution.py:294
  122.5 4.9 %collective-permute-start.8 = (f32[24,384]{1,0:T(8,128)S(1)}, f32[24,384]{1,0:T(8,128)S(1)}, u32[]{:S(2)}, u32[]{:S(2)}) collective-permute-start(f32[24,384]{1,0:T(8,128)S(1)} %add_add_fusion.mine_ref), channel_id=1, source_target_pairs={{0,1},{1,0},{2,3},{3,2},{4,5},{5,4},{6,7},{7,6},{8,9},{9,8},{10,11... | collective-permute-start | bytes 110600 | tf_op jit(solution)/shard_map/share_pair/ppermute | solution.py:294
  127.5 0.9 collective-permute-done.8.other_ref
  128.3 1.5 %adam_update.1 = (f32[48,1728]{1,0:T(8,128)}, f32[48,1728]{1,0:T(8,128)}, f32[48,1728]{1,0:T(8,128)}) custom-call(s32[1]{0:T(128)} %bitcast.core_ref, f32[24,384]{1,0:T(8,128)S(1)} %add_add_fusion.mine_ref, f32[24,384]{1,0:T(8,128)S(1)} %collective-permute-done.8.other_ref, bf16[1536,192]{1,0:T(8,128)(2,1)S(1)} %copy.19.w_ref, f32[48,1728]{1,0:T(8,128)S(1)} %copy-done.1, ...), custom_call_target="tpu_custom_call" | custom-call | tf_op jit(solution)/shard_map/adam_update/pallas_call | solution.py:283
  (27 shorter events, 0.2 us)
Async XLA Ops:
  0.6 9.0 %copy-start.8 = (bf16[1536,192]{0,1:T(8,128)(2,1)S(1)}, bf16[1536,192]{0,1:T(8,128)(2,1)}, u32[]{:S(2)}) copy-start(bf16[1536,192]{0,1:T(8,128)(2,1)} %param.11) | copy-start | bytes 1769476
  2.0 11.2 %all-to-all-start = ((s32[8,1,512]{2,1,0:T(1,128)}), s32[8,1,512]{2,1,0:T(1,128)S(1)}, u32[]{:S(2)}, u32[]{:S(2)}) async-start(s32[8,1,512]{2,1,0:T(1,128)} %all_to_all.9), calls=%async_computation | async-start | bytes 32768 | tf_op jit(solution)/shard_map/lists/all_to_all | solution.py:306
  11.1 2.0 %copy-start = (bf16[1,4096,128]{2,1,0:T(8,128)(2,1)S(1)}, bf16[1,4096,128]{2,1,0:T(8,128)(2,1)}, u32[]{:S(2)}) copy-start(bf16[1,4096,128]{2,1,0:T(8,128)(2,1)} %param.12) | copy-start | bytes 3145732
  18.7 0.7 copy-start.4
  19.3 33.4 %collective-permute-start = (bf16[2,512,128]{2,1,0:T(8,128)(2,1)S(1)}, bf16[2,512,128]{2,1,0:T(8,128)(2,1)S(1)}, u32[]{:S(2)}, u32[]{:S(2)}) collective-permute-start(bf16[2,512,128]{2,1,0:T(8,128)(2,1)S(1)} %get-tuple-element.21), channel_id=1, source_target_pairs={{0,2},{1,3},{2,0},{3,1},{4,6},{5,7},{6,4},{7,5},{8,10},{9,11},{10,... | collective-permute-start | bytes 786440 | tf_op jit(solution)/shard_map/rows/ppermute | solution.py:294
  19.9 32.9 %collective-permute-start.1 = (bf16[2,512,128]{2,1,0:T(8,128)(2,1)S(1)}, bf16[2,512,128]{2,1,0:T(8,128)(2,1)S(1)}, u32[]{:S(2)}, u32[]{:S(2)}) collective-permute-start(bf16[2,512,128]{2,1,0:T(8,128)(2,1)S(1)} %get-tuple-element.22), channel_id=1, source_target_pairs={{0,4},{1,5},{2,6},{3,7},{4,0},{5,1},{6,2},{7,3},{8,12},{9,13},{10,... | collective-permute-start | bytes 786440 | tf_op jit(solution)/shard_map/rows/ppermute | solution.py:294
  22.3 30.5 %collective-permute-start.2 = (bf16[2,512,128]{2,1,0:T(8,128)(2,1)S(1)}, bf16[2,512,128]{2,1,0:T(8,128)(2,1)S(1)}, u32[]{:S(2)}, u32[]{:S(2)}) collective-permute-start(bf16[2,512,128]{2,1,0:T(8,128)(2,1)S(1)} %get-tuple-element.23), channel_id=1, source_target_pairs={{0,6},{1,7},{2,4},{3,5},{4,2},{5,3},{6,0},{7,1},{8,14},{9,15},{10,... | collective-permute-start | bytes 786440 | tf_op jit(solution)/shard_map/rows/ppermute | solution.py:294
  52.8 3.3 %copy-start.5 = (bf16[2,512,128]{2,1,0:T(8,128)(2,1)}, bf16[2,512,128]{2,1,0:T(8,128)(2,1)S(1)}, u32[]{:S(2)}) copy-start(bf16[2,512,128]{2,1,0:T(8,128)(2,1)S(1)} %collective-permute-done.one_ref) | copy-start | bytes 786436
  52.8 3.3 %copy-start.6 = (bf16[2,512,128]{2,1,0:T(8,128)(2,1)}, bf16[2,512,128]{2,1,0:T(8,128)(2,1)S(1)}, u32[]{:S(2)}) copy-start(bf16[2,512,128]{2,1,0:T(8,128)(2,1)S(1)} %collective-permute-done.1.two_ref) | copy-start | bytes 786436
  52.8 3.3 %copy-start.7 = (bf16[2,512,128]{2,1,0:T(8,128)(2,1)}, bf16[2,512,128]{2,1,0:T(8,128)(2,1)S(1)}, u32[]{:S(2)}) copy-start(bf16[2,512,128]{2,1,0:T(8,128)(2,1)S(1)} %collective-permute-done.2.three_ref) | copy-start | bytes 786436
  52.9 3.2 %collective-permute-start.3 = (bf16[2048,128]{1,0:T(8,128)(2,1)S(1)}, bf16[2048,128]{1,0:T(8,128)(2,1)S(1)}, u32[]{:S(2)}, u32[]{:S(2)}) collective-permute-start(bf16[2048,128]{1,0:T(8,128)(2,1)S(1)} %pad_maximum_fusion.1), channel_id=1, source_target_pairs={{0,1},{1,0},{2,3},{3,2},{4,5},{5,4},{6,7},{7,6},{8,9},{9,8},{10,11... | collective-permute-start | bytes 1572872 | tf_op jit(solution)/shard_map/rows_pair/ppermute | solution.py:294
  56.1 0.8 copy-start.9
  86.1 3.1 %collective-permute-start.4 = (f32[32,24,384]{2,1,0:T(8,128)}, f32[32,24,384]{2,1,0:T(8,128)S(1)}, u32[]{:S(2)}, u32[]{:S(2)}) collective-permute-start(f32[32,24,384]{2,1,0:T(8,128)} %get-tuple-element.34), channel_id=1, source_target_pairs={{0,1},{1,0},{2,3},{3,2},{4,5},{5,4},{6,7},{7,6},{8,9},{9,8},{10,11... | collective-permute-start | bytes 3538952 | tf_op jit(solution)/shard_map/sum_pair/ppermute | solution.py:294
  90.6 37.8 %copy-start.1 = (f32[48,1728]{1,0:T(8,128)S(1)}, f32[48,1728]{1,0:T(8,128)}, u32[]{:S(2)}) copy-start(f32[48,1728]{1,0:T(8,128)} %master_ref.1) | copy-start | bytes 995332
  90.6 37.8 %copy-start.2 = (f32[48,1728]{1,0:T(8,128)S(1)}, f32[48,1728]{1,0:T(8,128)}, u32[]{:S(2)}) copy-start(f32[48,1728]{1,0:T(8,128)} %first_ref.1) | copy-start | bytes 995332
  90.6 37.8 %copy-start.3 = (f32[48,1728]{1,0:T(8,128)S(1)}, f32[48,1728]{1,0:T(8,128)}, u32[]{:S(2)}) copy-start(f32[48,1728]{1,0:T(8,128)} %second_ref.1) | copy-start | bytes 995332
  116.7 4.1 %collective-permute-start.7 = (f32[24,384]{1,0:T(8,128)S(1)}, f32[24,384]{1,0:T(8,128)S(1)}, u32[]{:S(2)}, u32[]{:S(2)}) collective-permute-start(f32[24,384]{1,0:T(8,128)S(1)} %convert_reduce_fusion), channel_id=1, source_target_pairs={{0,6},{1,7},{2,4},{3,5},{4,2},{5,3},{6,0},{7,1},{8,14},{9,15},{10,... | collective-permute-start | bytes 110600 | tf_op jit(solution)/shard_map/sum_x/ppermute | solution.py:294
  118.2 4.3 %collective-permute-start.6 = (f32[24,384]{1,0:T(8,128)S(1)}, f32[24,384]{1,0:T(8,128)S(1)}, u32[]{:S(2)}, u32[]{:S(2)}) collective-permute-start(f32[24,384]{1,0:T(8,128)S(1)} %convert_reduce_fusion), channel_id=1, source_target_pairs={{0,4},{1,5},{2,6},{3,7},{4,0},{5,1},{6,2},{7,3},{8,12},{9,13},{10,... | collective-permute-start | bytes 110600 | tf_op jit(solution)/shard_map/sum_x/ppermute | solution.py:294
  118.2 4.3 %collective-permute-start.5 = (f32[24,384]{1,0:T(8,128)S(1)}, f32[24,384]{1,0:T(8,128)S(1)}, u32[]{:S(2)}, u32[]{:S(2)}) collective-permute-start(f32[24,384]{1,0:T(8,128)S(1)} %convert_reduce_fusion), channel_id=1, source_target_pairs={{0,2},{1,3},{2,0},{3,1},{4,6},{5,7},{6,4},{7,5},{8,10},{9,11},{10,... | collective-permute-start | bytes 110600 | tf_op jit(solution)/shard_map/sum_x/ppermute | solution.py:294
  122.5 5.8 %collective-permute-start.8 = (f32[24,384]{1,0:T(8,128)S(1)}, f32[24,384]{1,0:T(8,128)S(1)}, u32[]{:S(2)}, u32[]{:S(2)}) collective-permute-start(f32[24,384]{1,0:T(8,128)S(1)} %add_add_fusion.mine_ref), channel_id=1, source_target_pairs={{0,1},{1,0},{2,3},{3,2},{4,5},{5,4},{6,7},{7,6},{8,9},{9,8},{10,11... | collective-permute-start | bytes 110600 | tf_op jit(solution)/shard_map/share_pair/ppermute | solution.py:294

commit v2 on v1

v2 whole, which is shorter than its diff:
```python
import functools
import math

import jax
import jax.numpy as jnp
from jax import lax
from jax.experimental import pallas as pl
from jax.experimental.pallas import tpu as pltpu
from jax.sharding import PartitionSpec as P

beta_one = 0.9
beta_two = 0.999
bias_one = 0.9999734386011124
bias_two = 0.0952078528862911
learn_rate = 0.01
adam_epsilon = 1e-08

bf16 = jnp.bfloat16
f32 = jnp.float32
i32 = jnp.int32

NT = (((1,), (1,)), ((), ()))
TN = (((0,), (0,)), ((), ()))

CHIPS = 4
CAP = 512
CH = 128
MIB = 1 << 20


def vmem():
    return pl.BlockSpec(memory_space=pltpu.VMEM)


def smem():
    return pl.BlockSpec(memory_space=pltpu.SMEM)


def split(value):
    high = value.astype(bf16)
    return high, (value - high.astype(f32)).astype(bf16)


def gather_kernel(me_ref, lists_ref, tile_ref, own_ref, pair_ref, one_ref, two_ref, three_ref, wide, rows):
    wide[...] = tile_ref[...].astype(f32)
    me = me_ref[0]
    places = (
        (own_ref, 0), (pair_ref, 0), (one_ref, 0), (one_ref, 1),
        (two_ref, 0), (two_ref, 1), (three_ref, 0), (three_ref, 1),
    )
    for block, (ref, part) in enumerate(places):
        start = jnp.bitwise_xor(me, block) * CAP

        def step(i, carry):
            base = i * 16
            for u in range(16):
                cell = lists_ref[start + base + u]
                rows[pl.ds(base + u, 1), :] = wide[pl.ds(cell, 1), :]
            return carry

        lax.fori_loop(0, CAP // 16, step, 0)
        ref[part] = rows[...].astype(bf16)


def gather_rows(me, lists, tile):
    one = jax.ShapeDtypeStruct((1, CAP, CH), bf16)
    two = jax.ShapeDtypeStruct((2, CAP, CH), bf16)
    return pl.pallas_call(
        gather_kernel,
        out_shape=(one, one, two, two, two),
        in_specs=[smem(), smem(), vmem()],
        out_specs=(vmem(),) * 5,
        scratch_shapes=[pltpu.VMEM(tile.shape, f32), pltpu.VMEM((CAP, CH), f32)],
        compiler_params=pltpu.CompilerParams(vmem_limit_bytes=16 * MIB),
        name="gather_rows",
    )(me, lists, tile)


def weights_kernel(me_ref, feat_ref, w_ref, slot_ref, wts_ref, occ_ref, ctx_ref, place_ref):
    block = feat_ref.shape[0]
    head = lax.dot_general(feat_ref[...], w_ref[...], NT, preferred_element_type=f32)
    ctx_ref[:, :CH], ctx_ref[:, CH:] = split(head[:, :CH])
    occ = 1.0 / (1.0 + jnp.exp(-head[:, CH:]))
    occ_ref[...] = jnp.concatenate([occ, occ], axis=1)
    slots = slot_ref[...]
    tile = (slots >> 9) ^ me_ref[0]
    slots = jnp.where(slots < 8 * CAP, ((tile & 1) << 11) | ((tile >> 1) << 9) | (slots & (CAP - 1)), 8 * CAP)
    place_ref[...] = jnp.concatenate([slots, slots], axis=1)
    lane = lax.broadcasted_iota(i32, (1, 128), 1)
    lane16 = lax.broadcasted_iota(i32, (16, 128), 1)
    sub16 = lax.broadcasted_iota(i32, (16, 128), 0)
    half16 = (lane16 >= 64).astype(i32)
    masks = [((sub16 & 7) == 2 * j + half16).astype(f32).astype(bf16) for j in range(4)]
    low_rows = [(sub16 + 16 * t).astype(f32).astype(bf16) for t in range(16)]
    zero = jnp.zeros((16, 128), bf16)
    one = jnp.ones((16, 128), bf16)

    def build(i, carry):
        base = pl.multiple_of(i * 16, 16)
        pair = []
        for q in range(2):
            slot = place_ref[pl.ds(base + q * 8, 8), :]
            occ = occ_ref[pl.ds(base + q * 8, 8), :]
            high = (slot >> 8).astype(f32)
            low = (slot & 255).astype(f32)
            key = jnp.concatenate([high, high - 1.0], axis=0).astype(bf16)
            hits = [key == jnp.asarray(2.0 * t, bf16) for t in range(8)]
            occ_high, occ_low = split(jnp.concatenate([occ, occ], axis=0))
            left_high, left_low, right = [], [], []
            for j in range(4):
                part_high = occ_high * masks[j]
                part_low = occ_low * masks[j]
                left_high.append(jnp.concatenate([jnp.where(hit, part_high, zero) for hit in hits], axis=0))
                left_low.append(jnp.concatenate([jnp.where(hit, part_low, zero) for hit in hits], axis=0))
                row = jnp.where(lane < 64, low[2 * j : 2 * j + 1], low[2 * j + 1 : 2 * j + 2])
                row = jnp.broadcast_to(row, (16, 128)).astype(bf16)
                right.append(jnp.concatenate([jnp.where(rows == row, one, zero) for rows in low_rows], axis=0))
            left = jnp.concatenate(
                [jnp.concatenate(left_high, axis=1), jnp.concatenate(left_low, axis=1)], axis=0
            )
            both = lax.dot_general(left, jnp.concatenate(right, axis=1), NT, preferred_element_type=f32)
            pair.append(both[:128] + both[128:])
        for h in range(16):
            rows = slice(h * 8, h * 8 + 8)
            value = jnp.concatenate([pair[0][rows], pair[1][rows]], axis=0)
            columns = slice(h * 256, h * 256 + 256)
            wts_ref[pl.ds(base, 16), columns], wts_ref[pl.ds(block + base, 16), columns] = split(value)
        return carry

    lax.fori_loop(0, block // 16, build, 0, unroll=8)


def pixel_weights(me, feat, w_head, slots, block=256):
    pixels, width = feat.shape
    depth = slots.shape[1]
    table = 8 * CAP
    return pl.pallas_call(
        weights_kernel,
        grid=(pixels // block,),
        out_shape=(
            jax.ShapeDtypeStruct((2 * pixels, table), bf16),
            jax.ShapeDtypeStruct((pixels, 128), f32),
            jax.ShapeDtypeStruct((pixels, 2 * CH), bf16),
            jax.ShapeDtypeStruct((pixels, 128), i32),
        ),
        in_specs=[
            smem(),
            pl.BlockSpec((block, width), lambda i: (i, 0)),
            pl.BlockSpec(w_head.shape, lambda i: (0, 0)),
            pl.BlockSpec((block, depth), lambda i: (i, 0)),
        ],
        out_specs=(
            pl.BlockSpec((2 * block, table), lambda i: (i, 0)),
            pl.BlockSpec((block, 128), lambda i: (i, 0)),
            pl.BlockSpec((block, 2 * CH), lambda i: (i, 0)),
            pl.BlockSpec((block, 128), lambda i: (i, 0)),
        ),
        compiler_params=pltpu.CompilerParams(vmem_limit_bytes=50 * MIB),
        cost_estimate=pl.CostEstimate(flops=20 * 10**9, bytes_accessed=24 * 10**6, transcendentals=0),
        name="pixel_weights",
    )(me, feat, w_head, slots)


def grads_kernel(
    core_ref, own_ref, one_ref, two_ref, three_ref, far_ref, wts_ref, occ_ref, place_ref, ctx_ref, x_hbm, feat_hbm,
    keep_ref, send_ref, table, flip, scores, mixed, picked, head, x_in, feat, sems,
):
    step = pl.program_id(0)
    last = pl.num_programs(0) - 1
    block = occ_ref.shape[0]
    count = table.shape[0]
    chunks = count // 256
    x_copy = pltpu.make_async_copy(x_hbm, x_in, sems.at[0])
    feat_copy = pltpu.make_async_copy(feat_hbm, feat, sems.at[1])

    def score(i):
        columns = pl.ds(pl.multiple_of(i * 256, 256), 256)
        part = flip[:, columns]
        scores[step % 2, :, columns] = jnp.dot(
            ctx_ref[...], jnp.concatenate([part, part], axis=0), preferred_element_type=f32
        )

    def pick(i):
        old = (step + 1) % 2
        for q in range(block // chunks // 8):
            base = pl.multiple_of(i * (block // chunks), 8) + q * 8
            place = place_ref[pl.ds(base, 8), :]
            low = place & 127
            high = place >> 7
            total = jnp.zeros((8, 128), f32)
            for g in range(count // 128):
                found = jnp.take_along_axis(
                    scores[old, pl.ds(base, 8), g * 128 : (g + 1) * 128], low, axis=1, mode="promise_in_bounds"
                )
                total = jnp.where(high == g, found, total)
            picked[pl.ds(base, 8), :] = total

    def mix(i):
        rows = pl.ds(pl.multiple_of(i * 256, 256), 256)
        mixed[...] += jnp.dot(wts_ref[:, rows], table[rows, :], preferred_element_type=f32)

    def finish():
        rows = pl.ds(pl.multiple_of((step - 1) * block, block), block)
        occ = occ_ref[...]
        head[rows, :CH] = (mixed[:block] + mixed[block:]).astype(bf16)
        head[rows, CH:] = (occ * (1.0 - occ) * picked[...]).astype(bf16)

    @pl.when(step == 0)
    def _():
        x_copy.start()
        feat_copy.start()
        for k, ref in enumerate((own_ref, one_ref, two_ref, three_ref)):
            table[k * CAP : (k + 1) * CAP, :] = ref[0]
        table[4 * CAP :, :] = far_ref[...]

        def body(i, carry):
            rows = pl.ds(pl.multiple_of(i * 256, 256), 256)
            flip[:, rows] = table[rows, :].T
            score(i)
            return carry

        lax.fori_loop(0, chunks, body, 0, unroll=8)

    @pl.when((step > 0) & (step < last))
    def _():
        mixed[...] = jnp.zeros_like(mixed)

        def body(i, carry):
            score(i)
            pick(i)
            mix(i)
            return carry

        lax.fori_loop(0, chunks, body, 0, unroll=8)
        finish()

    @pl.when(step == last)
    def _():
        mixed[...] = jnp.zeros_like(mixed)

        def body(i, carry):
            pick(i)
            mix(i)
            return carry

        lax.fori_loop(0, chunks, body, 0, unroll=8)
        finish()
        x_copy.wait()
        feat_copy.wait()
        owners, half_rows, width = keep_ref.shape
        span = 384
        per_span = span // (2 * half_rows)
        grads = head[...]
        lane = lax.broadcasted_iota(i32, (1, 128), 1)
        first = core_ref[0] == 0
        for n in range(x_in.shape[1] // span):
            columns = slice(n * span, (n + 1) * span)
            left = lax.dot_general(x_in[:, columns], grads, TN, preferred_element_type=f32)
            right = lax.dot_general(feat[:, columns], grads, TN, preferred_element_type=f32)
            tail = jnp.where(lane < 64, left[:, CH:], right[:, CH:])
            full = jnp.concatenate([left[:, :CH], right[:, :CH], tail], axis=1)
            full = full.reshape(per_span, 2, half_rows, width)
            part = slice(n * per_span, (n + 1) * per_span)
            keep_ref[part] = jnp.where(first, full[:, 0], full[:, 1])
            send_ref[part] = jnp.where(first, full[:, 1], full[:, 0])


def inner_halves(core, tables, wts, occ, places, ctx, x_in, feat, owners, block=256):
    pixels, width = feat.shape
    count = 8 * CAP
    blocks = pixels // block
    first = pl.BlockSpec((1, CAP, CH), lambda i: (0, 0, 0))
    halves = jax.ShapeDtypeStruct((owners, width // owners // 2, 384), f32)

    def behind(i):
        return (jnp.maximum(i - 1, 0), 0)

    return pl.pallas_call(
        grads_kernel,
        grid=(blocks + 1,),
        out_shape=(halves, halves),
        in_specs=[
            smem(),
            first, first, first, first,
            pl.BlockSpec((4 * CAP, CH), lambda i: (0, 0)),
            pl.BlockSpec((2 * block, count), behind),
            pl.BlockSpec((block, 128), behind),
            pl.BlockSpec((block, 128), behind),
            pl.BlockSpec((block, 2 * CH), lambda i: (jnp.minimum(i, blocks - 1), 0)),
            pl.BlockSpec(memory_space=pl.ANY),
            pl.BlockSpec(memory_space=pl.ANY),
        ],
        out_specs=(vmem(), vmem()),
        scratch_shapes=[
            pltpu.VMEM((count, CH), bf16),
            pltpu.VMEM((CH, count), bf16),
            pltpu.VMEM((2, block, count), f32),
            pltpu.VMEM((2 * block, CH), f32),
            pltpu.VMEM((block, 128), f32),
            pltpu.VMEM((pixels, 256), bf16),
            pltpu.VMEM((pixels, width), bf16),
            pltpu.VMEM((pixels, width), bf16),
            pltpu.SemaphoreType.DMA((2,)),
        ],
        compiler_params=pltpu.CompilerParams(vmem_limit_bytes=50 * MIB),
        name="inner_halves",
    )(core, *tables, wts, occ, places, ctx, x_in, feat)


def adam_kernel(core_ref, mine_ref, other_ref, w_ref, master_ref, first_ref, second_ref, out_m, out_f, out_s, *, scale):
    mine, other = mine_ref[...], other_ref[...]
    upper = core_ref[0] == 0
    inner = jnp.concatenate([jnp.where(upper, mine, other), jnp.where(upper, other, mine)], axis=0)
    rows = inner.shape[0]
    proj = jnp.concatenate([inner[:, :CH], inner[:, 2 * CH : 2 * CH + 64]], axis=1)
    high = proj.astype(bf16)
    rest = proj - high.astype(f32)
    mid, low = split(rest)
    three = jnp.dot(jnp.concatenate([high, mid, low], axis=0), w_ref[...], preferred_element_type=f32)
    wide = three[2 * rows :] + three[rows : 2 * rows] + three[:rows]
    tail = jnp.concatenate([inner[:, CH : 2 * CH], inner[:, 2 * CH + 64 :]], axis=1)
    gradient = jnp.concatenate([wide, tail], axis=1) * scale
    first_new = beta_one * first_ref[...] + (1.0 - beta_one) * gradient
    second_new = beta_two * second_ref[...] + (1.0 - beta_two) * gradient * gradient
    direction = first_new / bias_one / (jnp.sqrt(second_new / bias_two) + adam_epsilon)
    out_m[...] = master_ref[...] - learn_rate * direction
    out_f[...] = first_new
    out_s[...] = second_new


def adam_update(core, mine, other, w_head, master, first, second, scale):
    out = jax.ShapeDtypeStruct(master.shape, f32)
    return pl.pallas_call(
        functools.partial(adam_kernel, scale=scale),
        out_shape=(out, out, out),
        in_specs=[smem()] + [vmem()] * 6,
        out_specs=(vmem(),) * 3,
        compiler_params=pltpu.CompilerParams(vmem_limit_bytes=32 * MIB),
        name="adam_update",
    )(core, mine, other, w_head, master, first, second)


def hop(value, distance):
    return lax.ppermute(value, "cam", [(i, i ^ distance) for i in range(2 * CHIPS)])


def shards(x_in, feat, w_head, g_bev, cell_lists, point_slots, master, first_moment, second_moment):
    cam_count = lax.axis_size("cam")
    data_count = lax.axis_size("dp")
    me = lax.axis_index("cam").astype(i32)
    core = (me & 1).reshape(1)
    features = feat[0]
    pixels = features.shape[0]
    w_head = w_head.T

    with jax.named_scope("lists"):
        lists = lax.all_to_all(cell_lists[0, 0], "cam", 0, 0, tiled=True)
    own, pair, one, two, three = gather_rows(me.reshape(1), lists.reshape(-1), g_bev[0])
    with jax.named_scope("rows"):
        one, two, three = hop(one, 2), hop(two, 4), hop(three, 6)

    w_head_late, own = lax.optimization_barrier((w_head, own))
    wts, occ, ctx, places = pixel_weights(me.reshape(1), features, w_head_late, point_slots[0])
    with jax.named_scope("rows_pair"):
        one, two, three, ctx = lax.optimization_barrier((one, two, three, ctx))
        far = hop(jnp.concatenate([pair[0], one[1], two[1], three[1]], axis=0), 1)
    keep, send = inner_halves(
        core, (own, one, two, three, far), wts, occ, places, ctx, x_in[0], features, data_count
    )
    with jax.named_scope("sum_pair"):
        half = (keep + hop(send, 1)).astype(bf16)
    with jax.named_scope("sum_dp"):
        half = lax.all_to_all(half, "dp", 0, 0, tiled=True)
        half = jnp.sum(half.astype(f32), axis=0)
    with jax.named_scope("sum_x"):
        half = (half + hop(half, 2)) + (hop(half, 4) + hop(half, 6))
    with jax.named_scope("share_pair"):
        other = hop(half, 1)
    scale = 1.0 / math.sqrt(data_count * cam_count * pixels)
    return adam_update(core, half, other, w_head, master, first_moment, second_moment, scale)


def solution(mesh):
    placed = (
        P("dp", "cam", None),
        P("dp", "cam", None),
        P(),
        P("dp", "cam", None),
        P("dp", "cam", None, None),
        P("dp", "cam", None),
        P("dp", None),
        P("dp", None),
        P("dp", None),
    )
    return jax.shard_map(
        shards,
        mesh=mesh,
        in_specs=placed,
        out_specs=(P("dp", None), P("dp", None), P("dp", None)),
        check_vma=False,
    )
```

time: 130 us -> 105 us (0.81)
  Pallas kernels: 65.7 us -> 38.5 us
  waiting for transfers between devices: 8.45 us -> 10.8 us
  other arithmetic: 3.9 us -> 2.35 us
    pallas_call x1, Pallas kernels: 29.6 us -> 15.4 us  [pixel_weights(): pl.pallas_call(weights_kernel, grid=(pixels // block,), out_shape=(jax.Sh...]
    pallas_call x2 -> x1, Pallas kernels: 29.2 us -> 16.2 us  [inner_halves(): pl.pallas_call(grads_kernel, grid=(blocks + 1,), out_shape=(halves, halve...]
    all_to_all x1, waiting for transfers between devices: 0.84 us -> 3.52 us  [shards(): lists = lax.all_to_all(cell_lists[0, 0], 'cam', 0, 0, tiled=True)]
    concatenate x2 -> x0, other arithmetic: 2.16 us -> none  [the longest x1 1.16 us: shards(): w_wide = jnp.concatenate([w_head, w_head[:, CH:]], axis=1)]
    unnamed x22 -> x15, local copies, waits for them, and re-layouts: 2.91 us -> 3.94 us
  transfers between devices with their start and end apart: 10 -> 10, of which waited for: 6 -> 6; matrix products, arithmetic and copies ran while one was open for 3% -> 1% of each run, Pallas kernels for 23% -> 15%
where the time goes in v2:
time: 105 us; the launch traced here: 104 us
  Pallas kernels  38.5 us (37%)
  blocking collectives  26 us (25%)
  starting transfers between devices  20.6 us (20%)
  waiting for transfers between devices  10.8 us (10%)
  local copies, waits for them, and re-layouts  5.37 us (5%)
  other arithmetic  2.35 us (2%)
    all_to_all x1, blocking collectives, shards(): half = lax.all_to_all(half, 'dp', 0, 0, tiled=True)  26 us
    pallas_call x1, Pallas kernels, inner_halves(): pl.pallas_call(grads_kernel, grid=(blocks + 1,), out_shape=(halves, halve...  16.2 us
    pallas_call x1, Pallas kernels, pixel_weights(): pl.pallas_call(weights_kernel, grid=(pixels // block,), out_shape=(jax.Sh...  15.4 us
    ppermute x9, starting transfers between devices, hop(): lax.ppermute(value, 'cam', [(i, i ^ distance) for i in range(2 * CHIPS)])  14.2 us
    ppermute x9, waiting for transfers between devices, hop(): lax.ppermute(value, 'cam', [(i, i ^ distance) for i in range(2 * CHIPS)])  7.25 us
    all_to_all x1, starting transfers between devices, shards(): lists = lax.all_to_all(cell_lists[0, 0], 'cam', 0, 0, tiled=True)  6.48 us
    pallas_call x1, Pallas kernels, gather_rows(): pl.pallas_call(gather_kernel, out_shape=(one, one, two, two, two), in_spe...  5.48 us
    unnamed x15, local copies, waits for them, and re-layouts  3.94 us
  transfers between devices with their start and end apart: 10, of which 6 were waited for; matrix products, arithmetic and copies ran while one was open for 1% of the time, Pallas kernels for 15%

profile of v2, /device:TPU:1, one launch (start us, length us, event | category | flops | bytes accessed | tf_op | source)
XLA Modules:
  0.0 104.3 jit_solution(8990510081322059141)
XLA Ops:
  0.6 1.4 %all_to_all.9 = s32[8,1,512]{2,1,0:T(1,128)} reshape(s32[1,1,8,512]{3,2,1,0:T(8,128)} %param.13) | data formatting | bytes 32768 | tf_op jit(solution)/shard_map/lists/all_to_all | solution.py:357
  2.0 6.5 %all-to-all-start = ((s32[8,1,512]{2,1,0:T(1,128)}), s32[8,1,512]{2,1,0:T(1,128)S(1)}, u32[]{:S(2)}, u32[]{:S(2)}) async-start(s32[8,1,512]{2,1,0:T(1,128)} %all_to_all.9), calls=%async_computation | async-start | bytes 32768 | tf_op jit(solution)/shard_map/lists/all_to_all | solution.py:357
  8.5 1.1 %copy.13 = s32[1,1024,64]{2,1,0:T(8,128)S(1)} copy(s32[1,1024,64]{1,2,0:T(8,128)} %param.14) | data formatting | bytes 524288 | tf_op args[5]
  9.7 3.5 %all-to-all-done = s32[8,1,512]{2,1,0:T(1,128)S(1)} async-done(((s32[8,1,512]{2,1,0:T(1,128)}), s32[8,1,512]{2,1,0:T(1,128)S(1)}, u32[]{:S(2)}, u32[]{:S(2)}) %all-to-all-start) | async-done | bytes 16416 | tf_op jit(solution)/shard_map/lists/all_to_all | solution.py:357
  13.2 1.2 %copy-done = bf16[1,4096,128]{2,1,0:T(8,128)(2,1)S(1)} copy-done((bf16[1,4096,128]{2,1,0:T(8,128)(2,1)S(1)}, bf16[1,4096,128]{2,1,0:T(8,128)(2,1)}, u32[]{:S(2)}) %copy-start) | copy-done | bytes 1048600
  14.4 5.5 %gather_rows.1 = (bf16[1,512,128]{2,1,0:T(8,128)(2,1)S(1)}, bf16[1,512,128]{2,1,0:T(8,128)(2,1)S(1)}, bf16[2,512,128]{2,1,0:T(8,128)(2,1)S(1)}, bf16[2,512,128]{2,1,0:T(8,128)(2,1)S(1)}, bf16[2,512,128]{2,1,0:T(8,128)(2,1)S(1)}) custom-call(s32[1]{0:T(128)} %bitcast.2.me_ref, s32[4096]{0:T(1024)S(1)} %bitcast.22, bf16[4096,128]{1,0:T(8,128)(2,1)S(1)} %bitcast.17), custom_call_target="tpu_custom_call" | custom-call | tf_op jit(solution)/shard_map/gather_rows/pallas_call | solution.py:68
  19.9 0.0 copy-start.5
  19.9 0.6 copy-done.5
  20.6 0.3 collective-permute-start
  20.9 1.8 %collective-permute-start.1 = (bf16[2,512,128]{2,1,0:T(8,128)(2,1)S(1)}, bf16[2,512,128]{2,1,0:T(8,128)(2,1)S(1)}, u32[]{:S(2)}, u32[]{:S(2)}) collective-permute-start(bf16[2,512,128]{2,1,0:T(8,128)(2,1)S(1)} %get-tuple-element.23), channel_id=1, source_target_pairs={{0,4},{1,5},{2,6},{3,7},{4,0},{5,1},{6,2},{7,3},{8,12},{9,13},{10,... | collective-permute-start | bytes 786440 | tf_op jit(solution)/shard_map/rows/ppermute | solution.py:344
  22.6 1.8 %collective-permute-start.2 = (bf16[2,512,128]{2,1,0:T(8,128)(2,1)S(1)}, bf16[2,512,128]{2,1,0:T(8,128)(2,1)S(1)}, u32[]{:S(2)}, u32[]{:S(2)}) collective-permute-start(bf16[2,512,128]{2,1,0:T(8,128)(2,1)S(1)} %get-tuple-element.24), channel_id=1, source_target_pairs={{0,6},{1,7},{2,4},{3,5},{4,2},{5,3},{6,0},{7,1},{8,14},{9,15},{10,... | collective-permute-start | bytes 786440 | tf_op jit(solution)/shard_map/rows/ppermute | solution.py:344
  24.4 15.4 %pixel_weights.1 = (bf16[2048,4096]{1,0:T(8,128)(2,1)}, f32[1024,128]{1,0:T(8,128)S(1)}, bf16[1024,256]{1,0:T(8,128)(2,1)S(1)}, s32[1024,128]{1,0:T(8,128)S(1)}) custom-call(s32[1]{0:T(128)} %bitcast.2.me_ref, bf16[1024,1536]{1,0:T(8,128)(2,1)} %bitcast.23, bf16[192,1536]{1,0:T(8,128)(2,1)S(1)} %bitcast.18, s32[1024,64]{1,0:T(8,128)S(1)} %bitcast.20), custom_call_target="tpu_custom_call" | custom-call | flops 20000000000 | bytes 24000000 | tf_op jit(solution)/shard_map/pixel_weights/pallas_call | solution.py:137
  39.9 0.8 pad_maximum_fusion
  40.7 1.6 %collective-permute-start.3 = (bf16[2048,128]{1,0:T(8,128)(2,1)}, bf16[2048,128]{1,0:T(8,128)(2,1)S(1)}, u32[]{:S(2)}, u32[]{:S(2)}) collective-permute-start(bf16[2048,128]{1,0:T(8,128)(2,1)} %pad_maximum_fusion), channel_id=1, source_target_pairs={{0,1},{1,0},{2,3},{3,2},{4,5},{5,4},{6,7},{7,6},{8,9},{9,8},{10,11... | collective-permute-start | bytes 1572872 | tf_op jit(solution)/shard_map/rows_pair/ppermute | solution.py:344
  42.3 1.7 %collective-permute-done.3.far_ref = bf16[2048,128]{1,0:T(8,128)(2,1)S(1)} collective-permute-done((bf16[2048,128]{1,0:T(8,128)(2,1)}, bf16[2048,128]{1,0:T(8,128)(2,1)S(1)}, u32[]{:S(2)}, u32[]{:S(2)}) %collective-permute-start.3) | collective-permute-done | bytes 524320 | tf_op jit(solution)/shard_map/rows_pair/ppermute | solution.py:344
  44.1 0.9 copy-done.6
  45.0 16.2 %inner_halves.1 = (f32[32,24,384]{2,1,0:T(8,128)}, f32[32,24,384]{2,1,0:T(8,128)}) custom-call(s32[1]{0:T(128)} %bitcast.core_ref, bf16[1,512,128]{2,1,0:T(8,128)(2,1)S(1)} %copy-done.6, bf16[2,512,128]{2,1,0:T(8,128)(2,1)S(1)} %collective-permute-done.one_ref, bf16[2,512,128]{2,1,0:T(8,128)(2,1)S(1)} %collective-permute-done.1.two_ref, ...), custom_call_target="tpu_custom_call" | custom-call | tf_op jit(solution)/shard_map/inner_halves/pallas_call | solution.py:278
  61.2 0.5 collective-permute-start.4
  61.6 2.7 %collective-permute-done.4 = f32[32,24,384]{2,1,0:T(8,128)S(1)} collective-permute-done((f32[32,24,384]{2,1,0:T(8,128)}, f32[32,24,384]{2,1,0:T(8,128)S(1)}, u32[]{:S(2)}, u32[]{:S(2)}) %collective-permute-start.4) | collective-permute-done | bytes 1179680 | tf_op jit(solution)/shard_map/sum_pair/ppermute | solution.py:344
  64.3 1.4 %add_convert_fusion = bf16[32,24,384]{2,1,0:T(8,128)(2,1)S(1)} fusion(f32[32,24,384]{2,1,0:T(8,128)} %get-tuple-element.35, f32[32,24,384]{2,1,0:T(8,128)S(1)} %collective-permute-done.4), kind=kLoop, calls=%fused_computation.1 | loop fusion | flops 589824 | bytes 2949120 | tf_op jit(solution)/shard_map/sum_pair/convert_element_type | solution.py:371
  65.7 0.0 copy-start.2
  65.7 0.0 copy-start.3
  65.8 0.0 copy-start.4
  65.8 26.0 %all_to_all.14 = bf16[32,24,384]{2,1,0:T(8,128)(2,1)S(1)} all-to-all(bf16[32,24,384]{2,1,0:T(8,128)(2,1)S(1)} %add_convert_fusion), channel_id=1, replica_groups=mesh['dp'=32,'cam'=8] {'dp'}, dimensions={0} | all-to-all | bytes 1179648 | tf_op jit(solution)/shard_map/sum_dp/all_to_all | solution.py:373
  91.7 0.1 convert_reduce_fusion
  91.8 1.0 collective-permute-start.7
  92.8 2.4 %collective-permute-start.5 = (f32[24,384]{1,0:T(8,128)S(1)}, f32[24,384]{1,0:T(8,128)S(1)}, u32[]{:S(2)}, u32[]{:S(2)}) collective-permute-start(f32[24,384]{1,0:T(8,128)S(1)} %convert_reduce_fusion), channel_id=1, source_target_pairs={{0,2},{1,3},{2,0},{3,1},{4,6},{5,7},{6,4},{7,5},{8,10},{9,11},{10,... | collective-permute-start | bytes 110600 | tf_op jit(solution)/shard_map/sum_x/ppermute | solution.py:344
  95.2 0.8 collective-permute-done.7
  95.9 1.2 %collective-permute-done.6 = f32[24,384]{1,0:T(8,128)S(1)} collective-permute-done((f32[24,384]{1,0:T(8,128)S(1)}, f32[24,384]{1,0:T(8,128)S(1)}, u32[]{:S(2)}, u32[]{:S(2)}) %collective-permute-start.6) | collective-permute-done | bytes 36896 | tf_op jit(solution)/shard_map/sum_x/ppermute | solution.py:344
  97.1 4.9 %collective-permute-start.8 = (f32[24,384]{1,0:T(8,128)S(1)}, f32[24,384]{1,0:T(8,128)S(1)}, u32[]{:S(2)}, u32[]{:S(2)}) collective-permute-start(f32[24,384]{1,0:T(8,128)S(1)} %add_add_fusion.mine_ref), channel_id=1, source_target_pairs={{0,1},{1,0},{2,3},{3,2},{4,5},{5,4},{6,7},{7,6},{8,9},{9,8},{10,11... | collective-permute-start | bytes 110600 | tf_op jit(solution)/shard_map/share_pair/ppermute | solution.py:344
  102.1 0.9 collective-permute-done.8.other_ref
  102.9 1.4 %adam_update.1 = (f32[48,1728]{1,0:T(8,128)}, f32[48,1728]{1,0:T(8,128)}, f32[48,1728]{1,0:T(8,128)}) custom-call(s32[1]{0:T(128)} %bitcast.core_ref, f32[24,384]{1,0:T(8,128)S(1)} %add_add_fusion.mine_ref, f32[24,384]{1,0:T(8,128)S(1)} %collective-permute-done.8.other_ref, bf16[192,1536]{1,0:T(8,128)(2,1)S(1)} %bitcast.19, f32[48,1728]{1,0:T(8,128)S(1)} %copy-done.2, ...), custom_call_target="tpu_custom_call" | custom-call | tf_op jit(solution)/shard_map/adam_update/pallas_call | solution.py:333
  (15 shorter events, 0.1 us)
Async XLA Ops:
  0.6 23.8 %copy-start.1 = (bf16[1536,192]{0,1:T(8,128)(2,1)S(1)}, bf16[1536,192]{0,1:T(8,128)(2,1)}, u32[]{:S(2)}) copy-start(bf16[1536,192]{0,1:T(8,128)(2,1)} %param.11) | copy-start | bytes 1769476
  2.0 11.2 %all-to-all-start = ((s32[8,1,512]{2,1,0:T(1,128)}), s32[8,1,512]{2,1,0:T(1,128)S(1)}, u32[]{:S(2)}, u32[]{:S(2)}) async-start(s32[8,1,512]{2,1,0:T(1,128)} %all_to_all.9), calls=%async_computation | async-start | bytes 32768 | tf_op jit(solution)/shard_map/lists/all_to_all | solution.py:357
  13.2 1.2 %copy-start = (bf16[1,4096,128]{2,1,0:T(8,128)(2,1)S(1)}, bf16[1,4096,128]{2,1,0:T(8,128)(2,1)}, u32[]{:S(2)}) copy-start(bf16[1,4096,128]{2,1,0:T(8,128)(2,1)} %param.12) | copy-start | bytes 3145732
  19.9 0.7 copy-start.5
  20.6 19.3 %collective-permute-start = (bf16[2,512,128]{2,1,0:T(8,128)(2,1)S(1)}, bf16[2,512,128]{2,1,0:T(8,128)(2,1)S(1)}, u32[]{:S(2)}, u32[]{:S(2)}) collective-permute-start(bf16[2,512,128]{2,1,0:T(8,128)(2,1)S(1)} %get-tuple-element.22), channel_id=1, source_target_pairs={{0,2},{1,3},{2,0},{3,1},{4,6},{5,7},{6,4},{7,5},{8,10},{9,11},{10,... | collective-permute-start | bytes 786440 | tf_op jit(solution)/shard_map/rows/ppermute | solution.py:344
  20.9 19.0 %collective-permute-start.1 = (bf16[2,512,128]{2,1,0:T(8,128)(2,1)S(1)}, bf16[2,512,128]{2,1,0:T(8,128)(2,1)S(1)}, u32[]{:S(2)}, u32[]{:S(2)}) collective-permute-start(bf16[2,512,128]{2,1,0:T(8,128)(2,1)S(1)} %get-tuple-element.23), channel_id=1, source_target_pairs={{0,4},{1,5},{2,6},{3,7},{4,0},{5,1},{6,2},{7,3},{8,12},{9,13},{10,... | collective-permute-start | bytes 786440 | tf_op jit(solution)/shard_map/rows/ppermute | solution.py:344
  22.6 17.2 %collective-permute-start.2 = (bf16[2,512,128]{2,1,0:T(8,128)(2,1)S(1)}, bf16[2,512,128]{2,1,0:T(8,128)(2,1)S(1)}, u32[]{:S(2)}, u32[]{:S(2)}) collective-permute-start(bf16[2,512,128]{2,1,0:T(8,128)(2,1)S(1)} %get-tuple-element.24), channel_id=1, source_target_pairs={{0,6},{1,7},{2,4},{3,5},{4,2},{5,3},{6,0},{7,1},{8,14},{9,15},{10,... | collective-permute-start | bytes 786440 | tf_op jit(solution)/shard_map/rows/ppermute | solution.py:344
  40.7 3.3 %collective-permute-start.3 = (bf16[2048,128]{1,0:T(8,128)(2,1)}, bf16[2048,128]{1,0:T(8,128)(2,1)S(1)}, u32[]{:S(2)}, u32[]{:S(2)}) collective-permute-start(bf16[2048,128]{1,0:T(8,128)(2,1)} %pad_maximum_fusion), channel_id=1, source_target_pairs={{0,1},{1,0},{2,3},{3,2},{4,5},{5,4},{6,7},{7,6},{8,9},{9,8},{10,11... | collective-permute-start | bytes 1572872 | tf_op jit(solution)/shard_map/rows_pair/ppermute | solution.py:344
  44.1 0.9 copy-start.6
  61.2 3.2 %collective-permute-start.4 = (f32[32,24,384]{2,1,0:T(8,128)}, f32[32,24,384]{2,1,0:T(8,128)S(1)}, u32[]{:S(2)}, u32[]{:S(2)}) collective-permute-start(f32[32,24,384]{2,1,0:T(8,128)} %get-tuple-element.36), channel_id=1, source_target_pairs={{0,1},{1,0},{2,3},{3,2},{4,5},{5,4},{6,7},{7,6},{8,9},{9,8},{10,11... | collective-permute-start | bytes 3538952 | tf_op jit(solution)/shard_map/sum_pair/ppermute | solution.py:344
  65.7 37.2 %copy-start.2 = (f32[48,1728]{1,0:T(8,128)S(1)}, f32[48,1728]{1,0:T(8,128)}, u32[]{:S(2)}) copy-start(f32[48,1728]{1,0:T(8,128)} %master_ref.1) | copy-start | bytes 995332
  65.7 37.2 %copy-start.3 = (f32[48,1728]{1,0:T(8,128)S(1)}, f32[48,1728]{1,0:T(8,128)}, u32[]{:S(2)}) copy-start(f32[48,1728]{1,0:T(8,128)} %first_ref.1) | copy-start | bytes 995332
  65.8 37.2 %copy-start.4 = (f32[48,1728]{1,0:T(8,128)S(1)}, f32[48,1728]{1,0:T(8,128)}, u32[]{:S(2)}) copy-start(f32[48,1728]{1,0:T(8,128)} %second_ref.1) | copy-start | bytes 995332
  91.8 4.1 %collective-permute-start.7 = (f32[24,384]{1,0:T(8,128)S(1)}, f32[24,384]{1,0:T(8,128)S(1)}, u32[]{:S(2)}, u32[]{:S(2)}) collective-permute-start(f32[24,384]{1,0:T(8,128)S(1)} %convert_reduce_fusion), channel_id=1, source_target_pairs={{0,6},{1,7},{2,4},{3,5},{4,2},{5,3},{6,0},{7,1},{8,14},{9,15},{10,... | collective-permute-start | bytes 110600 | tf_op jit(solution)/shard_map/sum_x/ppermute | solution.py:344
  92.8 4.3 %collective-permute-start.6 = (f32[24,384]{1,0:T(8,128)S(1)}, f32[24,384]{1,0:T(8,128)S(1)}, u32[]{:S(2)}, u32[]{:S(2)}) collective-permute-start(f32[24,384]{1,0:T(8,128)S(1)} %convert_reduce_fusion), channel_id=1, source_target_pairs={{0,4},{1,5},{2,6},{3,7},{4,0},{5,1},{6,2},{7,3},{8,12},{9,13},{10,... | collective-permute-start | bytes 110600 | tf_op jit(solution)/shard_map/sum_x/ppermute | solution.py:344
  92.8 4.3 %collective-permute-start.5 = (f32[24,384]{1,0:T(8,128)S(1)}, f32[24,384]{1,0:T(8,128)S(1)}, u32[]{:S(2)}, u32[]{:S(2)}) collective-permute-start(f32[24,384]{1,0:T(8,128)S(1)} %convert_reduce_fusion), channel_id=1, source_target_pairs={{0,2},{1,3},{2,0},{3,1},{4,6},{5,7},{6,4},{7,5},{8,10},{9,11},{10,... | collective-permute-start | bytes 110600 | tf_op jit(solution)/shard_map/sum_x/ppermute | solution.py:344
  97.1 5.8 %collective-permute-start.8 = (f32[24,384]{1,0:T(8,128)S(1)}, f32[24,384]{1,0:T(8,128)S(1)}, u32[]{:S(2)}, u32[]{:S(2)}) collective-permute-start(f32[24,384]{1,0:T(8,128)S(1)} %add_add_fusion.mine_ref), channel_id=1, source_target_pairs={{0,1},{1,0},{2,3},{3,2},{4,5},{5,4},{6,7},{7,6},{8,9},{9,8},{10,11... | collective-permute-start | bytes 110600 | tf_op jit(solution)/shard_map/share_pair/ppermute | solution.py:344

commit v3 on v2

--- a/solution.py
+++ b/solution.py
@@ -25,6 +25,7 @@
 CHIPS = 4
 CAP = 512
 CH = 128
+SUMS = 128
 MIB = 1 << 20
 
 
@@ -76,16 +77,48 @@
     )(me, lists, tile)
 
 
-def weights_kernel(me_ref, feat_ref, w_ref, slot_ref, wts_ref, occ_ref, ctx_ref, place_ref):
-    block = feat_ref.shape[0]
+def head_kernel(me_ref, feat_ref, w_ref, slot_ref, occ_ref, ctx_ref, place_ref):
     head = lax.dot_general(feat_ref[...], w_ref[...], NT, preferred_element_type=f32)
     ctx_ref[:, :CH], ctx_ref[:, CH:] = split(head[:, :CH])
     occ = 1.0 / (1.0 + jnp.exp(-head[:, CH:]))
     occ_ref[...] = jnp.concatenate([occ, occ], axis=1)
-    slots = slot_ref[...]
+    slots = slot_ref[...].T
     tile = (slots >> 9) ^ me_ref[0]
     slots = jnp.where(slots < 8 * CAP, ((tile & 1) << 11) | ((tile >> 1) << 9) | (slots & (CAP - 1)), 8 * CAP)
     place_ref[...] = jnp.concatenate([slots, slots], axis=1)
+
+
+def head_values(me, feat, w_head, slots, block=256):
+    pixels, width = feat.shape
+
+    def rows(height, lanes):
+        return pl.BlockSpec((height, lanes), lambda i: (i, 0))
+
+    return pl.pallas_call(
+        head_kernel,
+        grid=(pixels // block,),
+        out_shape=(
+            jax.ShapeDtypeStruct((pixels, 128), f32),
+            jax.ShapeDtypeStruct((pixels, 2 * CH), bf16),
+            jax.ShapeDtypeStruct((pixels, 128), i32),
+        ),
+        in_specs=[
+            smem(),
+            rows(block, width),
+            pl.BlockSpec(w_head.shape, lambda i: (0, 0)),
+            pl.BlockSpec((slots.shape[0], block), lambda i: (0, i)),
+        ],
+        out_specs=(rows(block, 128), rows(block, 2 * CH), rows(block, 128)),
+        compiler_params=pltpu.CompilerParams(vmem_limit_bytes=60 * MIB),
+        cost_estimate=pl.CostEstimate(flops=4 * 10**9, bytes_accessed=8 * 10**6, transcendentals=0),
+        name="head_values",
+    )(me, feat, w_head, slots)
+
+
+def weights_kernel(*refs):
+    occ_ref, place_ref, wts_ref, token_ref = refs[-4:]
+    block = occ_ref.shape[0]
+    token_ref[...] = jnp.zeros_like(token_ref)
     lane = lax.broadcasted_iota(i32, (1, 128), 1)
     lane16 = lax.broadcasted_iota(i32, (16, 128), 1)
     sub16 = lax.broadcasted_iota(i32, (16, 128), 0)
@@ -130,40 +163,30 @@
     lax.fori_loop(0, block // 16, build, 0, unroll=8)
 
 
-def pixel_weights(me, feat, w_head, slots, block=256):
-    pixels, width = feat.shape
-    depth = slots.shape[1]
+def pixel_weights(after, occ, places, first, count, wts=None, block=SUMS):
+    pixels = occ.shape[0]
     table = 8 * CAP
+    operands = tuple(after) if wts is None else (wts, *after)
     return pl.pallas_call(
         weights_kernel,
-        grid=(pixels // block,),
-        out_shape=(
-            jax.ShapeDtypeStruct((2 * pixels, table), bf16),
-            jax.ShapeDtypeStruct((pixels, 128), f32),
-            jax.ShapeDtypeStruct((pixels, 2 * CH), bf16),
-            jax.ShapeDtypeStruct((pixels, 128), i32),
+        grid=(count,),
+        out_shape=(jax.ShapeDtypeStruct((2 * pixels, table), bf16), jax.ShapeDtypeStruct((8, 128), f32)),
+        in_specs=[pl.BlockSpec(memory_space=pl.ANY)] * len(operands)
+        + [pl.BlockSpec((block, 128), lambda i: (i + first, 0))] * 2,
+        out_specs=(
+            pl.BlockSpec((2 * block, table), lambda i: (i + first, 0)),
+            pl.BlockSpec((8, 128), lambda i: (0, 0)),
         ),
-        in_specs=[
-            smem(),
-            pl.BlockSpec((block, width), lambda i: (i, 0)),
-            pl.BlockSpec(w_head.shape, lambda i: (0, 0)),
-            pl.BlockSpec((block, depth), lambda i: (i, 0)),
-        ],
-        out_specs=(
-            pl.BlockSpec((2 * block, table), lambda i: (i, 0)),
-            pl.BlockSpec((block, 128), lambda i: (i, 0)),
-            pl.BlockSpec((block, 2 * CH), lambda i: (i, 0)),
-            pl.BlockSpec((block, 128), lambda i: (i, 0)),
-        ),
+        input_output_aliases={} if wts is None else {0: 0},
         compiler_params=pltpu.CompilerParams(vmem_limit_bytes=50 * MIB),
-        cost_estimate=pl.CostEstimate(flops=20 * 10**9, bytes_accessed=24 * 10**6, transcendentals=0),
+        cost_estimate=pl.CostEstimate(flops=25 * 10**8 * count, bytes_accessed=3 * 10**6 * count, transcendentals=0),
         name="pixel_weights",
-    )(me, feat, w_head, slots)
+    )(*operands, occ, places)
 
 
 def grads_kernel(
     core_ref, own_ref, one_ref, two_ref, three_ref, far_ref, wts_ref, occ_ref, place_ref, ctx_ref, x_hbm, feat_hbm,
-    keep_ref, send_ref, table, flip, scores, mixed, picked, head, x_in, feat, sems,
+    keep_ref, send_ref, table, flip, scores, mixed, picked, head, x_in, feat, sems, *, owners,
 ):
     step = pl.program_id(0)
     last = pl.num_programs(0) - 1
@@ -202,7 +225,8 @@
     def finish():
         rows = pl.ds(pl.multiple_of((step - 1) * block, block), block)
         occ = occ_ref[...]
-        head[rows, :CH] = (mixed[:block] + mixed[block:]).astype(bf16)
+        both = mixed[...].reshape(block // SUMS, 2, SUMS, CH)
+        head[rows, :CH] = (both[:, 0] + both[:, 1]).reshape(block, CH).astype(bf16)
         head[rows, CH:] = (occ * (1.0 - occ) * picked[...]).astype(bf16)
 
     @pl.when(step == 0)
@@ -247,7 +271,8 @@
         finish()
         x_copy.wait()
         feat_copy.wait()
-        owners, half_rows, width = keep_ref.shape
+        rows, width = keep_ref.shape
+        half_rows = rows // owners
         span = 384
         per_span = span // (2 * half_rows)
         grads = head[...]
@@ -260,9 +285,10 @@
             tail = jnp.where(lane < 64, left[:, CH:], right[:, CH:])
             full = jnp.concatenate([left[:, :CH], right[:, :CH], tail], axis=1)
             full = full.reshape(per_span, 2, half_rows, width)
-            part = slice(n * per_span, (n + 1) * per_span)
-            keep_ref[part] = jnp.where(first, full[:, 0], full[:, 1])
-            send_ref[part] = jnp.where(first, full[:, 1], full[:, 0])
+            height = per_span * half_rows
+            part = slice(n * height, (n + 1) * height)
+            keep_ref[part] = jnp.where(first, full[:, 0], full[:, 1]).reshape(height, width)
+            send_ref[part] = jnp.where(first, full[:, 1], full[:, 0]).reshape(height, width).astype(bf16)
 
 
 def inner_halves(core, tables, wts, occ, places, ctx, x_in, feat, owners, block=256):
@@ -270,15 +296,15 @@
     count = 8 * CAP
     blocks = pixels // block
     first = pl.BlockSpec((1, CAP, CH), lambda i: (0, 0, 0))
-    halves = jax.ShapeDtypeStruct((owners, width // owners // 2, 384), f32)
+    half = (width // 2, 384)
 
     def behind(i):
         return (jnp.maximum(i - 1, 0), 0)
 
     return pl.pallas_call(
-        grads_kernel,
+        functools.partial(grads_kernel, owners=owners),
         grid=(blocks + 1,),
-        out_shape=(halves, halves),
+        out_shape=(jax.ShapeDtypeStruct(half, f32), jax.ShapeDtypeStruct(half, bf16)),
         in_specs=[
             smem(),
             first, first, first, first,
@@ -355,20 +381,21 @@
 
     with jax.named_scope("lists"):
         lists = lax.all_to_all(cell_lists[0, 0], "cam", 0, 0, tiled=True)
+    occ, ctx, places = head_values(me.reshape(1), features, w_head, point_slots[0].T)
     own, pair, one, two, three = gather_rows(me.reshape(1), lists.reshape(-1), g_bev[0])
     with jax.named_scope("rows"):
         one, two, three = hop(one, 2), hop(two, 4), hop(three, 6)
-
-    w_head_late, own = lax.optimization_barrier((w_head, own))
-    wts, occ, ctx, places = pixel_weights(me.reshape(1), features, w_head_late, point_slots[0])
+    wts, token = pixel_weights((own,), occ, places, 0, pixels // SUMS - 1)
     with jax.named_scope("rows_pair"):
-        one, two, three, ctx = lax.optimization_barrier((one, two, three, ctx))
+        one, two, three, token = lax.optimization_barrier((one, two, three, token))
         far = hop(jnp.concatenate([pair[0], one[1], two[1], three[1]], axis=0), 1)
+    wts, _ = pixel_weights((token,), occ, places, pixels // SUMS - 1, 1, wts)
     keep, send = inner_halves(
         core, (own, one, two, three, far), wts, occ, places, ctx, x_in[0], features, data_count
     )
     with jax.named_scope("sum_pair"):
-        half = (keep + hop(send, 1)).astype(bf16)
+        half = (keep + hop(send, 1).astype(f32)).astype(bf16)
+        half = half.reshape(data_count, -1, half.shape[1])
     with jax.named_scope("sum_dp"):
         half = lax.all_to_all(half, "dp", 0, 0, tiled=True)
         half = jnp.sum(half.astype(f32), axis=0)

time: 105 us -> 101 us (0.962)
  waiting for transfers between devices: 10.8 us -> 6.24 us
  Pallas kernels: 38.5 us -> 41.2 us
  local copies, waits for them, and re-layouts: 5.37 us -> 3.49 us
    all_to_all x1, waiting for transfers between devices: 3.52 us -> 0.01 us  [shards(): lists = lax.all_to_all(cell_lists[0, 0], 'cam', 0, 0, tiled=True)]
    pallas_call x2 -> x4, Pallas kernels: 31.6 us -> 34.3 us  [the longest x1 15.9 us: inner_halves(): pl.pallas_call(functools.partial(grads_kernel, owners=owners), grid=(bloc...]
    unnamed x15 -> x20, local copies, waits for them, and re-layouts: 3.94 us -> 2.12 us
  transfers between devices with their start and end apart: 10 -> 10, of which waited for: 6 -> 5; matrix products, arithmetic and copies ran while one was open for 1% -> 0% of each run, Pallas kernels for 15% -> 18%
where the time goes in v3:
time: 101 us; the launch traced here: 100 us
  Pallas kernels  41.2 us (41%)
  blocking collectives  26.2 us (26%)
  starting transfers between devices  20.8 us (21%)
  waiting for transfers between devices  6.24 us (6%)
  local copies, waits for them, and re-layouts  3.49 us (3%)
  other arithmetic  1.52 us (2%)
    all_to_all x1, blocking collectives, shards(): half = lax.all_to_all(half, 'dp', 0, 0, tiled=True)  26.2 us
    pallas_call x1, Pallas kernels, inner_halves(): pl.pallas_call(functools.partial(grads_kernel, owners=owners), grid=(bloc...  15.9 us
    ppermute x9, starting transfers between devices, hop(): lax.ppermute(value, 'cam', [(i, i ^ distance) for i in range(2 * CHIPS)])  14.3 us
    pallas_call x2, Pallas kernels, pixel_weights(): pl.pallas_call(weights_kernel, grid=(count,), out_shape=(jax.ShapeDtypeSt...  13.3 us
    all_to_all x1, starting transfers between devices, shards(): lists = lax.all_to_all(cell_lists[0, 0], 'cam', 0, 0, tiled=True)  6.48 us
    ppermute x9, waiting for transfers between devices, hop(): lax.ppermute(value, 'cam', [(i, i ^ distance) for i in range(2 * CHIPS)])  6.23 us
    pallas_call x1, Pallas kernels, gather_rows(): pl.pallas_call(gather_kernel, out_shape=(one, one, two, two, two), in_spe...  5.48 us
    pallas_call x1, Pallas kernels, head_values(): pl.pallas_call(head_kernel, grid=(pixels // block,), out_shape=(jax.Shape...  5.2 us
  transfers between devices with their start and end apart: 10, of which 5 were waited for; matrix products, arithmetic and copies ran while one was open for 0% of the time, Pallas kernels for 18%

profile of v3, /device:TPU:1, one launch (start us, length us, event | category | flops | bytes accessed | tf_op | source)
XLA Modules:
  0.0 100.2 jit_solution(5610696625689972849)
XLA Ops:
  0.6 1.3 %all_to_all.9 = s32[8,1,512]{2,1,0:T(1,128)} reshape(s32[1,1,8,512]{3,2,1,0:T(8,128)} %param.13) | data formatting | bytes 32768 | tf_op jit(solution)/shard_map/lists/all_to_all | solution.py:383
  2.0 6.5 %all-to-all-start = ((s32[8,1,512]{2,1,0:T(1,128)}), s32[8,1,512]{2,1,0:T(1,128)S(1)}, u32[]{:S(2)}, u32[]{:S(2)}) async-start(s32[8,1,512]{2,1,0:T(1,128)} %all_to_all.9), calls=%async_computation | async-start | bytes 32768 | tf_op jit(solution)/shard_map/lists/all_to_all | solution.py:383
  8.4 5.2 %head_values.1 = (f32[1024,128]{1,0:T(8,128)}, bf16[1024,256]{1,0:T(8,128)(2,1)}, s32[1024,128]{1,0:T(8,128)}) custom-call(s32[1]{0:T(128)} %bitcast.1.me_ref, bf16[1024,1536]{1,0:T(8,128)(2,1)} %bitcast.25, bf16[192,1536]{1,0:T(8,128)(2,1)} %bitcast.21, s32[64,1024]{1,0:T(8,128)} %bitcast.29), custom_call_target="tpu_custom_call" | custom-call | flops 4000000000 | bytes 8000000 | tf_op jit(solution)/shard_map/head_values/pallas_call | solution.py:97
  13.7 0.0 all-to-all-done
  13.7 5.5 %gather_rows.1 = (bf16[1,512,128]{2,1,0:T(8,128)(2,1)S(1)}, bf16[1,512,128]{2,1,0:T(8,128)(2,1)S(1)}, bf16[2,512,128]{2,1,0:T(8,128)(2,1)S(1)}, bf16[2,512,128]{2,1,0:T(8,128)(2,1)S(1)}, bf16[2,512,128]{2,1,0:T(8,128)(2,1)S(1)}) custom-call(s32[1]{0:T(128)} %bitcast.1.me_ref, s32[4096]{0:T(1024)S(1)} %bitcast.24, bf16[4096,128]{1,0:T(8,128)(2,1)S(1)} %bitcast.20), custom_call_target="tpu_custom_call" | custom-call | tf_op jit(solution)/shard_map/gather_rows/pallas_call | solution.py:69
  19.1 1.5 %collective-permute-start = (bf16[2,512,128]{2,1,0:T(8,128)(2,1)S(1)}, bf16[2,512,128]{2,1,0:T(8,128)(2,1)S(1)}, u32[]{:S(2)}, u32[]{:S(2)}) collective-permute-start(bf16[2,512,128]{2,1,0:T(8,128)(2,1)S(1)} %get-tuple-element.21), channel_id=1, source_target_pairs={{0,2},{1,3},{2,0},{3,1},{4,6},{5,7},{6,4},{7,5},{8,10},{9,11},{10,... | collective-permute-start | bytes 786440 | tf_op jit(solution)/shard_map/rows/ppermute | solution.py:370
  20.6 2.4 %collective-permute-start.1 = (bf16[2,512,128]{2,1,0:T(8,128)(2,1)S(1)}, bf16[2,512,128]{2,1,0:T(8,128)(2,1)S(1)}, u32[]{:S(2)}, u32[]{:S(2)}) collective-permute-start(bf16[2,512,128]{2,1,0:T(8,128)(2,1)S(1)} %get-tuple-element.22), channel_id=1, source_target_pairs={{0,4},{1,5},{2,6},{3,7},{4,0},{5,1},{6,2},{7,3},{8,12},{9,13},{10,... | collective-permute-start | bytes 786440 | tf_op jit(solution)/shard_map/rows/ppermute | solution.py:370
  23.1 0.1 collective-permute-start.2
  23.1 1.0 %copy-done = f32[1024,128]{1,0:T(8,128)S(1)} copy-done((f32[1024,128]{1,0:T(8,128)S(1)}, f32[1024,128]{1,0:T(8,128)}, u32[]{:S(2)}) %copy-start) | copy-done | bytes 524312
  24.2 1.0 %copy-done.2 = s32[1024,128]{1,0:T(8,128)S(1)} copy-done((s32[1024,128]{1,0:T(8,128)S(1)}, s32[1024,128]{1,0:T(8,128)}, u32[]{:S(2)}) %copy-start.2) | copy-done | bytes 524312
  25.2 10.6 %pixel_weights.2 = (bf16[2048,4096]{1,0:T(8,128)(2,1)}, f32[8,128]{1,0:T(8,128)S(1)}) custom-call(bf16[1,512,128]{2,1,0:T(8,128)(2,1)S(1)} %get-tuple-element.20.refs_0_.own_ref, f32[1024,128]{1,0:T(8,128)S(1)} %copy-done, s32[1024,128]{1,0:T(8,128)S(1)} %copy-done.2), custom_call_target="tpu_custom_call" | custom-call | flops 17500000256 | bytes 21000000 | tf_op jit(solution)/shard_map/pixel_weights/pallas_call | solution.py:170
  35.9 0.0 collective-permute-done.1.two_ref
  35.9 0.9 collective-permute-done.2.three_ref
  36.8 1.9 %collective-permute-start.3 = (bf16[2048,128]{1,0:T(8,128)(2,1)S(1)}, bf16[2048,128]{1,0:T(8,128)(2,1)S(1)}, u32[]{:S(2)}, u32[]{:S(2)}) collective-permute-start(bf16[2048,128]{1,0:T(8,128)(2,1)S(1)} %pad_maximum_fusion), channel_id=1, source_target_pairs={{0,1},{1,0},{2,3},{3,2},{4,5},{5,4},{6,7},{7,6},{8,9},{9,8},{10,11... | collective-permute-start | bytes 1572872 | tf_op jit(solution)/shard_map/rows_pair/ppermute | solution.py:370
  38.8 2.6 %pixel_weights.3 = (bf16[2048,4096]{1,0:T(8,128)(2,1)}, f32[8,128]{1,0:T(8,128)}) custom-call(bf16[2048,4096]{1,0:T(8,128)(2,1)} %get-tuple-element.31.refs_0_, f32[8,128]{1,0:T(8,128)S(1)} %get-tuple-element.32.refs_1_, f32[1024,128]{1,0:T(8,128)S(1)} %copy-done.1, s32[1024,128]{1,0:T(8,128)S(1)} %copy-done.3), custom_call_target="tpu_custom_call", output_to_operand_aliasing={{0}: (0, {})} | custom-call | flops 2500000000 | bytes 3000000 | tf_op jit(solution)/shard_map/pixel_weights/pallas_call | solution.py:170
  41.4 15.9 %inner_halves.1 = (f32[768,384]{1,0:T(8,128)}, bf16[768,384]{1,0:T(8,128)(2,1)S(1)}) custom-call(s32[1]{0:T(128)} %bitcast.core_ref, bf16[1,512,128]{2,1,0:T(8,128)(2,1)S(1)} %get-tuple-element.20.refs_0_.own_ref, bf16[2,512,128]{2,1,0:T(8,128)(2,1)S(1)} %collective-permute-done.one_ref, bf16[2,512,128]{2,1,0:T(8,128)(2,1)S(1)} %collective-permute-done.1.two_ref, ...), custom_call_target="tpu_custom_call" | custom-call | tf_op jit(solution)/shard_map/inner_halves/pallas_call | solution.py:304
  57.3 0.1 collective-permute-start.4
  57.4 2.0 %collective-permute-done.4 = bf16[768,384]{1,0:T(8,128)(2,1)S(1)} collective-permute-done((bf16[768,384]{1,0:T(8,128)(2,1)S(1)}, bf16[768,384]{1,0:T(8,128)(2,1)S(1)}, u32[]{:S(2)}, u32[]{:S(2)}) %collective-permute-start.4) | collective-permute-done | bytes 589856 | tf_op jit(solution)/shard_map/sum_pair/ppermute | solution.py:370
  59.4 1.4 %add_convert_fusion = bf16[768,384]{1,0:T(8,128)(2,1)S(1)} fusion(f32[768,384]{1,0:T(8,128)} %get-tuple-element.35, bf16[768,384]{1,0:T(8,128)(2,1)S(1)} %collective-permute-done.4), kind=kLoop, calls=%fused_computation.1 | loop fusion | flops 884736 | bytes 2359296 | tf_op jit(solution)/shard_map/sum_pair/convert_element_type | solution.py:397
  60.8 0.0 copy-start.5
  60.8 0.0 copy-start.7
  60.8 0.0 copy-start.8
  60.8 0.0 copy-start.9
  60.8 26.2 %all_to_all.14 = bf16[32,24,384]{2,1,0:T(8,128)(2,1)S(1)} all-to-all(bf16[32,24,384]{2,1,0:T(8,128)(2,1)S(1)} %bitcast.28), channel_id=1, replica_groups=mesh['dp'=32,'cam'=8] {'dp'}, dimensions={0} | all-to-all | bytes 1179648 | tf_op jit(solution)/shard_map/sum_dp/all_to_all | solution.py:400
  87.1 0.1 convert_reduce_fusion
  87.1 1.5 %collective-permute-start.7 = (f32[24,384]{1,0:T(8,128)S(1)}, f32[24,384]{1,0:T(8,128)S(1)}, u32[]{:S(2)}, u32[]{:S(2)}) collective-permute-start(f32[24,384]{1,0:T(8,128)S(1)} %convert_reduce_fusion), channel_id=1, source_target_pairs={{0,6},{1,7},{2,4},{3,5},{4,2},{5,3},{6,0},{7,1},{8,14},{9,15},{10,... | collective-permute-start | bytes 110600 | tf_op jit(solution)/shard_map/sum_x/ppermute | solution.py:370
  88.7 1.8 %collective-permute-start.5 = (f32[24,384]{1,0:T(8,128)S(1)}, f32[24,384]{1,0:T(8,128)S(1)}, u32[]{:S(2)}, u32[]{:S(2)}) collective-permute-start(f32[24,384]{1,0:T(8,128)S(1)} %convert_reduce_fusion), channel_id=1, source_target_pairs={{0,2},{1,3},{2,0},{3,1},{4,6},{5,7},{6,4},{7,5},{8,10},{9,11},{10,... | collective-permute-start | bytes 110600 | tf_op jit(solution)/shard_map/sum_x/ppermute | solution.py:370
  90.5 0.8 collective-permute-done.7
  91.3 1.7 %collective-permute-done.6 = f32[24,384]{1,0:T(8,128)S(1)} collective-permute-done((f32[24,384]{1,0:T(8,128)S(1)}, f32[24,384]{1,0:T(8,128)S(1)}, u32[]{:S(2)}, u32[]{:S(2)}) %collective-permute-start.6) | collective-permute-done | bytes 36896 | tf_op jit(solution)/shard_map/sum_x/ppermute | solution.py:370
  93.0 4.9 %collective-permute-start.8 = (f32[24,384]{1,0:T(8,128)S(1)}, f32[24,384]{1,0:T(8,128)S(1)}, u32[]{:S(2)}, u32[]{:S(2)}) collective-permute-start(f32[24,384]{1,0:T(8,128)S(1)} %add_add_fusion.mine_ref), channel_id=1, source_target_pairs={{0,1},{1,0},{2,3},{3,2},{4,5},{5,4},{6,7},{7,6},{8,9},{9,8},{10,11... | collective-permute-start | bytes 110600 | tf_op jit(solution)/shard_map/share_pair/ppermute | solution.py:370
  97.9 0.9 collective-permute-done.8.other_ref
  98.8 1.4 %adam_update.1 = (f32[48,1728]{1,0:T(8,128)}, f32[48,1728]{1,0:T(8,128)}, f32[48,1728]{1,0:T(8,128)}) custom-call(s32[1]{0:T(128)} %bitcast.core_ref, f32[24,384]{1,0:T(8,128)S(1)} %add_add_fusion.mine_ref, f32[24,384]{1,0:T(8,128)S(1)} %collective-permute-done.8.other_ref, bf16[192,1536]{1,0:T(8,128)(2,1)S(1)} %bitcast.22, f32[48,1728]{1,0:T(8,128)S(1)} %copy-done.7, ...), custom_call_target="tpu_custom_call" | custom-call | tf_op jit(solution)/shard_map/adam_update/pallas_call | solution.py:359
  (22 shorter events, 0.1 us)
Async XLA Ops:
  2.0 11.7 %all-to-all-start = ((s32[8,1,512]{2,1,0:T(1,128)}), s32[8,1,512]{2,1,0:T(1,128)S(1)}, u32[]{:S(2)}, u32[]{:S(2)}) async-start(s32[8,1,512]{2,1,0:T(1,128)} %all_to_all.9), calls=%async_computation | async-start | bytes 32768 | tf_op jit(solution)/shard_map/lists/all_to_all | solution.py:383
  8.4 5.2 %copy-start.4 = (bf16[1,4096,128]{2,1,0:T(8,128)(2,1)S(1)}, bf16[1,4096,128]{2,1,0:T(8,128)(2,1)}, u32[]{:S(2)}) copy-start(bf16[1,4096,128]{2,1,0:T(8,128)(2,1)} %param.12) | copy-start | bytes 3145732
  19.1 16.7 %collective-permute-start = (bf16[2,512,128]{2,1,0:T(8,128)(2,1)S(1)}, bf16[2,512,128]{2,1,0:T(8,128)(2,1)S(1)}, u32[]{:S(2)}, u32[]{:S(2)}) collective-permute-start(bf16[2,512,128]{2,1,0:T(8,128)(2,1)S(1)} %get-tuple-element.21), channel_id=1, source_target_pairs={{0,2},{1,3},{2,0},{3,1},{4,6},{5,7},{6,4},{7,5},{8,10},{9,11},{10,... | collective-permute-start | bytes 786440 | tf_op jit(solution)/shard_map/rows/ppermute | solution.py:370
  20.6 15.2 %collective-permute-start.1 = (bf16[2,512,128]{2,1,0:T(8,128)(2,1)S(1)}, bf16[2,512,128]{2,1,0:T(8,128)(2,1)S(1)}, u32[]{:S(2)}, u32[]{:S(2)}) collective-permute-start(bf16[2,512,128]{2,1,0:T(8,128)(2,1)S(1)} %get-tuple-element.22), channel_id=1, source_target_pairs={{0,4},{1,5},{2,6},{3,7},{4,0},{5,1},{6,2},{7,3},{8,12},{9,13},{10,... | collective-permute-start | bytes 786440 | tf_op jit(solution)/shard_map/rows/ppermute | solution.py:370
  23.1 13.7 %collective-permute-start.2 = (bf16[2,512,128]{2,1,0:T(8,128)(2,1)S(1)}, bf16[2,512,128]{2,1,0:T(8,128)(2,1)S(1)}, u32[]{:S(2)}, u32[]{:S(2)}) collective-permute-start(bf16[2,512,128]{2,1,0:T(8,128)(2,1)S(1)} %get-tuple-element.23), channel_id=1, source_target_pairs={{0,6},{1,7},{2,4},{3,5},{4,2},{5,3},{6,0},{7,1},{8,14},{9,15},{10,... | collective-permute-start | bytes 786440 | tf_op jit(solution)/shard_map/rows/ppermute | solution.py:370
  23.1 1.0 %copy-start = (f32[1024,128]{1,0:T(8,128)S(1)}, f32[1024,128]{1,0:T(8,128)}, u32[]{:S(2)}) copy-start(f32[1024,128]{1,0:T(8,128)} %get-tuple-element.24.refs_1_.refs_2_.occ_ref) | copy-start | bytes 1572868
  24.2 1.0 %copy-start.2 = (s32[1024,128]{1,0:T(8,128)S(1)}, s32[1024,128]{1,0:T(8,128)}, u32[]{:S(2)}) copy-start(s32[1024,128]{1,0:T(8,128)} %get-tuple-element.25.refs_2_.refs_3_.place_ref) | copy-start | bytes 1572868
  35.8 2.9 %copy-start.1 = (f32[1024,128]{1,0:T(8,128)S(1)}, f32[1024,128]{1,0:T(8,128)}, u32[]{:S(2)}) copy-start(f32[1024,128]{1,0:T(8,128)} %get-tuple-element.24.refs_1_.refs_2_.occ_ref) | copy-start | bytes 1572868
  35.9 2.9 %copy-start.3 = (s32[1024,128]{1,0:T(8,128)S(1)}, s32[1024,128]{1,0:T(8,128)}, u32[]{:S(2)}) copy-start(s32[1024,128]{1,0:T(8,128)} %get-tuple-element.25.refs_2_.refs_3_.place_ref) | copy-start | bytes 1572868
  36.8 4.6 %collective-permute-start.3 = (bf16[2048,128]{1,0:T(8,128)(2,1)S(1)}, bf16[2048,128]{1,0:T(8,128)(2,1)S(1)}, u32[]{:S(2)}, u32[]{:S(2)}) collective-permute-start(bf16[2048,128]{1,0:T(8,128)(2,1)S(1)} %pad_maximum_fusion), channel_id=1, source_target_pairs={{0,1},{1,0},{2,3},{3,2},{4,5},{5,4},{6,7},{7,6},{8,9},{9,8},{10,11... | collective-permute-start | bytes 1572872 | tf_op jit(solution)/shard_map/rows_pair/ppermute | solution.py:370
  38.8 2.6 %copy-start.6 = (bf16[1024,256]{1,0:T(8,128)(2,1)S(1)}, bf16[1024,256]{1,0:T(8,128)(2,1)}, u32[]{:S(2)}) copy-start(bf16[1024,256]{1,0:T(8,128)(2,1)} %get-tuple-element.34.ctx_ref) | copy-start | bytes 1572868
  57.3 2.1 %collective-permute-start.4 = (bf16[768,384]{1,0:T(8,128)(2,1)S(1)}, bf16[768,384]{1,0:T(8,128)(2,1)S(1)}, u32[]{:S(2)}, u32[]{:S(2)}) collective-permute-start(bf16[768,384]{1,0:T(8,128)(2,1)S(1)} %get-tuple-element.36), channel_id=1, source_target_pairs={{0,1},{1,0},{2,3},{3,2},{4,5},{5,4},{6,7},{7,6},{8,9},{9,8},{10,11... | collective-permute-start | bytes 1769480 | tf_op jit(solution)/shard_map/sum_pair/ppermute | solution.py:370
  60.8 38.0 %copy-start.5 = (bf16[1536,192]{0,1:T(8,128)(2,1)S(1)}, bf16[1536,192]{0,1:T(8,128)(2,1)}, u32[]{:S(2)}) copy-start(bf16[1536,192]{0,1:T(8,128)(2,1)} %param.11) | copy-start | bytes 1769476
  60.8 38.0 %copy-start.7 = (f32[48,1728]{1,0:T(8,128)S(1)}, f32[48,1728]{1,0:T(8,128)}, u32[]{:S(2)}) copy-start(f32[48,1728]{1,0:T(8,128)} %master_ref.1) | copy-start | bytes 995332
  60.8 38.0 %copy-start.8 = (f32[48,1728]{1,0:T(8,128)S(1)}, f32[48,1728]{1,0:T(8,128)}, u32[]{:S(2)}) copy-start(f32[48,1728]{1,0:T(8,128)} %first_ref.1) | copy-start | bytes 995332
  60.8 38.0 %copy-start.9 = (f32[48,1728]{1,0:T(8,128)S(1)}, f32[48,1728]{1,0:T(8,128)}, u32[]{:S(2)}) copy-start(f32[48,1728]{1,0:T(8,128)} %second_ref.1) | copy-start | bytes 995332
  87.1 4.1 %collective-permute-start.7 = (f32[24,384]{1,0:T(8,128)S(1)}, f32[24,384]{1,0:T(8,128)S(1)}, u32[]{:S(2)}, u32[]{:S(2)}) collective-permute-start(f32[24,384]{1,0:T(8,128)S(1)} %convert_reduce_fusion), channel_id=1, source_target_pairs={{0,6},{1,7},{2,4},{3,5},{4,2},{5,3},{6,0},{7,1},{8,14},{9,15},{10,... | collective-permute-start | bytes 110600 | tf_op jit(solution)/shard_map/sum_x/ppermute | solution.py:370
  88.7 4.3 %collective-permute-start.6 = (f32[24,384]{1,0:T(8,128)S(1)}, f32[24,384]{1,0:T(8,128)S(1)}, u32[]{:S(2)}, u32[]{:S(2)}) collective-permute-start(f32[24,384]{1,0:T(8,128)S(1)} %convert_reduce_fusion), channel_id=1, source_target_pairs={{0,4},{1,5},{2,6},{3,7},{4,0},{5,1},{6,2},{7,3},{8,12},{9,13},{10,... | collective-permute-start | bytes 110600 | tf_op jit(solution)/shard_map/sum_x/ppermute | solution.py:370
  88.7 4.3 %collective-permute-start.5 = (f32[24,384]{1,0:T(8,128)S(1)}, f32[24,384]{1,0:T(8,128)S(1)}, u32[]{:S(2)}, u32[]{:S(2)}) collective-permute-start(f32[24,384]{1,0:T(8,128)S(1)} %convert_reduce_fusion), channel_id=1, source_target_pairs={{0,2},{1,3},{2,0},{3,1},{4,6},{5,7},{6,4},{7,5},{8,10},{9,11},{10,... | collective-permute-start | bytes 110600 | tf_op jit(solution)/shard_map/sum_x/ppermute | solution.py:370
  93.0 5.8 %collective-permute-start.8 = (f32[24,384]{1,0:T(8,128)S(1)}, f32[24,384]{1,0:T(8,128)S(1)}, u32[]{:S(2)}, u32[]{:S(2)}) collective-permute-start(f32[24,384]{1,0:T(8,128)S(1)} %add_add_fusion.mine_ref), channel_id=1, source_target_pairs={{0,1},{1,0},{2,3},{3,2},{4,5},{5,4},{6,7},{7,6},{8,9},{9,8},{10,11... | collective-permute-start | bytes 110600 | tf_op jit(solution)/shard_map/share_pair/ppermute | solution.py:370

commit v4 on v3

--- a/solution.py
+++ b/solution.py
@@ -53,13 +53,13 @@
         start = jnp.bitwise_xor(me, block) * CAP
 
         def step(i, carry):
-            base = i * 16
-            for u in range(16):
+            base = i * 64
+            for u in range(64):
                 cell = lists_ref[start + base + u]
                 rows[pl.ds(base + u, 1), :] = wide[pl.ds(cell, 1), :]
             return carry
 
-        lax.fori_loop(0, CAP // 16, step, 0)
+        lax.fori_loop(0, CAP // 64, step, 0)
         ref[part] = rows[...].astype(bf16)
 
 
@@ -88,7 +88,7 @@
     place_ref[...] = jnp.concatenate([slots, slots], axis=1)
 
 
-def head_values(me, feat, w_head, slots, block=256):
+def head_values(me, feat, w_head, slots, block=512):
     pixels, width = feat.shape
 
     def rows(height, lanes):
@@ -250,8 +250,8 @@
         mixed[...] = jnp.zeros_like(mixed)
 
         def body(i, carry):
+            pick(i)
             score(i)
-            pick(i)
             mix(i)
             return carry
 

time: 101 us -> 98.1 us (0.971)
  Pallas kernels: 41.2 us -> 38.7 us
    pallas_call x1, Pallas kernels: 5.2 us -> 3.87 us  [head_values(): pl.pallas_call(head_kernel, grid=(pixels // block,), out_shape=(jax.Shape...]
    ppermute x9, waiting for transfers between devices: 6.23 us -> 5.19 us  [hop(): lax.ppermute(value, 'cam', [(i, i ^ distance) for i in range(2 * CHIPS)])]
  transfers between devices with their start and end apart: 10 -> 10, of which waited for: 5 -> 6; matrix products, arithmetic and copies ran while one was open for 0% -> 0% of each run, Pallas kernels for 18% -> 18%
where the time goes in v4:
time: 98.1 us; the launch traced here: 97.7 us
  Pallas kernels  38.7 us (39%)
  blocking collectives  26 us (27%)
  starting transfers between devices  21.3 us (22%)
  waiting for transfers between devices  5.99 us (6%)
  local copies, waits for them, and re-layouts  3.49 us (4%)
  other arithmetic  1.52 us (2%)
    all_to_all x1, blocking collectives, shards(): half = lax.all_to_all(half, 'dp', 0, 0, tiled=True)  26 us
    pallas_call x1, Pallas kernels, inner_halves(): pl.pallas_call(functools.partial(grads_kernel, owners=owners), grid=(bloc...  15.6 us
    ppermute x9, starting transfers between devices, hop(): lax.ppermute(value, 'cam', [(i, i ^ distance) for i in range(2 * CHIPS)])  14.8 us
    pallas_call x2, Pallas kernels, pixel_weights(): pl.pallas_call(weights_kernel, grid=(count,), out_shape=(jax.ShapeDtypeSt...  13.3 us
    all_to_all x1, starting transfers between devices, shards(): lists = lax.all_to_all(cell_lists[0, 0], 'cam', 0, 0, tiled=True)  6.48 us
    ppermute x9, waiting for transfers between devices, hop(): lax.ppermute(value, 'cam', [(i, i ^ distance) for i in range(2 * CHIPS)])  5.19 us
    pallas_call x1, Pallas kernels, gather_rows(): pl.pallas_call(gather_kernel, out_shape=(one, one, two, two, two), in_spe...  4.56 us
    pallas_call x1, Pallas kernels, head_values(): pl.pallas_call(head_kernel, grid=(pixels // block,), out_shape=(jax.Shape...  3.87 us
  transfers between devices with their start and end apart: 10, of which 6 were waited for; matrix products, arithmetic and copies ran while one was open for 0% of the time, Pallas kernels for 18%

profile of v4, /device:TPU:1, one launch (start us, length us, event | category | flops | bytes accessed | tf_op | source)
XLA Modules:
  0.0 97.7 jit_solution(12455695356453128868)
XLA Ops:
  0.6 1.3 %all_to_all.9 = s32[8,1,512]{2,1,0:T(1,128)} reshape(s32[1,1,8,512]{3,2,1,0:T(8,128)} %param.13) | data formatting | bytes 32768 | tf_op jit(solution)/shard_map/lists/all_to_all | solution.py:383
  2.0 6.5 %all-to-all-start = ((s32[8,1,512]{2,1,0:T(1,128)}), s32[8,1,512]{2,1,0:T(1,128)S(1)}, u32[]{:S(2)}, u32[]{:S(2)}) async-start(s32[8,1,512]{2,1,0:T(1,128)} %all_to_all.9), calls=%async_computation | async-start | bytes 32768 | tf_op jit(solution)/shard_map/lists/all_to_all | solution.py:383
  8.4 3.9 %head_values.1 = (f32[1024,128]{1,0:T(8,128)}, bf16[1024,256]{1,0:T(8,128)(2,1)}, s32[1024,128]{1,0:T(8,128)}) custom-call(s32[1]{0:T(128)} %bitcast.1.me_ref, bf16[1024,1536]{1,0:T(8,128)(2,1)} %bitcast.25, bf16[192,1536]{1,0:T(8,128)(2,1)} %bitcast.21, s32[64,1024]{1,0:T(8,128)} %bitcast.29), custom_call_target="tpu_custom_call" | custom-call | flops 4000000000 | bytes 8000000 | tf_op jit(solution)/shard_map/head_values/pallas_call | solution.py:97
  12.3 0.8 all-to-all-done
  13.1 4.6 %gather_rows.1 = (bf16[1,512,128]{2,1,0:T(8,128)(2,1)S(1)}, bf16[1,512,128]{2,1,0:T(8,128)(2,1)S(1)}, bf16[2,512,128]{2,1,0:T(8,128)(2,1)S(1)}, bf16[2,512,128]{2,1,0:T(8,128)(2,1)S(1)}, bf16[2,512,128]{2,1,0:T(8,128)(2,1)S(1)}) custom-call(s32[1]{0:T(128)} %bitcast.1.me_ref, s32[4096]{0:T(1024)S(1)} %bitcast.24, bf16[4096,128]{1,0:T(8,128)(2,1)S(1)} %bitcast.20), custom_call_target="tpu_custom_call" | custom-call | tf_op jit(solution)/shard_map/gather_rows/pallas_call | solution.py:69
  17.7 0.7 collective-permute-start
  18.4 2.4 %collective-permute-start.1 = (bf16[2,512,128]{2,1,0:T(8,128)(2,1)S(1)}, bf16[2,512,128]{2,1,0:T(8,128)(2,1)S(1)}, u32[]{:S(2)}, u32[]{:S(2)}) collective-permute-start(bf16[2,512,128]{2,1,0:T(8,128)(2,1)S(1)} %get-tuple-element.22), channel_id=1, source_target_pairs={{0,4},{1,5},{2,6},{3,7},{4,0},{5,1},{6,2},{7,3},{8,12},{9,13},{10,... | collective-permute-start | bytes 786440 | tf_op jit(solution)/shard_map/rows/ppermute | solution.py:370
  20.8 0.8 collective-permute-start.2
  21.6 1.0 %copy-done = f32[1024,128]{1,0:T(8,128)S(1)} copy-done((f32[1024,128]{1,0:T(8,128)S(1)}, f32[1024,128]{1,0:T(8,128)}, u32[]{:S(2)}) %copy-start) | copy-done | bytes 524312
  22.7 1.0 %copy-done.2 = s32[1024,128]{1,0:T(8,128)S(1)} copy-done((s32[1024,128]{1,0:T(8,128)S(1)}, s32[1024,128]{1,0:T(8,128)}, u32[]{:S(2)}) %copy-start.2) | copy-done | bytes 524312
  23.7 10.6 %pixel_weights.2 = (bf16[2048,4096]{1,0:T(8,128)(2,1)}, f32[8,128]{1,0:T(8,128)S(1)}) custom-call(bf16[1,512,128]{2,1,0:T(8,128)(2,1)S(1)} %get-tuple-element.20.refs_0_.own_ref, f32[1024,128]{1,0:T(8,128)S(1)} %copy-done, s32[1024,128]{1,0:T(8,128)S(1)} %copy-done.2), custom_call_target="tpu_custom_call" | custom-call | flops 17500000256 | bytes 21000000 | tf_op jit(solution)/shard_map/pixel_weights/pallas_call | solution.py:170
  34.3 0.0 collective-permute-done.one_ref
  34.4 0.1 collective-permute-done.2.three_ref
  34.6 1.9 %collective-permute-start.3 = (bf16[2048,128]{1,0:T(8,128)(2,1)S(1)}, bf16[2048,128]{1,0:T(8,128)(2,1)S(1)}, u32[]{:S(2)}, u32[]{:S(2)}) collective-permute-start(bf16[2048,128]{1,0:T(8,128)(2,1)S(1)} %pad_maximum_fusion), channel_id=1, source_target_pairs={{0,1},{1,0},{2,3},{3,2},{4,5},{5,4},{6,7},{7,6},{8,9},{9,8},{10,11... | collective-permute-start | bytes 1572872 | tf_op jit(solution)/shard_map/rows_pair/ppermute | solution.py:370
  36.5 2.6 %pixel_weights.3 = (bf16[2048,4096]{1,0:T(8,128)(2,1)}, f32[8,128]{1,0:T(8,128)}) custom-call(bf16[2048,4096]{1,0:T(8,128)(2,1)} %get-tuple-element.31.refs_0_, f32[8,128]{1,0:T(8,128)S(1)} %get-tuple-element.32.refs_1_, f32[1024,128]{1,0:T(8,128)S(1)} %copy-done.1, s32[1024,128]{1,0:T(8,128)S(1)} %copy-done.3), custom_call_target="tpu_custom_call", output_to_operand_aliasing={{0}: (0, {})} | custom-call | flops 2500000000 | bytes 3000000 | tf_op jit(solution)/shard_map/pixel_weights/pallas_call | solution.py:170
  39.2 15.6 %inner_halves.1 = (f32[768,384]{1,0:T(8,128)}, bf16[768,384]{1,0:T(8,128)(2,1)S(1)}) custom-call(s32[1]{0:T(128)} %bitcast.core_ref, bf16[1,512,128]{2,1,0:T(8,128)(2,1)S(1)} %get-tuple-element.20.refs_0_.own_ref, bf16[2,512,128]{2,1,0:T(8,128)(2,1)S(1)} %collective-permute-done.one_ref, bf16[2,512,128]{2,1,0:T(8,128)(2,1)S(1)} %collective-permute-done.1.two_ref, ...), custom_call_target="tpu_custom_call" | custom-call | tf_op jit(solution)/shard_map/inner_halves/pallas_call | solution.py:304
  54.8 0.7 collective-permute-start.4
  55.5 1.6 %collective-permute-done.4 = bf16[768,384]{1,0:T(8,128)(2,1)S(1)} collective-permute-done((bf16[768,384]{1,0:T(8,128)(2,1)S(1)}, bf16[768,384]{1,0:T(8,128)(2,1)S(1)}, u32[]{:S(2)}, u32[]{:S(2)}) %collective-permute-start.4) | collective-permute-done | bytes 589856 | tf_op jit(solution)/shard_map/sum_pair/ppermute | solution.py:370
  57.1 1.4 %add_convert_fusion = bf16[768,384]{1,0:T(8,128)(2,1)S(1)} fusion(f32[768,384]{1,0:T(8,128)} %get-tuple-element.35, bf16[768,384]{1,0:T(8,128)(2,1)S(1)} %collective-permute-done.4), kind=kLoop, calls=%fused_computation.1 | loop fusion | flops 884736 | bytes 2359296 | tf_op jit(solution)/shard_map/sum_pair/convert_element_type | solution.py:397
  58.5 0.0 copy-start.5
  58.5 0.0 copy-start.7
  58.5 0.0 copy-start.8
  58.5 0.0 copy-start.9
  58.5 26.0 %all_to_all.14 = bf16[32,24,384]{2,1,0:T(8,128)(2,1)S(1)} all-to-all(bf16[32,24,384]{2,1,0:T(8,128)(2,1)S(1)} %bitcast.28), channel_id=1, replica_groups=mesh['dp'=32,'cam'=8] {'dp'}, dimensions={0} | all-to-all | bytes 1179648 | tf_op jit(solution)/shard_map/sum_dp/all_to_all | solution.py:400
  84.5 0.1 convert_reduce_fusion
  84.6 1.6 %collective-permute-start.7 = (f32[24,384]{1,0:T(8,128)S(1)}, f32[24,384]{1,0:T(8,128)S(1)}, u32[]{:S(2)}, u32[]{:S(2)}) collective-permute-start(f32[24,384]{1,0:T(8,128)S(1)} %convert_reduce_fusion), channel_id=1, source_target_pairs={{0,6},{1,7},{2,4},{3,5},{4,2},{5,3},{6,0},{7,1},{8,14},{9,15},{10,... | collective-permute-start | bytes 110600 | tf_op jit(solution)/shard_map/sum_x/ppermute | solution.py:370
  86.2 1.8 %collective-permute-start.5 = (f32[24,384]{1,0:T(8,128)S(1)}, f32[24,384]{1,0:T(8,128)S(1)}, u32[]{:S(2)}, u32[]{:S(2)}) collective-permute-start(f32[24,384]{1,0:T(8,128)S(1)} %convert_reduce_fusion), channel_id=1, source_target_pairs={{0,2},{1,3},{2,0},{3,1},{4,6},{5,7},{6,4},{7,5},{8,10},{9,11},{10,... | collective-permute-start | bytes 110600 | tf_op jit(solution)/shard_map/sum_x/ppermute | solution.py:370
  87.9 0.8 collective-permute-done.7
  88.7 1.8 %collective-permute-done.6 = f32[24,384]{1,0:T(8,128)S(1)} collective-permute-done((f32[24,384]{1,0:T(8,128)S(1)}, f32[24,384]{1,0:T(8,128)S(1)}, u32[]{:S(2)}, u32[]{:S(2)}) %collective-permute-start.6) | collective-permute-done | bytes 36896 | tf_op jit(solution)/shard_map/sum_x/ppermute | solution.py:370
  90.5 4.9 %collective-permute-start.8 = (f32[24,384]{1,0:T(8,128)S(1)}, f32[24,384]{1,0:T(8,128)S(1)}, u32[]{:S(2)}, u32[]{:S(2)}) collective-permute-start(f32[24,384]{1,0:T(8,128)S(1)} %add_add_fusion.mine_ref), channel_id=1, source_target_pairs={{0,1},{1,0},{2,3},{3,2},{4,5},{5,4},{6,7},{7,6},{8,9},{9,8},{10,11... | collective-permute-start | bytes 110600 | tf_op jit(solution)/shard_map/share_pair/ppermute | solution.py:370
  95.4 0.9 collective-permute-done.8.other_ref
  96.3 1.4 %adam_update.1 = (f32[48,1728]{1,0:T(8,128)}, f32[48,1728]{1,0:T(8,128)}, f32[48,1728]{1,0:T(8,128)}) custom-call(s32[1]{0:T(128)} %bitcast.core_ref, f32[24,384]{1,0:T(8,128)S(1)} %add_add_fusion.mine_ref, f32[24,384]{1,0:T(8,128)S(1)} %collective-permute-done.8.other_ref, bf16[192,1536]{1,0:T(8,128)(2,1)S(1)} %bitcast.22, f32[48,1728]{1,0:T(8,128)S(1)} %copy-done.7, ...), custom_call_target="tpu_custom_call" | custom-call | tf_op jit(solution)/shard_map/adam_update/pallas_call | solution.py:359
  (22 shorter events, 0.1 us)
Async XLA Ops:
  2.0 11.2 %all-to-all-start = ((s32[8,1,512]{2,1,0:T(1,128)}), s32[8,1,512]{2,1,0:T(1,128)S(1)}, u32[]{:S(2)}, u32[]{:S(2)}) async-start(s32[8,1,512]{2,1,0:T(1,128)} %all_to_all.9), calls=%async_computation | async-start | bytes 32768 | tf_op jit(solution)/shard_map/lists/all_to_all | solution.py:383
  8.4 4.7 %copy-start.4 = (bf16[1,4096,128]{2,1,0:T(8,128)(2,1)S(1)}, bf16[1,4096,128]{2,1,0:T(8,128)(2,1)}, u32[]{:S(2)}) copy-start(bf16[1,4096,128]{2,1,0:T(8,128)(2,1)} %param.12) | copy-start | bytes 3145732
  17.7 16.7 %collective-permute-start = (bf16[2,512,128]{2,1,0:T(8,128)(2,1)S(1)}, bf16[2,512,128]{2,1,0:T(8,128)(2,1)S(1)}, u32[]{:S(2)}, u32[]{:S(2)}) collective-permute-start(bf16[2,512,128]{2,1,0:T(8,128)(2,1)S(1)} %get-tuple-element.21), channel_id=1, source_target_pairs={{0,2},{1,3},{2,0},{3,1},{4,6},{5,7},{6,4},{7,5},{8,10},{9,11},{10,... | collective-permute-start | bytes 786440 | tf_op jit(solution)/shard_map/rows/ppermute | solution.py:370
  18.4 16.0 %collective-permute-start.1 = (bf16[2,512,128]{2,1,0:T(8,128)(2,1)S(1)}, bf16[2,512,128]{2,1,0:T(8,128)(2,1)S(1)}, u32[]{:S(2)}, u32[]{:S(2)}) collective-permute-start(bf16[2,512,128]{2,1,0:T(8,128)(2,1)S(1)} %get-tuple-element.22), channel_id=1, source_target_pairs={{0,4},{1,5},{2,6},{3,7},{4,0},{5,1},{6,2},{7,3},{8,12},{9,13},{10,... | collective-permute-start | bytes 786440 | tf_op jit(solution)/shard_map/rows/ppermute | solution.py:370
  20.8 13.7 %collective-permute-start.2 = (bf16[2,512,128]{2,1,0:T(8,128)(2,1)S(1)}, bf16[2,512,128]{2,1,0:T(8,128)(2,1)S(1)}, u32[]{:S(2)}, u32[]{:S(2)}) collective-permute-start(bf16[2,512,128]{2,1,0:T(8,128)(2,1)S(1)} %get-tuple-element.23), channel_id=1, source_target_pairs={{0,6},{1,7},{2,4},{3,5},{4,2},{5,3},{6,0},{7,1},{8,14},{9,15},{10,... | collective-permute-start | bytes 786440 | tf_op jit(solution)/shard_map/rows/ppermute | solution.py:370
  21.6 1.0 %copy-start = (f32[1024,128]{1,0:T(8,128)S(1)}, f32[1024,128]{1,0:T(8,128)}, u32[]{:S(2)}) copy-start(f32[1024,128]{1,0:T(8,128)} %get-tuple-element.24.refs_1_.refs_2_.occ_ref) | copy-start | bytes 1572868
  22.7 1.0 %copy-start.2 = (s32[1024,128]{1,0:T(8,128)S(1)}, s32[1024,128]{1,0:T(8,128)}, u32[]{:S(2)}) copy-start(s32[1024,128]{1,0:T(8,128)} %get-tuple-element.25.refs_2_.refs_3_.place_ref) | copy-start | bytes 1572868
  34.3 2.2 %copy-start.1 = (f32[1024,128]{1,0:T(8,128)S(1)}, f32[1024,128]{1,0:T(8,128)}, u32[]{:S(2)}) copy-start(f32[1024,128]{1,0:T(8,128)} %get-tuple-element.24.refs_1_.refs_2_.occ_ref) | copy-start | bytes 1572868
  34.3 2.2 %copy-start.3 = (s32[1024,128]{1,0:T(8,128)S(1)}, s32[1024,128]{1,0:T(8,128)}, u32[]{:S(2)}) copy-start(s32[1024,128]{1,0:T(8,128)} %get-tuple-element.25.refs_2_.refs_3_.place_ref) | copy-start | bytes 1572868
  34.6 4.6 %collective-permute-start.3 = (bf16[2048,128]{1,0:T(8,128)(2,1)S(1)}, bf16[2048,128]{1,0:T(8,128)(2,1)S(1)}, u32[]{:S(2)}, u32[]{:S(2)}) collective-permute-start(bf16[2048,128]{1,0:T(8,128)(2,1)S(1)} %pad_maximum_fusion), channel_id=1, source_target_pairs={{0,1},{1,0},{2,3},{3,2},{4,5},{5,4},{6,7},{7,6},{8,9},{9,8},{10,11... | collective-permute-start | bytes 1572872 | tf_op jit(solution)/shard_map/rows_pair/ppermute | solution.py:370
  36.5 2.6 %copy-start.6 = (bf16[1024,256]{1,0:T(8,128)(2,1)S(1)}, bf16[1024,256]{1,0:T(8,128)(2,1)}, u32[]{:S(2)}) copy-start(bf16[1024,256]{1,0:T(8,128)(2,1)} %get-tuple-element.34.ctx_ref) | copy-start | bytes 1572868
  54.8 2.3 %collective-permute-start.4 = (bf16[768,384]{1,0:T(8,128)(2,1)S(1)}, bf16[768,384]{1,0:T(8,128)(2,1)S(1)}, u32[]{:S(2)}, u32[]{:S(2)}) collective-permute-start(bf16[768,384]{1,0:T(8,128)(2,1)S(1)} %get-tuple-element.36), channel_id=1, source_target_pairs={{0,1},{1,0},{2,3},{3,2},{4,5},{5,4},{6,7},{7,6},{8,9},{9,8},{10,11... | collective-permute-start | bytes 1769480 | tf_op jit(solution)/shard_map/sum_pair/ppermute | solution.py:370
  58.5 37.8 %copy-start.5 = (bf16[1536,192]{0,1:T(8,128)(2,1)S(1)}, bf16[1536,192]{0,1:T(8,128)(2,1)}, u32[]{:S(2)}) copy-start(bf16[1536,192]{0,1:T(8,128)(2,1)} %param.11) | copy-start | bytes 1769476
  58.5 37.8 %copy-start.7 = (f32[48,1728]{1,0:T(8,128)S(1)}, f32[48,1728]{1,0:T(8,128)}, u32[]{:S(2)}) copy-start(f32[48,1728]{1,0:T(8,128)} %master_ref.1) | copy-start | bytes 995332
  58.5 37.8 %copy-start.8 = (f32[48,1728]{1,0:T(8,128)S(1)}, f32[48,1728]{1,0:T(8,128)}, u32[]{:S(2)}) copy-start(f32[48,1728]{1,0:T(8,128)} %first_ref.1) | copy-start | bytes 995332
  58.5 37.8 %copy-start.9 = (f32[48,1728]{1,0:T(8,128)S(1)}, f32[48,1728]{1,0:T(8,128)}, u32[]{:S(2)}) copy-start(f32[48,1728]{1,0:T(8,128)} %second_ref.1) | copy-start | bytes 995332
  84.6 4.1 %collective-permute-start.7 = (f32[24,384]{1,0:T(8,128)S(1)}, f32[24,384]{1,0:T(8,128)S(1)}, u32[]{:S(2)}, u32[]{:S(2)}) collective-permute-start(f32[24,384]{1,0:T(8,128)S(1)} %convert_reduce_fusion), channel_id=1, source_target_pairs={{0,6},{1,7},{2,4},{3,5},{4,2},{5,3},{6,0},{7,1},{8,14},{9,15},{10,... | collective-permute-start | bytes 110600 | tf_op jit(solution)/shard_map/sum_x/ppermute | solution.py:370
  86.2 4.3 %collective-permute-start.6 = (f32[24,384]{1,0:T(8,128)S(1)}, f32[24,384]{1,0:T(8,128)S(1)}, u32[]{:S(2)}, u32[]{:S(2)}) collective-permute-start(f32[24,384]{1,0:T(8,128)S(1)} %convert_reduce_fusion), channel_id=1, source_target_pairs={{0,4},{1,5},{2,6},{3,7},{4,0},{5,1},{6,2},{7,3},{8,12},{9,13},{10,... | collective-permute-start | bytes 110600 | tf_op jit(solution)/shard_map/sum_x/ppermute | solution.py:370
  86.2 4.3 %collective-permute-start.5 = (f32[24,384]{1,0:T(8,128)S(1)}, f32[24,384]{1,0:T(8,128)S(1)}, u32[]{:S(2)}, u32[]{:S(2)}) collective-permute-start(f32[24,384]{1,0:T(8,128)S(1)} %convert_reduce_fusion), channel_id=1, source_target_pairs={{0,2},{1,3},{2,0},{3,1},{4,6},{5,7},{6,4},{7,5},{8,10},{9,11},{10,... | collective-permute-start | bytes 110600 | tf_op jit(solution)/shard_map/sum_x/ppermute | solution.py:370
  90.5 5.8 %collective-permute-start.8 = (f32[24,384]{1,0:T(8,128)S(1)}, f32[24,384]{1,0:T(8,128)S(1)}, u32[]{:S(2)}, u32[]{:S(2)}) collective-permute-start(f32[24,384]{1,0:T(8,128)S(1)} %add_add_fusion.mine_ref), channel_id=1, source_target_pairs={{0,1},{1,0},{2,3},{3,2},{4,5},{5,4},{6,7},{7,6},{8,9},{9,8},{10,11... | collective-permute-start | bytes 110600 | tf_op jit(solution)/shard_map/share_pair/ppermute | solution.py:370

commit v5 on v4

--- a/solution.py
+++ b/solution.py
@@ -400,7 +400,8 @@
         half = lax.all_to_all(half, "dp", 0, 0, tiled=True)
         half = jnp.sum(half.astype(f32), axis=0)
     with jax.named_scope("sum_x"):
-        half = (half + hop(half, 2)) + (hop(half, 4) + hop(half, 6))
+        half = half + hop(half, 2)
+        half = half + hop(half, 6)
     with jax.named_scope("share_pair"):
         other = hop(half, 1)
     scale = 1.0 / math.sqrt(data_count * cam_count * pixels)

time: 98.1 us -> 100 us (1.019)
  waiting for transfers between devices: 5.99 us -> 8.82 us
  starting transfers between devices: 21.3 us -> 20.3 us
    ppermute x9 -> x8, waiting for transfers between devices: 5.19 us -> 8 us  [hop(): lax.ppermute(value, 'cam', [(i, i ^ distance) for i in range(2 * CHIPS)])]
    ppermute x9 -> x8, starting transfers between devices: 14.8 us -> 13.8 us  [hop(): lax.ppermute(value, 'cam', [(i, i ^ distance) for i in range(2 * CHIPS)])]
  transfers between devices with their start and end apart: 10 -> 9, of which waited for: 6 -> 6; matrix products, arithmetic and copies ran while one was open for 0% -> 0% of each run, Pallas kernels for 18% -> 17%
where the time goes in v5:
time: 100 us; the launch traced here: 99.5 us
  Pallas kernels  38.7 us (39%)
  blocking collectives  26 us (26%)
  starting transfers between devices  20.3 us (20%)
  waiting for transfers between devices  8.82 us (9%)
  local copies, waits for them, and re-layouts  3.49 us (3%)
  other arithmetic  1.52 us (2%)
    all_to_all x1, blocking collectives, shards(): half = lax.all_to_all(half, 'dp', 0, 0, tiled=True)  26 us
    pallas_call x1, Pallas kernels, inner_halves(): pl.pallas_call(functools.partial(grads_kernel, owners=owners), grid=(bloc...  15.6 us
    ppermute x8, starting transfers between devices, hop(): lax.ppermute(value, 'cam', [(i, i ^ distance) for i in range(2 * CHIPS)])  13.8 us
    pallas_call x2, Pallas kernels, pixel_weights(): pl.pallas_call(weights_kernel, grid=(count,), out_shape=(jax.ShapeDtypeSt...  13.3 us
    ppermute x8, waiting for transfers between devices, hop(): lax.ppermute(value, 'cam', [(i, i ^ distance) for i in range(2 * CHIPS)])  8 us
    all_to_all x1, starting transfers between devices, shards(): lists = lax.all_to_all(cell_lists[0, 0], 'cam', 0, 0, tiled=True)  6.48 us
    pallas_call x1, Pallas kernels, gather_rows(): pl.pallas_call(gather_kernel, out_shape=(one, one, two, two, two), in_spe...  4.56 us
    pallas_call x1, Pallas kernels, head_values(): pl.pallas_call(head_kernel, grid=(pixels // block,), out_shape=(jax.Shape...  3.85 us
  transfers between devices with their start and end apart: 9, of which 6 were waited for; matrix products, arithmetic and copies ran while one was open for 0% of the time, Pallas kernels for 17%

profile of v5, /device:TPU:1, one launch (start us, length us, event | category | flops | bytes accessed | tf_op | source)
XLA Modules:
  0.0 99.5 jit_solution(5012684495625620174)
XLA Ops:
  0.6 1.3 %all_to_all.9 = s32[8,1,512]{2,1,0:T(1,128)} reshape(s32[1,1,8,512]{3,2,1,0:T(8,128)} %param.13) | data formatting | bytes 32768 | tf_op jit(solution)/shard_map/lists/all_to_all | solution.py:383
  2.0 6.5 %all-to-all-start = ((s32[8,1,512]{2,1,0:T(1,128)}), s32[8,1,512]{2,1,0:T(1,128)S(1)}, u32[]{:S(2)}, u32[]{:S(2)}) async-start(s32[8,1,512]{2,1,0:T(1,128)} %all_to_all.9), calls=%async_computation | async-start | bytes 32768 | tf_op jit(solution)/shard_map/lists/all_to_all | solution.py:383
  8.4 3.9 %head_values.1 = (f32[1024,128]{1,0:T(8,128)}, bf16[1024,256]{1,0:T(8,128)(2,1)}, s32[1024,128]{1,0:T(8,128)}) custom-call(s32[1]{0:T(128)} %bitcast.1.me_ref, bf16[1024,1536]{1,0:T(8,128)(2,1)} %bitcast.25, bf16[192,1536]{1,0:T(8,128)(2,1)} %bitcast.21, s32[64,1024]{1,0:T(8,128)} %bitcast.29), custom_call_target="tpu_custom_call" | custom-call | flops 4000000000 | bytes 8000000 | tf_op jit(solution)/shard_map/head_values/pallas_call | solution.py:97
  12.3 0.8 all-to-all-done
  13.1 4.6 %gather_rows.1 = (bf16[1,512,128]{2,1,0:T(8,128)(2,1)S(1)}, bf16[1,512,128]{2,1,0:T(8,128)(2,1)S(1)}, bf16[2,512,128]{2,1,0:T(8,128)(2,1)S(1)}, bf16[2,512,128]{2,1,0:T(8,128)(2,1)S(1)}, bf16[2,512,128]{2,1,0:T(8,128)(2,1)S(1)}) custom-call(s32[1]{0:T(128)} %bitcast.1.me_ref, s32[4096]{0:T(1024)S(1)} %bitcast.24, bf16[4096,128]{1,0:T(8,128)(2,1)S(1)} %bitcast.20), custom_call_target="tpu_custom_call" | custom-call | tf_op jit(solution)/shard_map/gather_rows/pallas_call | solution.py:69
  17.7 0.7 collective-permute-start
  18.4 2.4 %collective-permute-start.1 = (bf16[2,512,128]{2,1,0:T(8,128)(2,1)S(1)}, bf16[2,512,128]{2,1,0:T(8,128)(2,1)S(1)}, u32[]{:S(2)}, u32[]{:S(2)}) collective-permute-start(bf16[2,512,128]{2,1,0:T(8,128)(2,1)S(1)} %get-tuple-element.22), channel_id=1, source_target_pairs={{0,4},{1,5},{2,6},{3,7},{4,0},{5,1},{6,2},{7,3},{8,12},{9,13},{10,... | collective-permute-start | bytes 786440 | tf_op jit(solution)/shard_map/rows/ppermute | solution.py:370
  20.8 0.9 collective-permute-start.2
  21.6 1.0 %copy-done = f32[1024,128]{1,0:T(8,128)S(1)} copy-done((f32[1024,128]{1,0:T(8,128)S(1)}, f32[1024,128]{1,0:T(8,128)}, u32[]{:S(2)}) %copy-start) | copy-done | bytes 524312
  22.7 1.0 %copy-done.2 = s32[1024,128]{1,0:T(8,128)S(1)} copy-done((s32[1024,128]{1,0:T(8,128)S(1)}, s32[1024,128]{1,0:T(8,128)}, u32[]{:S(2)}) %copy-start.2) | copy-done | bytes 524312
  23.7 10.6 %pixel_weights.2 = (bf16[2048,4096]{1,0:T(8,128)(2,1)}, f32[8,128]{1,0:T(8,128)S(1)}) custom-call(bf16[1,512,128]{2,1,0:T(8,128)(2,1)S(1)} %get-tuple-element.20.refs_0_.own_ref, f32[1024,128]{1,0:T(8,128)S(1)} %copy-done, s32[1024,128]{1,0:T(8,128)S(1)} %copy-done.2), custom_call_target="tpu_custom_call" | custom-call | flops 17500000256 | bytes 21000000 | tf_op jit(solution)/shard_map/pixel_weights/pallas_call | solution.py:170
  34.4 0.0 collective-permute-done.one_ref
  34.4 0.1 collective-permute-done.2.three_ref
  34.6 1.9 %collective-permute-start.3 = (bf16[2048,128]{1,0:T(8,128)(2,1)S(1)}, bf16[2048,128]{1,0:T(8,128)(2,1)S(1)}, u32[]{:S(2)}, u32[]{:S(2)}) collective-permute-start(bf16[2048,128]{1,0:T(8,128)(2,1)S(1)} %pad_maximum_fusion), channel_id=1, source_target_pairs={{0,1},{1,0},{2,3},{3,2},{4,5},{5,4},{6,7},{7,6},{8,9},{9,8},{10,11... | collective-permute-start | bytes 1572872 | tf_op jit(solution)/shard_map/rows_pair/ppermute | solution.py:370
  36.5 2.6 %pixel_weights.3 = (bf16[2048,4096]{1,0:T(8,128)(2,1)}, f32[8,128]{1,0:T(8,128)}) custom-call(bf16[2048,4096]{1,0:T(8,128)(2,1)} %get-tuple-element.31.refs_0_, f32[8,128]{1,0:T(8,128)S(1)} %get-tuple-element.32.refs_1_, f32[1024,128]{1,0:T(8,128)S(1)} %copy-done.1, s32[1024,128]{1,0:T(8,128)S(1)} %copy-done.3), custom_call_target="tpu_custom_call", output_to_operand_aliasing={{0}: (0, {})} | custom-call | flops 2500000000 | bytes 3000000 | tf_op jit(solution)/shard_map/pixel_weights/pallas_call | solution.py:170
  39.1 15.6 %inner_halves.1 = (f32[768,384]{1,0:T(8,128)}, bf16[768,384]{1,0:T(8,128)(2,1)S(1)}) custom-call(s32[1]{0:T(128)} %bitcast.core_ref, bf16[1,512,128]{2,1,0:T(8,128)(2,1)S(1)} %get-tuple-element.20.refs_0_.own_ref, bf16[2,512,128]{2,1,0:T(8,128)(2,1)S(1)} %collective-permute-done.one_ref, bf16[2,512,128]{2,1,0:T(8,128)(2,1)S(1)} %collective-permute-done.1.two_ref, ...), custom_call_target="tpu_custom_call" | custom-call | tf_op jit(solution)/shard_map/inner_halves/pallas_call | solution.py:304
  54.8 0.7 collective-permute-start.4
  55.5 1.6 %collective-permute-done.4 = bf16[768,384]{1,0:T(8,128)(2,1)S(1)} collective-permute-done((bf16[768,384]{1,0:T(8,128)(2,1)S(1)}, bf16[768,384]{1,0:T(8,128)(2,1)S(1)}, u32[]{:S(2)}, u32[]{:S(2)}) %collective-permute-start.4) | collective-permute-done | bytes 589856 | tf_op jit(solution)/shard_map/sum_pair/ppermute | solution.py:370
  57.1 1.4 %add_convert_fusion = bf16[768,384]{1,0:T(8,128)(2,1)S(1)} fusion(f32[768,384]{1,0:T(8,128)} %get-tuple-element.35, bf16[768,384]{1,0:T(8,128)(2,1)S(1)} %collective-permute-done.4), kind=kLoop, calls=%fused_computation.1 | loop fusion | flops 884736 | bytes 2359296 | tf_op jit(solution)/shard_map/sum_pair/convert_element_type | solution.py:397
  58.5 0.0 copy-start.5
  58.5 0.0 copy-start.7
  58.5 0.0 copy-start.8
  58.5 0.0 copy-start.9
  58.5 26.0 %all_to_all.14 = bf16[32,24,384]{2,1,0:T(8,128)(2,1)S(1)} all-to-all(bf16[32,24,384]{2,1,0:T(8,128)(2,1)S(1)} %bitcast.28), channel_id=1, replica_groups=mesh['dp'=32,'cam'=8] {'dp'}, dimensions={0} | all-to-all | bytes 1179648 | tf_op jit(solution)/shard_map/sum_dp/all_to_all | solution.py:400
  84.5 0.1 convert_reduce_fusion
  84.6 0.1 collective-permute-start.5
  84.7 2.8 %collective-permute-done.5 = f32[24,384]{1,0:T(8,128)S(1)} collective-permute-done((f32[24,384]{1,0:T(8,128)S(1)}, f32[24,384]{1,0:T(8,128)S(1)}, u32[]{:S(2)}, u32[]{:S(2)}) %collective-permute-start.5) | collective-permute-done | bytes 36896 | tf_op jit(solution)/shard_map/sum_x/ppermute | solution.py:370
  87.5 1.5 %collective-permute-start.6 = (f32[24,384]{1,0:T(8,128)S(1)}, f32[24,384]{1,0:T(8,128)S(1)}, u32[]{:S(2)}, u32[]{:S(2)}) collective-permute-start(f32[24,384]{1,0:T(8,128)S(1)} %add.10), channel_id=1, source_target_pairs={{0,6},{1,7},{2,4},{3,5},{4,2},{5,3},{6,0},{7,1},{8,14},{9,15},{10,... | collective-permute-start | bytes 110600 | tf_op jit(solution)/shard_map/sum_x/ppermute | solution.py:370
  89.0 2.6 %collective-permute-done.6 = f32[24,384]{1,0:T(8,128)S(1)} collective-permute-done((f32[24,384]{1,0:T(8,128)S(1)}, f32[24,384]{1,0:T(8,128)S(1)}, u32[]{:S(2)}, u32[]{:S(2)}) %collective-permute-start.6) | collective-permute-done | bytes 36896 | tf_op jit(solution)/shard_map/sum_x/ppermute | solution.py:370
  91.6 5.7 %collective-permute-start.7 = (f32[24,384]{1,0:T(8,128)S(1)}, f32[24,384]{1,0:T(8,128)S(1)}, u32[]{:S(2)}, u32[]{:S(2)}) collective-permute-start(f32[24,384]{1,0:T(8,128)S(1)} %add.11.mine_ref), channel_id=1, source_target_pairs={{0,1},{1,0},{2,3},{3,2},{4,5},{5,4},{6,7},{7,6},{8,9},{9,8},{10,11... | collective-permute-start | bytes 110600 | tf_op jit(solution)/shard_map/share_pair/ppermute | solution.py:370
  97.3 0.9 collective-permute-done.7.other_ref
  98.1 1.4 %adam_update.1 = (f32[48,1728]{1,0:T(8,128)}, f32[48,1728]{1,0:T(8,128)}, f32[48,1728]{1,0:T(8,128)}) custom-call(s32[1]{0:T(128)} %bitcast.core_ref, f32[24,384]{1,0:T(8,128)S(1)} %add.11.mine_ref, f32[24,384]{1,0:T(8,128)S(1)} %collective-permute-done.7.other_ref, bf16[192,1536]{1,0:T(8,128)(2,1)S(1)} %bitcast.22, f32[48,1728]{1,0:T(8,128)S(1)} %copy-done.7, ...), custom_call_target="tpu_custom_call" | custom-call | tf_op jit(solution)/shard_map/adam_update/pallas_call | solution.py:359
  (21 shorter events, 0.1 us)
Async XLA Ops:
  2.0 11.2 %all-to-all-start = ((s32[8,1,512]{2,1,0:T(1,128)}), s32[8,1,512]{2,1,0:T(1,128)S(1)}, u32[]{:S(2)}, u32[]{:S(2)}) async-start(s32[8,1,512]{2,1,0:T(1,128)} %all_to_all.9), calls=%async_computation | async-start | bytes 32768 | tf_op jit(solution)/shard_map/lists/all_to_all | solution.py:383
  8.4 4.7 %copy-start.4 = (bf16[1,4096,128]{2,1,0:T(8,128)(2,1)S(1)}, bf16[1,4096,128]{2,1,0:T(8,128)(2,1)}, u32[]{:S(2)}) copy-start(bf16[1,4096,128]{2,1,0:T(8,128)(2,1)} %param.12) | copy-start | bytes 3145732
  17.7 16.7 %collective-permute-start = (bf16[2,512,128]{2,1,0:T(8,128)(2,1)S(1)}, bf16[2,512,128]{2,1,0:T(8,128)(2,1)S(1)}, u32[]{:S(2)}, u32[]{:S(2)}) collective-permute-start(bf16[2,512,128]{2,1,0:T(8,128)(2,1)S(1)} %get-tuple-element.21), channel_id=1, source_target_pairs={{0,2},{1,3},{2,0},{3,1},{4,6},{5,7},{6,4},{7,5},{8,10},{9,11},{10,... | collective-permute-start | bytes 786440 | tf_op jit(solution)/shard_map/rows/ppermute | solution.py:370
  18.4 16.0 %collective-permute-start.1 = (bf16[2,512,128]{2,1,0:T(8,128)(2,1)S(1)}, bf16[2,512,128]{2,1,0:T(8,128)(2,1)S(1)}, u32[]{:S(2)}, u32[]{:S(2)}) collective-permute-start(bf16[2,512,128]{2,1,0:T(8,128)(2,1)S(1)} %get-tuple-element.22), channel_id=1, source_target_pairs={{0,4},{1,5},{2,6},{3,7},{4,0},{5,1},{6,2},{7,3},{8,12},{9,13},{10,... | collective-permute-start | bytes 786440 | tf_op jit(solution)/shard_map/rows/ppermute | solution.py:370
  20.8 13.7 %collective-permute-start.2 = (bf16[2,512,128]{2,1,0:T(8,128)(2,1)S(1)}, bf16[2,512,128]{2,1,0:T(8,128)(2,1)S(1)}, u32[]{:S(2)}, u32[]{:S(2)}) collective-permute-start(bf16[2,512,128]{2,1,0:T(8,128)(2,1)S(1)} %get-tuple-element.23), channel_id=1, source_target_pairs={{0,6},{1,7},{2,4},{3,5},{4,2},{5,3},{6,0},{7,1},{8,14},{9,15},{10,... | collective-permute-start | bytes 786440 | tf_op jit(solution)/shard_map/rows/ppermute | solution.py:370
  21.6 1.0 %copy-start = (f32[1024,128]{1,0:T(8,128)S(1)}, f32[1024,128]{1,0:T(8,128)}, u32[]{:S(2)}) copy-start(f32[1024,128]{1,0:T(8,128)} %get-tuple-element.24.refs_1_.refs_2_.occ_ref) | copy-start | bytes 1572868
  22.7 1.0 %copy-start.2 = (s32[1024,128]{1,0:T(8,128)S(1)}, s32[1024,128]{1,0:T(8,128)}, u32[]{:S(2)}) copy-start(s32[1024,128]{1,0:T(8,128)} %get-tuple-element.25.refs_2_.refs_3_.place_ref) | copy-start | bytes 1572868
  34.4 2.1 %copy-start.1 = (f32[1024,128]{1,0:T(8,128)S(1)}, f32[1024,128]{1,0:T(8,128)}, u32[]{:S(2)}) copy-start(f32[1024,128]{1,0:T(8,128)} %get-tuple-element.24.refs_1_.refs_2_.occ_ref) | copy-start | bytes 1572868
  34.4 2.1 %copy-start.3 = (s32[1024,128]{1,0:T(8,128)S(1)}, s32[1024,128]{1,0:T(8,128)}, u32[]{:S(2)}) copy-start(s32[1024,128]{1,0:T(8,128)} %get-tuple-element.25.refs_2_.refs_3_.place_ref) | copy-start | bytes 1572868
  34.6 4.6 %collective-permute-start.3 = (bf16[2048,128]{1,0:T(8,128)(2,1)S(1)}, bf16[2048,128]{1,0:T(8,128)(2,1)S(1)}, u32[]{:S(2)}, u32[]{:S(2)}) collective-permute-start(bf16[2048,128]{1,0:T(8,128)(2,1)S(1)} %pad_maximum_fusion), channel_id=1, source_target_pairs={{0,1},{1,0},{2,3},{3,2},{4,5},{5,4},{6,7},{7,6},{8,9},{9,8},{10,11... | collective-permute-start | bytes 1572872 | tf_op jit(solution)/shard_map/rows_pair/ppermute | solution.py:370
  36.5 2.6 %copy-start.6 = (bf16[1024,256]{1,0:T(8,128)(2,1)S(1)}, bf16[1024,256]{1,0:T(8,128)(2,1)}, u32[]{:S(2)}) copy-start(bf16[1024,256]{1,0:T(8,128)(2,1)} %get-tuple-element.34.ctx_ref) | copy-start | bytes 1572868
  54.8 2.3 %collective-permute-start.4 = (bf16[768,384]{1,0:T(8,128)(2,1)S(1)}, bf16[768,384]{1,0:T(8,128)(2,1)S(1)}, u32[]{:S(2)}, u32[]{:S(2)}) collective-permute-start(bf16[768,384]{1,0:T(8,128)(2,1)S(1)} %get-tuple-element.36), channel_id=1, source_target_pairs={{0,1},{1,0},{2,3},{3,2},{4,5},{5,4},{6,7},{7,6},{8,9},{9,8},{10,11... | collective-permute-start | bytes 1769480 | tf_op jit(solution)/shard_map/sum_pair/ppermute | solution.py:370
  58.5 39.6 %copy-start.5 = (bf16[1536,192]{0,1:T(8,128)(2,1)S(1)}, bf16[1536,192]{0,1:T(8,128)(2,1)}, u32[]{:S(2)}) copy-start(bf16[1536,192]{0,1:T(8,128)(2,1)} %param.11) | copy-start | bytes 1769476
  58.5 39.6 %copy-start.7 = (f32[48,1728]{1,0:T(8,128)S(1)}, f32[48,1728]{1,0:T(8,128)}, u32[]{:S(2)}) copy-start(f32[48,1728]{1,0:T(8,128)} %master_ref.1) | copy-start | bytes 995332
  58.5 39.6 %copy-start.8 = (f32[48,1728]{1,0:T(8,128)S(1)}, f32[48,1728]{1,0:T(8,128)}, u32[]{:S(2)}) copy-start(f32[48,1728]{1,0:T(8,128)} %first_ref.1) | copy-start | bytes 995332
  58.5 39.6 %copy-start.9 = (f32[48,1728]{1,0:T(8,128)S(1)}, f32[48,1728]{1,0:T(8,128)}, u32[]{:S(2)}) copy-start(f32[48,1728]{1,0:T(8,128)} %second_ref.1) | copy-start | bytes 995332
  84.6 2.9 %collective-permute-start.5 = (f32[24,384]{1,0:T(8,128)S(1)}, f32[24,384]{1,0:T(8,128)S(1)}, u32[]{:S(2)}, u32[]{:S(2)}) collective-permute-start(f32[24,384]{1,0:T(8,128)S(1)} %convert_reduce_fusion), channel_id=1, source_target_pairs={{0,2},{1,3},{2,0},{3,1},{4,6},{5,7},{6,4},{7,5},{8,10},{9,11},{10,... | collective-permute-start | bytes 110600 | tf_op jit(solution)/shard_map/sum_x/ppermute | solution.py:370
  87.5 4.0 %collective-permute-start.6 = (f32[24,384]{1,0:T(8,128)S(1)}, f32[24,384]{1,0:T(8,128)S(1)}, u32[]{:S(2)}, u32[]{:S(2)}) collective-permute-start(f32[24,384]{1,0:T(8,128)S(1)} %add.10), channel_id=1, source_target_pairs={{0,6},{1,7},{2,4},{3,5},{4,2},{5,3},{6,0},{7,1},{8,14},{9,15},{10,... | collective-permute-start | bytes 110600 | tf_op jit(solution)/shard_map/sum_x/ppermute | solution.py:370
  91.6 6.5 %collective-permute-start.7 = (f32[24,384]{1,0:T(8,128)S(1)}, f32[24,384]{1,0:T(8,128)S(1)}, u32[]{:S(2)}, u32[]{:S(2)}) collective-permute-start(f32[24,384]{1,0:T(8,128)S(1)} %add.11.mine_ref), channel_id=1, source_target_pairs={{0,1},{1,0},{2,3},{3,2},{4,5},{5,4},{6,7},{7,6},{8,9},{9,8},{10,11... | collective-permute-start | bytes 110600 | tf_op jit(solution)/shard_map/share_pair/ppermute | solution.py:370

commit v6 on v4

--- a/solution.py
+++ b/solution.py
@@ -109,7 +109,7 @@
             pl.BlockSpec((slots.shape[0], block), lambda i: (0, i)),
         ],
         out_specs=(rows(block, 128), rows(block, 2 * CH), rows(block, 128)),
-        compiler_params=pltpu.CompilerParams(vmem_limit_bytes=60 * MIB),
+        compiler_params=pltpu.CompilerParams(vmem_limit_bytes=52 * MIB),
         cost_estimate=pl.CostEstimate(flops=4 * 10**9, bytes_accessed=8 * 10**6, transcendentals=0),
         name="head_values",
     )(me, feat, w_head, slots)

time: 98.1 us -> 97.9 us (level)
  waiting for transfers between devices: 5.99 us -> 7.68 us
  local copies, waits for them, and re-layouts: 3.49 us -> 2.34 us
    ppermute x9, waiting for transfers between devices: 5.19 us -> 6.97 us  [hop(): lax.ppermute(value, 'cam', [(i, i ^ distance) for i in range(2 * CHIPS)])]
    unnamed x20 -> x12, local copies, waits for them, and re-layouts: 2.12 us -> 0.98 us
  transfers between devices with their start and end apart: 10 -> 10, of which waited for: 6 -> 7; matrix products, arithmetic and copies ran while one was open for 0% -> 0% of each run, Pallas kernels for 18% -> 17%
where the time goes in v6:
time: 97.9 us; the launch traced here: 97.5 us
  Pallas kernels  37.8 us (39%)
  blocking collectives  26.2 us (27%)
  starting transfers between devices  20.5 us (21%)
  waiting for transfers between devices  7.68 us (8%)
  local copies, waits for them, and re-layouts  2.34 us (2%)
  other arithmetic  2.32 us (2%)
    all_to_all x1, blocking collectives, shards(): half = lax.all_to_all(half, 'dp', 0, 0, tiled=True)  26.2 us
    pallas_call x1, Pallas kernels, inner_halves(): pl.pallas_call(functools.partial(grads_kernel, owners=owners), grid=(bloc...  15.5 us
    ppermute x9, starting transfers between devices, hop(): lax.ppermute(value, 'cam', [(i, i ^ distance) for i in range(2 * CHIPS)])  14 us
    pallas_call x2, Pallas kernels, pixel_weights(): pl.pallas_call(weights_kernel, grid=(count,), out_shape=(jax.ShapeDtypeSt...  13.3 us
    ppermute x9, waiting for transfers between devices, hop(): lax.ppermute(value, 'cam', [(i, i ^ distance) for i in range(2 * CHIPS)])  6.97 us
    all_to_all x1, starting transfers between devices, shards(): lists = lax.all_to_all(cell_lists[0, 0], 'cam', 0, 0, tiled=True)  6.48 us
    pallas_call x1, Pallas kernels, gather_rows(): pl.pallas_call(gather_kernel, out_shape=(one, one, two, two, two), in_spe...  4.56 us
    pallas_call x1, Pallas kernels, head_values(): pl.pallas_call(head_kernel, grid=(pixels // block,), out_shape=(jax.Shape...  3.01 us
  transfers between devices with their start and end apart: 10, of which 7 were waited for; matrix products, arithmetic and copies ran while one was open for 0% of the time, Pallas kernels for 17%

profile of v6, /device:TPU:1, one launch (start us, length us, event | category | flops | bytes accessed | tf_op | source)
XLA Modules:
  0.0 97.5 jit_solution(8977125049261439235)
XLA Ops:
  0.6 1.3 %all_to_all.9 = s32[8,1,512]{2,1,0:T(1,128)} reshape(s32[1,1,8,512]{3,2,1,0:T(8,128)} %param.13) | data formatting | bytes 32768 | tf_op jit(solution)/shard_map/lists/all_to_all | solution.py:383
  2.0 6.5 %all-to-all-start = ((s32[8,1,512]{2,1,0:T(1,128)}), s32[8,1,512]{2,1,0:T(1,128)S(1)}, u32[]{:S(2)}, u32[]{:S(2)}) async-start(s32[8,1,512]{2,1,0:T(1,128)} %all_to_all.9), calls=%async_computation | async-start | bytes 32768 | tf_op jit(solution)/shard_map/lists/all_to_all | solution.py:383
  8.4 0.9 copy-done.5
  9.4 3.0 %head_values.1 = (f32[1024,128]{1,0:T(8,128)S(1)}, bf16[1024,256]{1,0:T(8,128)(2,1)S(1)}, s32[1024,128]{1,0:T(8,128)S(1)}) custom-call(s32[1]{0:T(128)} %bitcast.1.me_ref, bf16[1024,1536]{1,0:T(8,128)(2,1)} %bitcast.26, bf16[192,1536]{1,0:T(8,128)(2,1)} %bitcast.21, s32[64,1024]{1,0:T(8,128)S(1)} %bitcast.25), custom_call_target="tpu_custom_call" | custom-call | flops 4000000000 | bytes 8000000 | tf_op jit(solution)/shard_map/head_values/pallas_call | solution.py:97
  12.4 0.7 all-to-all-done
  13.1 4.6 %gather_rows.1 = (bf16[1,512,128]{2,1,0:T(8,128)(2,1)S(1)}, bf16[1,512,128]{2,1,0:T(8,128)(2,1)S(1)}, bf16[2,512,128]{2,1,0:T(8,128)(2,1)S(1)}, bf16[2,512,128]{2,1,0:T(8,128)(2,1)S(1)}, bf16[2,512,128]{2,1,0:T(8,128)(2,1)S(1)}) custom-call(s32[1]{0:T(128)} %bitcast.1.me_ref, s32[4096]{0:T(1024)S(1)} %bitcast.24, bf16[4096,128]{1,0:T(8,128)(2,1)S(1)} %bitcast.20), custom_call_target="tpu_custom_call" | custom-call | tf_op jit(solution)/shard_map/gather_rows/pallas_call | solution.py:69
  17.7 0.8 collective-permute-start
  18.5 2.4 %collective-permute-start.1 = (bf16[2,512,128]{2,1,0:T(8,128)(2,1)S(1)}, bf16[2,512,128]{2,1,0:T(8,128)(2,1)S(1)}, u32[]{:S(2)}, u32[]{:S(2)}) collective-permute-start(bf16[2,512,128]{2,1,0:T(8,128)(2,1)S(1)} %get-tuple-element.22), channel_id=1, source_target_pairs={{0,4},{1,5},{2,6},{3,7},{4,0},{5,1},{6,2},{7,3},{8,12},{9,13},{10,... | collective-permute-start | bytes 786440 | tf_op jit(solution)/shard_map/rows/ppermute | solution.py:370
  20.9 0.7 collective-permute-start.2
  21.6 10.7 %pixel_weights.2 = (bf16[2048,4096]{1,0:T(8,128)(2,1)}, f32[8,128]{1,0:T(8,128)S(1)}) custom-call(bf16[1,512,128]{2,1,0:T(8,128)(2,1)S(1)} %get-tuple-element.20.refs_0_.own_ref, f32[1024,128]{1,0:T(8,128)S(1)} %get-tuple-element.24.refs_1_.refs_2_.occ_ref, s32[1024,128]{1,0:T(8,128)S(1)} %get-tuple-element.25.refs_2_.refs_3_.place_ref), custom_call_target="tpu_custom_call" | custom-call | flops 17500000256 | bytes 21000000 | tf_op jit(solution)/shard_map/pixel_weights/pallas_call | solution.py:170
  32.3 0.3 collective-permute-done.1.two_ref
  32.6 2.0 %collective-permute-done.2.three_ref = bf16[2,512,128]{2,1,0:T(8,128)(2,1)S(1)} collective-permute-done((bf16[2,512,128]{2,1,0:T(8,128)(2,1)S(1)}, bf16[2,512,128]{2,1,0:T(8,128)(2,1)S(1)}, u32[]{:S(2)}, u32[]{:S(2)}) %collective-permute-start.2) | collective-permute-done | bytes 262176 | tf_op jit(solution)/shard_map/rows/ppermute | solution.py:370
  34.7 0.8 pad_maximum_fusion
  35.5 1.8 %collective-permute-start.3 = (bf16[2048,128]{1,0:T(8,128)(2,1)}, bf16[2048,128]{1,0:T(8,128)(2,1)S(1)}, u32[]{:S(2)}, u32[]{:S(2)}) collective-permute-start(bf16[2048,128]{1,0:T(8,128)(2,1)} %pad_maximum_fusion), channel_id=1, source_target_pairs={{0,1},{1,0},{2,3},{3,2},{4,5},{5,4},{6,7},{7,6},{8,9},{9,8},{10,11... | collective-permute-start | bytes 1572872 | tf_op jit(solution)/shard_map/rows_pair/ppermute | solution.py:370
  37.3 2.6 %pixel_weights.3 = (bf16[2048,4096]{1,0:T(8,128)(2,1)}, f32[8,128]{1,0:T(8,128)}) custom-call(bf16[2048,4096]{1,0:T(8,128)(2,1)} %get-tuple-element.31.refs_0_, f32[8,128]{1,0:T(8,128)S(1)} %get-tuple-element.32.refs_1_, f32[1024,128]{1,0:T(8,128)S(1)} %get-tuple-element.24.refs_1_.refs_2_.occ_ref, ...), custom_call_target="tpu_custom_call", output_to_operand_aliasing={{0}: (0, {})} | custom-call | flops 2500000000 | bytes 3000000 | tf_op jit(solution)/shard_map/pixel_weights/pallas_call | solution.py:170
  39.9 15.5 %inner_halves.1 = (f32[768,384]{1,0:T(8,128)}, bf16[768,384]{1,0:T(8,128)(2,1)S(1)}) custom-call(s32[1]{0:T(128)} %bitcast.core_ref, bf16[1,512,128]{2,1,0:T(8,128)(2,1)S(1)} %get-tuple-element.20.refs_0_.own_ref, bf16[2,512,128]{2,1,0:T(8,128)(2,1)S(1)} %collective-permute-done.one_ref, bf16[2,512,128]{2,1,0:T(8,128)(2,1)S(1)} %collective-permute-done.1.two_ref, ...), custom_call_target="tpu_custom_call" | custom-call | tf_op jit(solution)/shard_map/inner_halves/pallas_call | solution.py:304
  55.5 0.1 collective-permute-start.4
  55.6 2.0 %collective-permute-done.4 = bf16[768,384]{1,0:T(8,128)(2,1)S(1)} collective-permute-done((bf16[768,384]{1,0:T(8,128)(2,1)S(1)}, bf16[768,384]{1,0:T(8,128)(2,1)S(1)}, u32[]{:S(2)}, u32[]{:S(2)}) %collective-permute-start.4) | collective-permute-done | bytes 589856 | tf_op jit(solution)/shard_map/sum_pair/ppermute | solution.py:370
  57.6 1.4 %add_convert_fusion = bf16[768,384]{1,0:T(8,128)(2,1)S(1)} fusion(f32[768,384]{1,0:T(8,128)} %get-tuple-element.35, bf16[768,384]{1,0:T(8,128)(2,1)S(1)} %collective-permute-done.4), kind=kLoop, calls=%fused_computation.1 | loop fusion | flops 884736 | bytes 2359296 | tf_op jit(solution)/shard_map/sum_pair/convert_element_type | solution.py:397
  59.0 0.0 copy-start.1
  59.0 0.0 copy-start.2
  59.0 0.0 copy-start.3
  59.0 0.0 copy-start.4
  59.0 26.2 %all_to_all.14 = bf16[32,24,384]{2,1,0:T(8,128)(2,1)S(1)} all-to-all(bf16[32,24,384]{2,1,0:T(8,128)(2,1)S(1)} %bitcast.29), channel_id=1, replica_groups=mesh['dp'=32,'cam'=8] {'dp'}, dimensions={0} | all-to-all | bytes 1179648 | tf_op jit(solution)/shard_map/sum_dp/all_to_all | solution.py:400
  85.2 0.1 convert_reduce_fusion
  85.3 0.8 collective-permute-start.7
  86.1 2.5 %collective-permute-start.5 = (f32[24,384]{1,0:T(8,128)S(1)}, f32[24,384]{1,0:T(8,128)S(1)}, u32[]{:S(2)}, u32[]{:S(2)}) collective-permute-start(f32[24,384]{1,0:T(8,128)S(1)} %convert_reduce_fusion), channel_id=1, source_target_pairs={{0,2},{1,3},{2,0},{3,1},{4,6},{5,7},{6,4},{7,5},{8,10},{9,11},{10,... | collective-permute-start | bytes 110600 | tf_op jit(solution)/shard_map/sum_x/ppermute | solution.py:370
  88.7 0.8 collective-permute-done.7
  89.4 1.0 %collective-permute-done.6 = f32[24,384]{1,0:T(8,128)S(1)} collective-permute-done((f32[24,384]{1,0:T(8,128)S(1)}, f32[24,384]{1,0:T(8,128)S(1)}, u32[]{:S(2)}, u32[]{:S(2)}) %collective-permute-start.6) | collective-permute-done | bytes 36896 | tf_op jit(solution)/shard_map/sum_x/ppermute | solution.py:370
  90.5 4.8 %collective-permute-start.8 = (f32[24,384]{1,0:T(8,128)S(1)}, f32[24,384]{1,0:T(8,128)S(1)}, u32[]{:S(2)}, u32[]{:S(2)}) collective-permute-start(f32[24,384]{1,0:T(8,128)S(1)} %add_add_fusion.mine_ref), channel_id=1, source_target_pairs={{0,1},{1,0},{2,3},{3,2},{4,5},{5,4},{6,7},{7,6},{8,9},{9,8},{10,11... | collective-permute-start | bytes 110600 | tf_op jit(solution)/shard_map/share_pair/ppermute | solution.py:370
  95.2 0.9 collective-permute-done.8.other_ref
  96.1 1.4 %adam_update.1 = (f32[48,1728]{1,0:T(8,128)}, f32[48,1728]{1,0:T(8,128)}, f32[48,1728]{1,0:T(8,128)}) custom-call(s32[1]{0:T(128)} %bitcast.core_ref, f32[24,384]{1,0:T(8,128)S(1)} %add_add_fusion.mine_ref, f32[24,384]{1,0:T(8,128)S(1)} %collective-permute-done.8.other_ref, bf16[192,1536]{1,0:T(8,128)(2,1)S(1)} %bitcast.22, f32[48,1728]{1,0:T(8,128)S(1)} %copy-done.2, ...), custom_call_target="tpu_custom_call" | custom-call | tf_op jit(solution)/shard_map/adam_update/pallas_call | solution.py:359
  (14 shorter events, 0.1 us)
Async XLA Ops:
  2.0 11.2 %all-to-all-start = ((s32[8,1,512]{2,1,0:T(1,128)}), s32[8,1,512]{2,1,0:T(1,128)S(1)}, u32[]{:S(2)}, u32[]{:S(2)}) async-start(s32[8,1,512]{2,1,0:T(1,128)} %all_to_all.9), calls=%async_computation | async-start | bytes 32768 | tf_op jit(solution)/shard_map/lists/all_to_all | solution.py:383
  8.4 0.9 copy-start.5
  9.4 3.7 %copy-start = (bf16[1,4096,128]{2,1,0:T(8,128)(2,1)S(1)}, bf16[1,4096,128]{2,1,0:T(8,128)(2,1)}, u32[]{:S(2)}) copy-start(bf16[1,4096,128]{2,1,0:T(8,128)(2,1)} %param.12) | copy-start | bytes 3145732
  17.7 14.6 %collective-permute-start = (bf16[2,512,128]{2,1,0:T(8,128)(2,1)S(1)}, bf16[2,512,128]{2,1,0:T(8,128)(2,1)S(1)}, u32[]{:S(2)}, u32[]{:S(2)}) collective-permute-start(bf16[2,512,128]{2,1,0:T(8,128)(2,1)S(1)} %get-tuple-element.21), channel_id=1, source_target_pairs={{0,2},{1,3},{2,0},{3,1},{4,6},{5,7},{6,4},{7,5},{8,10},{9,11},{10,... | collective-permute-start | bytes 786440 | tf_op jit(solution)/shard_map/rows/ppermute | solution.py:370
  18.5 14.1 %collective-permute-start.1 = (bf16[2,512,128]{2,1,0:T(8,128)(2,1)S(1)}, bf16[2,512,128]{2,1,0:T(8,128)(2,1)S(1)}, u32[]{:S(2)}, u32[]{:S(2)}) collective-permute-start(bf16[2,512,128]{2,1,0:T(8,128)(2,1)S(1)} %get-tuple-element.22), channel_id=1, source_target_pairs={{0,4},{1,5},{2,6},{3,7},{4,0},{5,1},{6,2},{7,3},{8,12},{9,13},{10,... | collective-permute-start | bytes 786440 | tf_op jit(solution)/shard_map/rows/ppermute | solution.py:370
  20.9 13.7 %collective-permute-start.2 = (bf16[2,512,128]{2,1,0:T(8,128)(2,1)S(1)}, bf16[2,512,128]{2,1,0:T(8,128)(2,1)S(1)}, u32[]{:S(2)}, u32[]{:S(2)}) collective-permute-start(bf16[2,512,128]{2,1,0:T(8,128)(2,1)S(1)} %get-tuple-element.23), channel_id=1, source_target_pairs={{0,6},{1,7},{2,4},{3,5},{4,2},{5,3},{6,0},{7,1},{8,14},{9,15},{10,... | collective-permute-start | bytes 786440 | tf_op jit(solution)/shard_map/rows/ppermute | solution.py:370
  35.5 4.4 %collective-permute-start.3 = (bf16[2048,128]{1,0:T(8,128)(2,1)}, bf16[2048,128]{1,0:T(8,128)(2,1)S(1)}, u32[]{:S(2)}, u32[]{:S(2)}) collective-permute-start(bf16[2048,128]{1,0:T(8,128)(2,1)} %pad_maximum_fusion), channel_id=1, source_target_pairs={{0,1},{1,0},{2,3},{3,2},{4,5},{5,4},{6,7},{7,6},{8,9},{9,8},{10,11... | collective-permute-start | bytes 1572872 | tf_op jit(solution)/shard_map/rows_pair/ppermute | solution.py:370
  55.5 2.1 %collective-permute-start.4 = (bf16[768,384]{1,0:T(8,128)(2,1)S(1)}, bf16[768,384]{1,0:T(8,128)(2,1)S(1)}, u32[]{:S(2)}, u32[]{:S(2)}) collective-permute-start(bf16[768,384]{1,0:T(8,128)(2,1)S(1)} %get-tuple-element.36), channel_id=1, source_target_pairs={{0,1},{1,0},{2,3},{3,2},{4,5},{5,4},{6,7},{7,6},{8,9},{9,8},{10,11... | collective-permute-start | bytes 1769480 | tf_op jit(solution)/shard_map/sum_pair/ppermute | solution.py:370
  59.0 37.2 %copy-start.1 = (bf16[1536,192]{0,1:T(8,128)(2,1)S(1)}, bf16[1536,192]{0,1:T(8,128)(2,1)}, u32[]{:S(2)}) copy-start(bf16[1536,192]{0,1:T(8,128)(2,1)} %param.11) | copy-start | bytes 1769476
  59.0 37.1 %copy-start.2 = (f32[48,1728]{1,0:T(8,128)S(1)}, f32[48,1728]{1,0:T(8,128)}, u32[]{:S(2)}) copy-start(f32[48,1728]{1,0:T(8,128)} %master_ref.1) | copy-start | bytes 995332
  59.0 37.1 %copy-start.3 = (f32[48,1728]{1,0:T(8,128)S(1)}, f32[48,1728]{1,0:T(8,128)}, u32[]{:S(2)}) copy-start(f32[48,1728]{1,0:T(8,128)} %first_ref.1) | copy-start | bytes 995332
  59.0 37.1 %copy-start.4 = (f32[48,1728]{1,0:T(8,128)S(1)}, f32[48,1728]{1,0:T(8,128)}, u32[]{:S(2)}) copy-start(f32[48,1728]{1,0:T(8,128)} %second_ref.1) | copy-start | bytes 995332
  85.3 4.1 %collective-permute-start.7 = (f32[24,384]{1,0:T(8,128)S(1)}, f32[24,384]{1,0:T(8,128)S(1)}, u32[]{:S(2)}, u32[]{:S(2)}) collective-permute-start(f32[24,384]{1,0:T(8,128)S(1)} %convert_reduce_fusion), channel_id=1, source_target_pairs={{0,6},{1,7},{2,4},{3,5},{4,2},{5,3},{6,0},{7,1},{8,14},{9,15},{10,... | collective-permute-start | bytes 110600 | tf_op jit(solution)/shard_map/sum_x/ppermute | solution.py:370
  86.1 4.3 %collective-permute-start.6 = (f32[24,384]{1,0:T(8,128)S(1)}, f32[24,384]{1,0:T(8,128)S(1)}, u32[]{:S(2)}, u32[]{:S(2)}) collective-permute-start(f32[24,384]{1,0:T(8,128)S(1)} %convert_reduce_fusion), channel_id=1, source_target_pairs={{0,4},{1,5},{2,6},{3,7},{4,0},{5,1},{6,2},{7,3},{8,12},{9,13},{10,... | collective-permute-start | bytes 110600 | tf_op jit(solution)/shard_map/sum_x/ppermute | solution.py:370
  86.1 4.3 %collective-permute-start.5 = (f32[24,384]{1,0:T(8,128)S(1)}, f32[24,384]{1,0:T(8,128)S(1)}, u32[]{:S(2)}, u32[]{:S(2)}) collective-permute-start(f32[24,384]{1,0:T(8,128)S(1)} %convert_reduce_fusion), channel_id=1, source_target_pairs={{0,2},{1,3},{2,0},{3,1},{4,6},{5,7},{6,4},{7,5},{8,10},{9,11},{10,... | collective-permute-start | bytes 110600 | tf_op jit(solution)/shard_map/sum_x/ppermute | solution.py:370
  90.5 5.6 %collective-permute-start.8 = (f32[24,384]{1,0:T(8,128)S(1)}, f32[24,384]{1,0:T(8,128)S(1)}, u32[]{:S(2)}, u32[]{:S(2)}) collective-permute-start(f32[24,384]{1,0:T(8,128)S(1)} %add_add_fusion.mine_ref), channel_id=1, source_target_pairs={{0,1},{1,0},{2,3},{3,2},{4,5},{5,4},{6,7},{7,6},{8,9},{9,8},{10,11... | collective-permute-start | bytes 110600 | tf_op jit(solution)/shard_map/share_pair/ppermute | solution.py:370
